TPU v7x, 32 devices: a whole 2x2x4 slice. The times are simulated.
32 devices in a mesh: pix: 8 (over z, y), ch: 4 (over x, core).
Axes of the slice: x: 2, y: 2, z: 4, core: 2. Of those that a mesh axis runs over, the one named last changes fastest.
Arguments:
- features: bfloat16 [32, 128, 2048], P('pix', None, 'ch'), may hold values from -7.5 to 7.5
- valid_mask: int32 [32, 128], P('pix'), may hold values from 0 to 1, as said below
- sem_label: int32 [32, 128], P('pix'), may hold values from 0 to 18
- depth_target: float32 [32, 128], P('pix'), may hold values from -6 to 6
- normal_target: float32 [3, 32, 128], P(None, 'pix'), may hold values from -6 to 6
- label_mask: int32 [3, 32, 128], P(None, 'pix'), may hold values from 0 to 1, as said below
- w_reduce: float32 [2048, 512], P('ch', 'pix'), may hold values from -0.125 to 0.125
- m_reduce: float32 [2048, 512], P('ch', 'pix'), may hold values from -2.3841858e-06 to 2.3841858e-06
- v_reduce: float32 [2048, 512], P('ch', 'pix'), may hold values from 5.0711002e-17 to 2.0284401e-16
- w_dilated: float32 [9, 512, 512], P(None, 'pix', 'ch'), may hold values from -0.09375 to 0.09375
- m_dilated: float32 [9, 512, 512], P(None, 'pix', 'ch'), may hold values from -2.3841858e-06 to 2.3841858e-06
- v_dilated: float32 [9, 512, 512], P(None, 'pix', 'ch'), may hold values from 6.761467e-17 to 2.7045868e-16
- w_expand: float32 [512, 2048], P('pix', 'ch'), may hold values from -0.25 to 0.25
- m_expand: float32 [512, 2048], P('pix', 'ch'), may hold values from -2.3841858e-06 to 2.3841858e-06
- v_expand: float32 [512, 2048], P('pix', 'ch'), may hold values from 2.5355501e-17 to 1.01422005e-16
- head_weight: float32 [2048, 768], P('ch', 'pix'), may hold values from -0.125 to 0.125
- m_head: float32 [2048, 768], P('ch', 'pix'), may hold values from -2.3841858e-06 to 2.3841858e-06
- v_head: float32 [2048, 768], P('ch', 'pix'), may hold values from 2.02844e-15 to 8.11376e-15
- head_rates: float32 [3, 9, 768, 2048], P(None, None, 'pix', 'ch'), may hold values from -0.046875 to 0.046875
- m_rates: float32 [3, 9, 768, 2048], P(None, None, 'pix', 'ch'), may hold values from -2.3841858e-06 to 2.3841858e-06
- v_rates: float32 [3, 9, 768, 2048], P(None, None, 'pix', 'ch'), may hold values from 2.02844e-15 to 8.11376e-15
- head_proj: float32 [3, 1024, 256], P(None, 'pix'), may hold values from -0.1875 to 0.1875
- m_proj: float32 [3, 1024, 256], P(None, 'pix'), may hold values from -2.3841858e-06 to 2.3841858e-06
- v_proj: float32 [3, 1024, 256], P(None, 'pix'), may hold values from 2.02844e-15 to 8.11376e-15
- norm_params: float32 [2, 3072], replicated, may hold values from -0.6 to 1.8, as said below
- norm_m: float32 [2, 3072], replicated, may hold values from -2.3841858e-06 to 2.3841858e-06
- norm_v: float32 [2, 3072], replicated, may hold values from 4.0568802e-17 to 1.6227521e-16
- head_small: float32 [9751], replicated, may hold values from -1.2 to 1.2
- small_m: float32 [9751], replicated, may hold values from -2.3841858e-06 to 2.3841858e-06
- small_v: float32 [9751], replicated, may hold values from 2.02844e-15 to 8.11376e-15
Outputs:
- block_out: bfloat16 [32, 128, 2048], P('pix', None, 'ch')
- input_grad: float32 [32, 128, 2048], P('pix', None, 'ch')
- grad_norm: float32 [], replicated
- reduce_new: float32 [2048, 512], P('ch', 'pix')
- reduce_first: float32 [2048, 512], P('ch', 'pix')
- reduce_second: float32 [2048, 512], P('ch', 'pix')
- reduce_copy: bfloat16 [2048, 512], P('ch', 'pix')
- dilated_new: float32 [9, 512, 512], P(None, 'pix', 'ch')
- dilated_first: float32 [9, 512, 512], P(None, 'pix', 'ch')
- dilated_second: float32 [9, 512, 512], P(None, 'pix', 'ch')
- dilated_copy: bfloat16 [9, 512, 512], P(None, 'pix', 'ch')
- expand_new: float32 [512, 2048], P('pix', 'ch')
- expand_first: float32 [512, 2048], P('pix', 'ch')
- expand_second: float32 [512, 2048], P('pix', 'ch')
- expand_copy: bfloat16 [512, 2048], P('pix', 'ch')
- head_new: float32 [2048, 768], P('ch', 'pix')
- head_first: float32 [2048, 768], P('ch', 'pix')
- head_second: float32 [2048, 768], P('ch', 'pix')
- head_copy: bfloat16 [2048, 768], P('ch', 'pix')
- rates_new: float32 [3, 9, 768, 2048], P(None, None, 'pix', 'ch')
- rates_first: float32 [3, 9, 768, 2048], P(None, None, 'pix', 'ch')
- rates_second: float32 [3, 9, 768, 2048], P(None, None, 'pix', 'ch')
- rates_copy: bfloat16 [3, 9, 768, 2048], P(None, None, 'pix', 'ch')
- proj_new: float32 [3, 1024, 256], P(None, 'pix')
- proj_first: float32 [3, 1024, 256], P(None, 'pix')
- proj_second: float32 [3, 1024, 256], P(None, 'pix')
- proj_copy: bfloat16 [3, 1024, 256], P(None, 'pix')
- norm_new: float32 [2, 3072], replicated
- norm_first: float32 [2, 3072], replicated
- norm_second: float32 [2, 3072], replicated
- small_new: float32 [9751], replicated
- small_first: float32 [9751], replicated
- small_second: float32 [9751], replicated
- depth_bias_grad: float32 [], replicated
Inputs may be any that keep to these rules, and one draw needn't show every extreme that they name: `valid_mask`: in each band of 4 rows a run of 4 columns (shorter at the right edge) is 0, the rest 1. `label_mask`: the share of valid labels grows from about a quarter in the first rows to about three quarters in the last. `norm_params`: gains are positive.
All inputs are finite; a program needn't handle non-finite values.
Results may differ from a plain program's by a relative error of at most 0.015.
Values may be sent and summed in bfloat16 or wider, within the bound.
A program may use at most 320 MiB of HBM per device.

v0:
```python
import jax
import jax.numpy as jnp
from jax import lax
from jax.sharding import PartitionSpec as P

C = 2048
M = 512
HID = 256
NCLS = 19
DILATION_RATE = 4
STEP = 10


EPS_NORM = 1e-05
BETA_ONE = 0.9
BETA_TWO = 0.999
ADAM_EPS = 1e-08
RATE_MATRIX = 0.02
RATE_SMALL = 0.2
DECAY = 0.01
CLIP_NORM = 0.01
aspp_rates = (12, 24, 36)


def shifted(value, axis, steps):
    count = lax.axis_size(axis)
    leading, last = (max(0, -steps), min(count, count - steps))
    return lax.ppermute(value, axis, [(source, source + steps) for source in range(leading, last)])


def with_halo(cells, sides, width):
    for axis, dim in sides:
        count = lax.axis_size(axis)
        ends = count - 1
        head = lax.slice_in_dim(cells, 0, width, axis=dim)
        tail = lax.slice_in_dim(cells, cells.shape[dim] - width, cells.shape[dim], axis=dim)
        cells = jnp.concatenate(
            [
                lax.ppermute(tail, axis, [(i, (i + 1) % count) for i in range(ends)]),
                cells,
                lax.ppermute(head, axis, [((i + 1) % count, i) for i in range(ends)]),
            ],
            axis=dim,
        )
    return cells


def smooth(values):
    return jax.nn.gelu(values, approximate=True)


def smooth_slope(values):
    return jax.vjp(smooth, values)[1](jnp.ones_like(values))[0]


def contract_first(left, right):
    return lax.dot_general(
        left, right, (((0,), (0,)), ((), ())), preferred_element_type=jnp.float32
    )


def contract_last(left, right):
    return lax.dot_general(
        left, right, (((1,), (1,)), ((), ())), preferred_element_type=jnp.float32
    )


def split_tasks(slopes, weight):
    pixels = slopes.shape[0]
    return lax.dot_general(
        slopes.reshape(pixels, 3, -1),
        weight.reshape(weight.shape[0], 3, -1),
        (((2,), (2,)), ((1,), (1,))),
        preferred_element_type=jnp.float32,
    )


def split_tasks_rows(slopes, weight):
    pixels = slopes.shape[0]
    return lax.dot_general(
        slopes.reshape(pixels, 3, -1),
        weight.reshape(3, -1, weight.shape[1]),
        (((2,), (1,)), ((1,), (0,))),
        preferred_element_type=jnp.float32,
    )


def unpack_small(vector):
    lengths = (12 * HID, 3 * HID, HID * NCLS, HID, HID * 3, NCLS, 1, 3)
    pieces = []
    offset = 0
    for length in lengths:
        pieces.append(lax.slice_in_dim(vector, offset, offset + length, axis=0))
        offset = offset + length
    return (
        pieces[0].reshape(4, 3 * HID),
        pieces[1].reshape(3, HID),
        pieces[2].reshape(HID, NCLS),
        pieces[3].reshape(HID, 1),
        pieces[4].reshape(HID, 3),
        pieces[5],
        pieces[6],
        pieces[7],
    )


def pack_small(pieces):
    return jnp.concatenate([piece.reshape(-1) for piece in pieces])


def fetch_rows(grid, step):
    if abs(step) >= lax.axis_size("pix"):
        return jnp.zeros_like(grid)
    return shifted(grid, "pix", -step)


def fetch_grads(grid, step):
    if abs(step) >= lax.axis_size("pix"):
        return jnp.zeros_like(grid)
    return shifted(grid, "pix", -step)


def row_view(grid, offset, fetch):
    height = grid.shape[0]
    lead, rest = divmod(offset, height)
    return fetch(grid, lead)


def column_view(grid, offset):
    width = grid.shape[1]
    reach = abs(offset)
    if reach == 0:
        return grid
    padded_canvas = jnp.pad(grid, ((0, 0), (reach, reach), (0, 0)))
    return padded_canvas[:, reach + offset : reach + offset + width]


def imtl_weights(gram):
    lengths = jnp.sqrt(jnp.diagonal(gram) + 1e-12)

    def pairing(row_task, col_task):
        return (
            gram[0, 0] / lengths[0]
            - gram[0, col_task] / lengths[col_task]
            - gram[row_task, 0] / lengths[0]
            + gram[row_task, col_task] / lengths[col_task]
        )

    right_one = gram[0, 0] / lengths[0] - gram[0, 1] / lengths[1]
    right_two = gram[0, 0] / lengths[0] - gram[0, 2] / lengths[2]
    upper_left = pairing(1, 1)
    upper_right = pairing(1, 2)
    lower_left = pairing(2, 1)
    lower_right = pairing(2, 2)
    determinant = upper_left * lower_right - upper_right * lower_left
    alpha_one = (right_one * lower_right - right_two * lower_left) / determinant
    alpha_two = (right_two * upper_left - right_one * upper_right) / determinant
    return jnp.stack([1.0 - alpha_one - alpha_two, alpha_one, alpha_two])


def adam_step(weight, first, second, grad, rate, decay):
    first_new = BETA_ONE * first + (1.0 - BETA_ONE) * grad
    second_new = BETA_TWO * second + (1.0 - BETA_TWO) * grad * grad
    first_hat = first_new / (1.0 - BETA_ONE**STEP)
    second_hat = second_new / (1.0 - BETA_TWO**STEP)
    weight_new = weight - rate * (first_hat / (jnp.sqrt(second_hat) + ADAM_EPS) + decay * weight)
    return (weight_new, first_new, second_new)


def pixel_sums(first, second):
    return lax.psum((first, second), "pix")


def back_pair(first, second):
    return lax.psum((first, second), "pix")


def channel_gather(piece):
    return lax.all_gather(piece, "ch", axis=1, tiled=True)


def channel_parts(partial_sum):
    return lax.psum_scatter(partial_sum, "ch", scatter_dimension=1, tiled=True)


def forward_norm(inputs, sums, squares, count, gain_row, shift_row):
    mean_row = sums / count
    scale_row = lax.rsqrt(squares / count - mean_row * mean_row + EPS_NORM)
    normed = (inputs - mean_row) * scale_row
    return (normed * gain_row + shift_row, normed, scale_row)


def backward_norm(upstream, normed, scale_row, count, gain_row):
    shift_grad, gain_grad = back_pair(jnp.sum(upstream, axis=0), jnp.sum(upstream * normed, axis=0))
    inner = gain_row * scale_row * (upstream - shift_grad / count - normed * (gain_grad / count))
    return (inner, gain_grad, shift_grad)


def loss_slopes(
    logits, depth_pred, normal_pred, sem_label, depth_target, normal_target, label_mask, counts
):
    masks = label_mask.reshape(3, -1).astype(jnp.float32)
    classes = lax.broadcasted_iota(jnp.int32, (1, NCLS), 1)
    onehot = (sem_label.reshape(-1, 1) == classes).astype(jnp.float32)
    highest = jnp.max(logits, axis=1, keepdims=True)
    raised = jnp.exp(logits - highest)
    probs = raised / jnp.sum(raised, axis=1, keepdims=True)
    sem_slope = masks[0][:, None] * (probs - onehot) / counts[0]
    depth_gap = depth_pred[:, 0] - depth_target.reshape(-1)
    depth_slope = (masks[1] * depth_gap / jnp.sqrt(depth_gap * depth_gap + 1.0) / counts[1])[
        :, None
    ]
    normal_slope = masks[2][:, None] * (normal_pred - normal_target.reshape(3, -1).T) / counts[2]
    return (
        sem_slope.astype(jnp.bfloat16),
        depth_slope.astype(jnp.bfloat16),
        normal_slope.astype(jnp.bfloat16),
    )


def per_device(
    features,
    valid_mask,
    sem_label,
    depth_target,
    normal_target,
    label_mask,
    w_reduce,
    m_reduce,
    v_reduce,
    w_dilated,
    m_dilated,
    v_dilated,
    w_expand,
    m_expand,
    v_expand,
    head_weight,
    m_head,
    v_head,
    head_rates,
    m_rates,
    v_rates,
    head_proj,
    m_proj,
    v_proj,
    norm_params,
    norm_m,
    norm_v,
    head_small,
    small_m,
    small_v,
):
    rows_per_shard, columns_per_shard, wide_dev = features.shape
    pixels = rows_per_shard * columns_per_shard
    groups = lax.axis_size("ch")
    block_id = lax.axis_index("ch")
    pix_devices = lax.axis_size("pix")
    middle_per_shard = M // groups
    count_all = float(pixels * pix_devices)
    flat_in = features.reshape(pixels, wide_dev)
    mask_flat = valid_mask.reshape(pixels).astype(jnp.float32)
    gains = norm_params[0]
    shifts = norm_params[1]

    def owned(vector, offset, width):
        return lax.dynamic_slice_in_dim(vector, offset + block_id * width, width)

    reduce_w, dilated_w, expand_w, heads_w, rates_w, proj_w = (
        lax.all_gather(w_reduce.astype(jnp.bfloat16), "pix", axis=1, tiled=True),
        lax.all_gather(w_dilated.astype(jnp.bfloat16), "pix", axis=1, tiled=True),
        lax.all_gather(w_expand.astype(jnp.bfloat16), "pix", axis=0, tiled=True),
        lax.all_gather(head_weight.astype(jnp.bfloat16), "pix", axis=1, tiled=True),
        lax.all_gather(head_rates.astype(jnp.bfloat16), "pix", axis=2, tiled=True),
        lax.all_gather(head_proj.astype(jnp.bfloat16), "pix", axis=1, tiled=True),
    )
    reduced = lax.psum_scatter(
        jnp.dot(flat_in, reduce_w, preferred_element_type=jnp.float32),
        "ch",
        scatter_dimension=1,
        tiled=True,
    )
    local_counts = jnp.sum(label_mask.astype(jnp.float32), axis=(1, 2))
    reduced_sum = jnp.sum(reduced, axis=0)
    reduced_sq = jnp.sum(reduced * reduced, axis=0)
    reduced_sum, reduced_sq = lax.psum((reduced_sum, reduced_sq), "pix")
    task_counts = lax.psum(local_counts, "pix")
    task_counts = jnp.maximum(task_counts, 1.0)
    gain_one = owned(gains, 0, middle_per_shard)
    norm_one, hat_one, scale_one = forward_norm(
        reduced, reduced_sum, reduced_sq, count_all, gain_one, owned(shifts, 0, middle_per_shard)
    )
    first = (smooth(norm_one) * mask_flat[:, None]).astype(jnp.bfloat16)
    first_gathered = channel_gather(first).reshape(rows_per_shard, columns_per_shard, M)
    bordered_input = with_halo(first_gathered, (("pix", 0),), DILATION_RATE)
    bordered_input = jnp.pad(bordered_input, ((0, 0), (DILATION_RATE, DILATION_RATE), (0, 0)))
    middle = jnp.zeros((pixels, middle_per_shard), jnp.float32)
    for tap_index in range(9):
        kernel_row, kernel_column = divmod(tap_index, 3)
        sliding_patch = bordered_input[
            kernel_row * DILATION_RATE : kernel_row * DILATION_RATE + rows_per_shard,
            kernel_column * DILATION_RATE : kernel_column * DILATION_RATE + columns_per_shard,
        ].reshape(pixels, M)
        middle = middle + jnp.dot(
            sliding_patch, dilated_w[tap_index], preferred_element_type=jnp.float32
        )
    gain_two = owned(gains, M, middle_per_shard)
    middle_sum, middle_sq = pixel_sums(jnp.sum(middle, axis=0), jnp.sum(middle * middle, axis=0))
    norm_two, hat_two, scale_two = forward_norm(
        middle, middle_sum, middle_sq, count_all, gain_two, owned(shifts, M, middle_per_shard)
    )
    second = smooth(norm_two).astype(jnp.bfloat16)
    second_all = channel_gather(second)
    expanded = jnp.dot(second_all, expand_w, preferred_element_type=jnp.float32)
    gain_three = owned(gains, 2 * M, wide_dev)
    expand_sum, expand_sq = pixel_sums(
        jnp.sum(expanded, axis=0), jnp.sum(expanded * expanded, axis=0)
    )
    norm_three, hat_three, scale_three = forward_norm(
        expanded, expand_sum, expand_sq, count_all, gain_three, owned(shifts, 2 * M, wide_dev)
    )
    summed_in = norm_three + flat_in.astype(jnp.float32)
    shared = smooth(summed_in).astype(jnp.bfloat16)
    branch_bias, proj_bias, sem_w, depth_w, normal_w, sem_b, depth_b, normal_b = unpack_small(
        head_small
    )
    out_weights = (
        sem_w.astype(jnp.bfloat16),
        depth_w.astype(jnp.bfloat16),
        normal_w.astype(jnp.bfloat16),
    )
    grid_shared = shared.reshape(rows_per_shard, columns_per_shard, wide_dev)
    row_views = []
    pre_list = [jnp.dot(shared, heads_w, preferred_element_type=jnp.float32)]
    for rate_index, rate in enumerate(aspp_rates):
        views = (
            row_view(grid_shared, -rate, fetch_rows),
            grid_shared,
            row_view(grid_shared, rate, fetch_rows),
        )
        row_views.append(views)
        summed = jnp.zeros((pixels, 3 * HID), jnp.float32)
        for tap_index in range(9):
            kernel_row, kernel_column = divmod(tap_index, 3)
            sliding_patch = column_view(views[kernel_row], (kernel_column - 1) * rate).reshape(
                pixels, wide_dev
            )
            summed = summed + contract_last(sliding_patch, rates_w[rate_index, tap_index])
        pre_list.append(summed)
    pre_parts = jnp.stack(pre_list, axis=1)
    before = lax.psum(pre_parts, "ch") + branch_bias[None]
    hidden = smooth(before).astype(jnp.bfloat16)
    branch_slope = smooth_slope(before).reshape(pixels, 4, 3, HID)
    joined_list = []
    projected_list = []
    top_list = []
    produced = []
    for task_index in range(3):
        joined = hidden[:, :, task_index * HID : (task_index + 1) * HID].reshape(pixels, 4 * HID)
        projected = (
            jnp.dot(joined, proj_w[task_index], preferred_element_type=jnp.float32)
            + proj_bias[task_index]
        )
        top = smooth(projected).astype(jnp.bfloat16)
        produced.append(jnp.dot(top, out_weights[task_index], preferred_element_type=jnp.float32))
        joined_list.append(joined)
        projected_list.append(projected)
        top_list.append(top)
    logits = produced[0] + sem_b
    depth_pred = produced[1] + depth_b
    normal_pred = produced[2] + normal_b
    slopes = loss_slopes(
        logits,
        depth_pred,
        normal_pred,
        sem_label,
        depth_target,
        normal_target,
        label_mask,
        task_counts,
    )
    out_grads = []
    out_bias_grads = []
    proj_grads = []
    proj_bias_grads = []
    joined_backs = []
    for task_index in range(3):
        top_back = contract_last(slopes[task_index], out_weights[task_index])
        proj_back = (top_back * smooth_slope(projected_list[task_index])).astype(jnp.bfloat16)
        out_grads.append(contract_first(top_list[task_index], slopes[task_index]))
        out_bias_grads.append(jnp.sum(slopes[task_index], axis=0, dtype=jnp.float32))
        proj_grads.append(contract_first(joined_list[task_index], proj_back))
        proj_bias_grads.append(jnp.sum(proj_back, axis=0, dtype=jnp.float32))
        joined_backs.append(contract_last(proj_back, proj_w[task_index]).reshape(pixels, 4, HID))
    joined_back = jnp.stack(joined_backs, axis=2)
    pre_grad = (joined_back * branch_slope).astype(jnp.bfloat16).reshape(pixels, 4, 3 * HID)
    small_term = (
        pack_small(
            [jnp.sum(pre_grad, axis=0, dtype=jnp.float32), jnp.stack(proj_bias_grads)]
            + out_grads
            + out_bias_grads
        )
        / groups
    )
    proj_grad = jnp.stack(proj_grads)
    first_branch = pre_grad[:, 0]
    task_sum = split_tasks(first_branch, heads_w)
    rates_list = []
    for rate_index, rate in enumerate(aspp_rates):
        flat_back = pre_grad[:, rate_index + 1]
        rate_back = flat_back.reshape(rows_per_shard, columns_per_shard, 3 * HID)
        back_views = (
            row_view(rate_back, rate, fetch_grads),
            rate_back,
            row_view(rate_back, -rate, fetch_grads),
        )
        for tap_index in range(9):
            kernel_row, kernel_column = divmod(tap_index, 3)
            sliding_patch = column_view(
                row_views[rate_index][kernel_row], (kernel_column - 1) * rate
            ).reshape(pixels, wide_dev)
            rates_list.append(contract_first(flat_back, sliding_patch))
            spread = column_view(back_views[kernel_row], (1 - kernel_column) * rate).reshape(
                pixels, 3 * HID
            )
            task_sum = task_sum + split_tasks_rows(spread, rates_w[rate_index, tap_index])
    rates_grad = jnp.stack(rates_list).reshape(3, 9, 3 * HID, wide_dev)
    task_grads = [task_sum[0], task_sum[1], task_sum[2]]
    head_grad = contract_first(shared, first_branch)
    local_gram = jnp.stack(
        [
            jnp.stack(
                [jnp.sum(task_grads[row_task] * task_grads[col_task]) for col_task in range(3)]
            )
            for row_task in range(3)
        ]
    )
    gram = lax.psum(local_gram, ("pix", "ch"))
    alphas = imtl_weights(gram)
    combined = alphas[0] * task_grads[0] + alphas[1] * task_grads[1] + alphas[2] * task_grads[2]
    shared_slope = combined * smooth_slope(summed_in)
    expand_up, gain_three_grad, shift_three_grad = backward_norm(
        shared_slope, hat_three, scale_three, count_all, gain_three
    )
    expand_back = expand_up.astype(jnp.bfloat16)
    expand_grad = contract_first(second_all, expand_back)
    second_back = channel_parts(contract_last(expand_back, expand_w))
    middle_up, gain_two_grad, shift_two_grad = backward_norm(
        second_back * smooth_slope(norm_two), hat_two, scale_two, count_all, gain_two
    )
    middle_gradient = middle_up.astype(jnp.bfloat16)
    dilated_list = []
    for tap_index in range(9):
        kernel_row, kernel_column = divmod(tap_index, 3)
        sliding_patch = bordered_input[
            kernel_row * DILATION_RATE : kernel_row * DILATION_RATE + rows_per_shard,
            kernel_column * DILATION_RATE : kernel_column * DILATION_RATE + columns_per_shard,
        ].reshape(pixels, M)
        dilated_list.append(contract_first(sliding_patch, middle_gradient))
    dilated_grad = jnp.stack(dilated_list)
    canvas_gradient = with_halo(
        middle_gradient.reshape(rows_per_shard, columns_per_shard, middle_per_shard),
        (("pix", 0),),
        DILATION_RATE,
    )
    canvas_gradient = jnp.pad(canvas_gradient, ((0, 0), (DILATION_RATE, DILATION_RATE), (0, 0)))
    first_part = jnp.zeros((pixels, M), jnp.float32)
    for tap_index in range(9):
        kernel_row, kernel_column = divmod(tap_index, 3)
        sliding_patch = canvas_gradient[
            (2 - kernel_row) * DILATION_RATE : (2 - kernel_row) * DILATION_RATE + rows_per_shard,
            (2 - kernel_column) * DILATION_RATE : (2 - kernel_column) * DILATION_RATE
            + columns_per_shard,
        ].reshape(pixels, middle_per_shard)
        first_part = first_part + contract_last(sliding_patch, dilated_w[tap_index])
    first_back = channel_parts(first_part) * mask_flat[:, None] * smooth_slope(norm_one)
    reduce_up, gain_one_grad, shift_one_grad = backward_norm(
        first_back, hat_one, scale_one, count_all, gain_one
    )
    reduce_all = channel_gather(reduce_up.astype(jnp.bfloat16))
    reduce_grad = contract_first(flat_in, reduce_all)
    input_grad = contract_last(reduce_all, reduce_w) + shared_slope
    reduce_shard, dilated_shard, expand_shard, head_shard, rates_shard, proj_shard = (
        lax.psum_scatter(reduce_grad, "pix", scatter_dimension=1, tiled=True),
        lax.psum_scatter(dilated_grad, "pix", scatter_dimension=1, tiled=True),
        lax.psum_scatter(expand_grad, "pix", scatter_dimension=0, tiled=True),
        lax.psum_scatter(head_grad, "pix", scatter_dimension=1, tiled=True),
        lax.psum_scatter(rates_grad, "pix", scatter_dimension=2, tiled=True),
        lax.psum_scatter(proj_grad, "pix", scatter_dimension=1, tiled=True),
    )
    norm_local = jnp.zeros((2, 2 * M + C), jnp.float32)
    for offset, width, gain_grad, shift_grad in (
        (0, middle_per_shard, gain_one_grad, shift_one_grad),
        (M, middle_per_shard, gain_two_grad, shift_two_grad),
        (2 * M, wide_dev, gain_three_grad, shift_three_grad),
    ):
        norm_local = lax.dynamic_update_slice(
            norm_local, jnp.stack([gain_grad, shift_grad]), (0, offset + block_id * width)
        )
    big_local = (
        jnp.sum(reduce_shard * reduce_shard)
        + jnp.sum(dilated_shard * dilated_shard)
        + jnp.sum(expand_shard * expand_shard)
        + jnp.sum(head_shard * head_shard)
        + jnp.sum(rates_shard * rates_shard)
        + jnp.sum(proj_shard * proj_shard) / groups
    )
    big_squares, norm_grad, small_grad = lax.psum(
        (big_local, norm_local / pix_devices, small_term), ("pix", "ch")
    )
    grad_norm = jnp.sqrt(
        big_squares + jnp.sum(norm_grad * norm_grad) + jnp.sum(small_grad * small_grad)
    )
    factor = jnp.minimum(1.0, CLIP_NORM / (grad_norm + 1e-06))
    reduce_new, reduce_first, reduce_second = adam_step(
        w_reduce, m_reduce, v_reduce, reduce_shard * factor, RATE_MATRIX, DECAY
    )
    dilated_new, dilated_first, dilated_second = adam_step(
        w_dilated, m_dilated, v_dilated, dilated_shard * factor, RATE_MATRIX, DECAY
    )
    expand_new, expand_first, expand_second = adam_step(
        w_expand, m_expand, v_expand, expand_shard * factor, RATE_MATRIX, DECAY
    )
    head_new, head_first, head_second = adam_step(
        head_weight, m_head, v_head, head_shard * factor, RATE_MATRIX, DECAY
    )
    rates_new, rates_first, rates_second = adam_step(
        head_rates, m_rates, v_rates, rates_shard * factor, RATE_MATRIX, DECAY
    )
    proj_new, proj_first, proj_second = adam_step(
        head_proj, m_proj, v_proj, proj_shard * factor, RATE_MATRIX, DECAY
    )
    norm_new, norm_first, norm_second = adam_step(
        norm_params, norm_m, norm_v, norm_grad * factor, RATE_SMALL, 0.0
    )
    small_new, small_first, small_second = adam_step(
        head_small, small_m, small_v, small_grad * factor, RATE_SMALL, 0.0
    )
    depth_bias_grad = small_grad[small_grad.shape[0] - 4]
    return (
        shared.reshape(rows_per_shard, columns_per_shard, wide_dev),
        input_grad.reshape(rows_per_shard, columns_per_shard, wide_dev),
        grad_norm,
        reduce_new,
        reduce_first,
        reduce_second,
        reduce_new.astype(jnp.bfloat16),
        dilated_new,
        dilated_first,
        dilated_second,
        dilated_new.astype(jnp.bfloat16),
        expand_new,
        expand_first,
        expand_second,
        expand_new.astype(jnp.bfloat16),
        head_new,
        head_first,
        head_second,
        head_new.astype(jnp.bfloat16),
        rates_new,
        rates_first,
        rates_second,
        rates_new.astype(jnp.bfloat16),
        proj_new,
        proj_first,
        proj_second,
        proj_new.astype(jnp.bfloat16),
        norm_new,
        norm_first,
        norm_second,
        small_new,
        small_first,
        small_second,
        depth_bias_grad,
    )


def solution(mesh):
    placed = (
        P("pix", None, "ch"),
        P("pix", None),
        P("pix", None),
        P("pix", None),
        P(None, "pix", None),
        P(None, "pix", None),
        P("ch", "pix"),
        P("ch", "pix"),
        P("ch", "pix"),
        P(None, "pix", "ch"),
        P(None, "pix", "ch"),
        P(None, "pix", "ch"),
        P("pix", "ch"),
        P("pix", "ch"),
        P("pix", "ch"),
        P("ch", "pix"),
        P("ch", "pix"),
        P("ch", "pix"),
        P(None, None, "pix", "ch"),
        P(None, None, "pix", "ch"),
        P(None, None, "pix", "ch"),
        P(None, "pix", None),
        P(None, "pix", None),
        P(None, "pix", None),
        P(),
        P(),
        P(),
        P(),
        P(),
        P(),
    )
    return jax.shard_map(
        per_device,
        mesh=mesh,
        in_specs=placed,
        out_specs=(
            P("pix", None, "ch"),
            P("pix", None, "ch"),
            P(),
            P("ch", "pix"),
            P("ch", "pix"),
            P("ch", "pix"),
            P("ch", "pix"),
            P(None, "pix", "ch"),
            P(None, "pix", "ch"),
            P(None, "pix", "ch"),
            P(None, "pix", "ch"),
            P("pix", "ch"),
            P("pix", "ch"),
            P("pix", "ch"),
            P("pix", "ch"),
            P("ch", "pix"),
            P("ch", "pix"),
            P("ch", "pix"),
            P("ch", "pix"),
            P(None, None, "pix", "ch"),
            P(None, None, "pix", "ch"),
            P(None, None, "pix", "ch"),
            P(None, None, "pix", "ch"),
            P(None, "pix", None),
            P(None, "pix", None),
            P(None, "pix", None),
            P(None, "pix", None),
            P(),
            P(),
            P(),
            P(),
            P(),
            P(),
            P(),
        ),
        check_vma=False,
    )
```

profile of v0, /device:TPU:0, one launch (start us, length us, event | category | flops | bytes accessed | tf_op | source)
XLA Modules:
  0.0 2224.3 jit_solution(11313403866060531616)
XLA Ops:
  9.1 33.0 %all_gather.27 = bf16[512,512]{0,1:T(8,128)(2,1)S(1)} all-gather(bf16[512,64]{0,1:T(8,128)(2,1)S(1)} %convert_element_type.211), channel_id=1, replica_groups=mesh['pix'=8,'ch'=4] {'pix'}, dimensions={1}, use_global_device_ids=true | all-gather | bytes 589824 | tf_op jit(solution)/shard_map/all_gather | solution.py:269
  54.1 33.3 %all_gather.32 = bf16[512,768]{0,1:T(8,128)(2,1)S(1)} all-gather(bf16[512,96]{0,1:T(8,128)(2,1)S(1)} %convert_element_type.221), channel_id=1, replica_groups=mesh['pix'=8,'ch'=4] {'pix'}, dimensions={1}, use_global_device_ids=true | all-gather | bytes 884736 | tf_op jit(solution)/shard_map/all_gather | solution.py:272
  88.9 21.2 all-reduce.23
  120.5 26.9 %collective-permute-start = (bf16[4,128,512]{2,1,0:T(8,128)(2,1)S(1)}, bf16[4,128,512]{2,1,0:T(8,128)(2,1)S(1)}, u32[]{:S(2)}, u32[]{:S(2)}) collective-permute-start(bf16[4,128,512]{2,1,0:T(8,128)(2,1)S(1)} %bitcast.717), channel_id=1, source_target_pairs={{0,4},{4,8},{8,12},{12,16},{16,20},{20,24},{24,28},{1,5},{5,9},{9,... | collective-permute-start | bytes 1572872 | tf_op jit(solution)/shard_map/ppermute | solution.py:39
  149.7 80.0 %all_gather.31 = bf16[512,512]{1,0:T(8,128)(2,1)S(1)} all-gather(bf16[64,512]{1,0:T(8,128)(2,1)S(1)} %convert_element_type.217), channel_id=1, replica_groups=mesh['pix'=8,'ch'=4] {'pix'}, dimensions={0}, use_global_device_ids=true | all-gather | bytes 589824 | tf_op jit(solution)/shard_map/all_gather | solution.py:271
  235.5 26.0 %all-reduce.22 = (f32[128]{0:T(128)S(1)}, f32[128]{0:T(128)S(1)}) all-reduce(f32[128]{0:T(128)S(1)} %get-tuple-element.49, f32[128]{0:T(128)S(1)} %get-tuple-element.48), channel_id=1, replica_groups=mesh['pix'=8,'ch'=4] {'pix'}, use_global_device_ids=true, to_apply=%region_8.9 | all-reduce | flops 256 | bytes 2048 | tf_op jit(solution)/shard_map/psum | solution.py:171
  270.6 28.5 %all-reduce.21 = (f32[512]{0:T(512)S(1)}, f32[512]{0:T(512)S(1)}, f32[3]{0:T(128)S(1)}) all-reduce(f32[512]{0:T(512)S(1)} %get-tuple-element.43, f32[512]{0:T(512)S(1)} %get-tuple-element.42, f32[3]{0:T(128)S(1)} %copy-done.179), channel_id=1, replica_groups=mesh['pix'=8,'ch'=4] {'pix'}, use_global_device_ids=true, to_apply=%region_12.13 | all-reduce | flops 1027 | bytes 8216 | tf_op jit(solution)/shard_map/psum | solution.py:171
  321.3 34.3 %collective-permute-done.2 = bf16[4,128,512]{2,1,0:T(8,128)(2,1)S(1)} collective-permute-done((bf16[4,128,512]{2,1,0:T(8,128)(2,1)S(1)}, bf16[4,128,512]{2,1,0:T(8,128)(2,1)S(1)}, u32[]{:S(2)}, u32[]{:S(2)}) %collective-permute-start.2) | collective-permute-done | bytes 524320 | tf_op jit(solution)/shard_map/ppermute | solution.py:28
  360.4 185.7 %all-gather.6.cloned.1.call-done = bf16[3,9,768,512]{3,2,1,0:T(8,128)(2,1)} async-done(((bf16[3,9,96,512]{3,2,1,0:T(8,128)(2,1)}), bf16[3,9,768,512]{3,2,1,0:T(8,128)(2,1)}) %all-gather.6.cloned.1.call-update) | async-done | bytes 21233680 | tf_op jit(solution)/shard_map/all_gather | solution.py:273
  608.6 9.4 fusion.311
  637.1 99.6 %all-reduce.26.cloned.1.call-done = f32[512,4,768]{2,0,1:T(8,128)} async-done(((f32[512,4,768]{2,0,1:T(8,128)}), f32[512,4,768]{2,0,1:T(8,128)}) %all-reduce.26.cloned.1.call-update) | async-done | bytes 6291472 | tf_op jit(solution)/shard_map/psum | solution.py:350
  907.9 25.6 %add_add_fusion = f32[3,512,512]{2,1,0:T(8,128)S(1)} fusion(f32[3,512,512]{2,1,0:T(8,128)} %fusion.157, f32[3,512,512]{2,1,0:T(8,128)} %fusion.161, f32[3,512,512]{2,1,0:T(8,128)} %fusion.165, f32[3,512,512]{2,1,0:T(8,128)} %fusion.347, f32[3,512,512]{2,1,0:T(8,128)} %fusion.346, f32[3,512,512]{2,1,0:T(8,128)} %fusion.345, f32[3,512,512]{2,1,0:T(8,128)} %fusion.159, ...), kind=kOutput, calls=%fused_computation.24 | convolution fusion | flops 423886848 | bytes 89653248 | tf_op jit(solution)/shard_map/dot_general | solution.py:80
  941.0 45.7 %psum.134 = f32[3,3]{1,0:T(4,128)S(1)} all-reduce(f32[3,3]{1,0:T(4,128)S(1)} %pad_maximum_fusion.4), channel_id=1, replica_groups=mesh['pix'=8,'ch'=4] {'pix','ch'}, use_global_device_ids=true, to_apply=%region_24.25 | all-reduce | flops 9 | bytes 72 | tf_op jit(solution)/shard_map/psum | solution.py:437
  1004.3 20.6 all-reduce.20
  1030.2 21.5 reduce-scatter.12.cloned.1.call-done
  1052.8 21.4 all-reduce.19
  1123.3 20.2 all-reduce.18
  1203.3 43.1 %reduce-scatter.22.cloned.1.call-done = f32[512,96]{0,1:T(8,128)} async-done(((f32[512,768]{0,1:T(8,128)}), f32[512,96]{0,1:T(8,128)}) %reduce-scatter.22.cloned.1.call-update) | async-done | bytes 196624 | tf_op jit(solution)/shard_map/reduce_scatter | solution.py:486
  1248.7 76.3 %reduce-scatter.26.cloned.1.call-done = f32[3,128,256]{2,1,0:T(8,128)} async-done(((f32[3,1024,256]{2,1,0:T(8,128)}), f32[3,128,256]{2,1,0:T(8,128)}) %reduce-scatter.26.cloned.1.call-update) | async-done | bytes 393232 | tf_op jit(solution)/shard_map/reduce_scatter | solution.py:488
  1327.4 64.6 %reduce-scatter.16.cloned.1.call-done = f32[512,64]{0,1:T(8,128)} async-done(((f32[512,512]{0,1:T(8,128)}), f32[512,64]{0,1:T(8,128)}) %reduce-scatter.16.cloned.1.call-update) | async-done | bytes 131088 | tf_op jit(solution)/shard_map/reduce_scatter | solution.py:483
  1393.5 71.0 %reduce-scatter.18.cloned.1.call-done = f32[9,64,128]{2,1,0:T(8,128)} async-done(((f32[9,512,128]{2,1,0:T(8,128)}), f32[9,64,128]{2,1,0:T(8,128)}) %reduce-scatter.18.cloned.1.call-update) | async-done | bytes 294928 | tf_op jit(solution)/shard_map/reduce_scatter | solution.py:484
  1468.8 671.5 %reduce-scatter.24.cloned.1.call-done = f32[3,9,96,512]{3,2,1,0:T(8,128)} async-done(((f32[3,9,768,512]{3,2,1,0:T(8,128)}), f32[3,9,96,512]{3,2,1,0:T(8,128)}) %reduce-scatter.24.cloned.1.call-update) | async-done | bytes 5308432 | tf_op jit(solution)/shard_map/reduce_scatter | solution.py:487
  2147.0 40.7 %all-reduce.17 = (f32[]{:T(128)}, f32[2,3072]{1,0:T(2,128)S(1)}, f32[9751]{0:T(1024)S(1)}) all-reduce(f32[]{:T(128)S(6)} %add.805, f32[2,3072]{1,0:T(2,128)} %broadcast_multiply_fusion.1, f32[9751]{0:T(1024)} %broadcast_multiply_fusion), channel_id=1, replica_groups=mesh['pix'=8,'ch'=4] {'pix','ch'}, use_global_device_ids=true, to_apply=%region_51.52 | all-reduce | flops 15896 | bytes 127168 | tf_op jit(solution)/shard_map/psum | solution.py:507
  2203.2 11.9 fusion.293
  (737 shorter events, 474.8 us)
Async XLA Ops:
  8.1 79.8 %reduce-scatter.10.cloned.1.call-start = ((), (), s32[]{:S(2)}) async-start(), calls=%async_computation.9 | async-start | bytes 1310720 | tf_op jit(solution)/shard_map/reduce_scatter | solution.py:276
  45.4 184.4 %all-gather.4.cloned.1.call-start = ((), (), s32[]{:S(2)}) async-start(), calls=%async_computation.10 | async-start | bytes 1327104 | tf_op jit(solution)/shard_map/all_gather | solution.py:270
  46.1 499.9 %all-gather.6.cloned.1.call-start = ((), (), s32[]{:S(2)}) async-start(), calls=%async_computation.11 | async-start | bytes 23887872 | tf_op jit(solution)/shard_map/all_gather | solution.py:273
  50.7 555.3 %all-gather.8.cloned.1.call-start = ((), (), s32[]{:S(2)}) async-start(), calls=%async_computation.13 | async-start | bytes 1769472 | tf_op jit(solution)/shard_map/all_gather | solution.py:274
  51.5 685.2 %all-reduce.26.cloned.1.call-start = ((), (), s32[]{:S(2)}) async-start(), calls=%async_computation.12 | async-start | bytes 12582912 | tf_op jit(solution)/shard_map/psum | solution.py:350
  119.2 111.9 %collective-permute-start.1 = (bf16[4,128,512]{2,1,0:T(8,128)(2,1)S(1)}, bf16[4,128,512]{2,1,0:T(8,128)(2,1)S(1)}, u32[]{:S(2)}, u32[]{:S(2)}) collective-permute-start(bf16[4,128,512]{2,1,0:T(8,128)(2,1)S(1)} %bitcast.716), channel_id=1, source_target_pairs={{4,0},{8,4},{12,8},{16,12},{20,16},{24,20},{28,24},{5,1},{9,5},{13... | collective-permute-start | bytes 1572872 | tf_op jit(solution)/shard_map/ppermute | solution.py:41
  120.5 110.6 %collective-permute-start = (bf16[4,128,512]{2,1,0:T(8,128)(2,1)S(1)}, bf16[4,128,512]{2,1,0:T(8,128)(2,1)S(1)}, u32[]{:S(2)}, u32[]{:S(2)}) collective-permute-start(bf16[4,128,512]{2,1,0:T(8,128)(2,1)S(1)} %bitcast.717), channel_id=1, source_target_pairs={{0,4},{4,8},{8,12},{12,16},{16,20},{20,24},{24,28},{1,5},{5,9},{9,... | collective-permute-start | bytes 1572872 | tf_op jit(solution)/shard_map/ppermute | solution.py:39
  300.3 58.9 %collective-permute-start.5 = (bf16[4,128,512]{2,1,0:T(8,128)(2,1)S(1)}, bf16[4,128,512]{2,1,0:T(8,128)(2,1)S(1)}, u32[]{:S(2)}, u32[]{:S(2)}) collective-permute-start(bf16[4,128,512]{2,1,0:T(8,128)(2,1)S(1)} %bitcast.704), channel_id=1, source_target_pairs={{24,0},{28,4},{25,1},{29,5},{26,2},{30,6},{27,3},{31,7}} | collective-permute-start | bytes 1572872 | tf_op jit(solution)/shard_map/ppermute | solution.py:28
  301.6 56.4 %collective-permute-start.4 = (bf16[4,128,512]{2,1,0:T(8,128)(2,1)S(1)}, bf16[4,128,512]{2,1,0:T(8,128)(2,1)S(1)}, u32[]{:S(2)}, u32[]{:S(2)}) collective-permute-start(bf16[4,128,512]{2,1,0:T(8,128)(2,1)S(1)} %bitcast.705), channel_id=1, source_target_pairs={{0,24},{4,28},{1,25},{5,29},{2,26},{6,30},{3,27},{7,31}} | collective-permute-start | bytes 1572872 | tf_op jit(solution)/shard_map/ppermute | solution.py:28
  310.1 46.6 %collective-permute-start.3 = (bf16[4,128,512]{2,1,0:T(8,128)(2,1)S(1)}, bf16[4,128,512]{2,1,0:T(8,128)(2,1)S(1)}, u32[]{:S(2)}, u32[]{:S(2)}) collective-permute-start(bf16[4,128,512]{2,1,0:T(8,128)(2,1)S(1)} %bitcast.706), channel_id=1, source_target_pairs={{12,0},{16,4},{20,8},{24,12},{28,16},{13,1},{17,5},{21,9},{25,13},... | collective-permute-start | bytes 1572872 | tf_op jit(solution)/shard_map/ppermute | solution.py:28
  311.4 44.2 %collective-permute-start.2 = (bf16[4,128,512]{2,1,0:T(8,128)(2,1)S(1)}, bf16[4,128,512]{2,1,0:T(8,128)(2,1)S(1)}, u32[]{:S(2)}, u32[]{:S(2)}) collective-permute-start(bf16[4,128,512]{2,1,0:T(8,128)(2,1)S(1)} %bitcast.707), channel_id=1, source_target_pairs={{0,12},{4,16},{8,20},{12,24},{16,28},{1,13},{5,17},{9,21},{13,25},... | collective-permute-start | bytes 1572872 | tf_op jit(solution)/shard_map/ppermute | solution.py:28
  604.1 447.5 %reduce-scatter.12.cloned.1.call-start = ((), (), s32[]{:S(2)}) async-start(), calls=%async_computation.14 | async-start | bytes 1310720 | tf_op jit(solution)/shard_map/reduce_scatter | solution.py:183
  781.6 68.5 %collective-permute-start.9 = (bf16[4,128,768]{1,0,2:T(4,128)(2,1)}, bf16[4,128,768]{1,0,2:T(4,128)(2,1)}, u32[]{:S(2)}, u32[]{:S(2)}) collective-permute-start(bf16[4,128,768]{1,0,2:T(4,128)(2,1)} %copy.90), channel_id=1, source_target_pairs={{0,24},{4,28},{1,25},{5,29},{2,26},{6,30},{3,27},{7,31}} | collective-permute-start | bytes 2359304 | tf_op jit(solution)/shard_map/ppermute | solution.py:28
  787.8 66.3 %collective-permute-start.8 = (bf16[4,128,768]{1,0,2:T(4,128)(2,1)}, bf16[4,128,768]{1,0,2:T(4,128)(2,1)}, u32[]{:S(2)}, u32[]{:S(2)}) collective-permute-start(bf16[4,128,768]{1,0,2:T(4,128)(2,1)} %copy.90), channel_id=1, source_target_pairs={{24,0},{28,4},{25,1},{29,5},{26,2},{30,6},{27,3},{31,7}} | collective-permute-start | bytes 2359304 | tf_op jit(solution)/shard_map/ppermute | solution.py:28
  793.5 64.5 %collective-permute-start.7 = (bf16[4,128,768]{1,0,2:T(4,128)(2,1)}, bf16[4,128,768]{1,0,2:T(4,128)(2,1)}, u32[]{:S(2)}, u32[]{:S(2)}) collective-permute-start(bf16[4,128,768]{1,0,2:T(4,128)(2,1)} %copy.77), channel_id=1, source_target_pairs={{0,12},{4,16},{8,20},{12,24},{16,28},{1,13},{5,17},{9,21},{13,25},... | collective-permute-start | bytes 2359304 | tf_op jit(solution)/shard_map/ppermute | solution.py:28
  795.7 67.1 %collective-permute-start.6 = (bf16[4,128,768]{1,0,2:T(4,128)(2,1)}, bf16[4,128,768]{1,0,2:T(4,128)(2,1)}, u32[]{:S(2)}, u32[]{:S(2)}) collective-permute-start(bf16[4,128,768]{1,0,2:T(4,128)(2,1)} %copy.77), channel_id=1, source_target_pairs={{12,0},{16,4},{20,8},{24,12},{28,16},{13,1},{17,5},{21,9},{25,13},... | collective-permute-start | bytes 2359304 | tf_op jit(solution)/shard_map/ppermute | solution.py:28
  1030.1 90.7 %reduce-scatter.14.cloned.1.call-start = ((), (), s32[]{:S(2)}) async-start(), calls=%async_computation.15 | async-start | bytes 1310720 | tf_op jit(solution)/shard_map/reduce_scatter | solution.py:183
  1076.1 7.1 collective-permute-start.10
  1088.2 113.6 %reduce-scatter.20.cloned.1.call-start = ((), (), s32[]{:S(2)}) async-start(), calls=%async_computation.18 | async-start | bytes 1179648 | tf_op jit(solution)/shard_map/reduce_scatter | solution.py:485
  1090.9 155.5 %reduce-scatter.22.cloned.1.call-start = ((), (), s32[]{:S(2)}) async-start(), calls=%async_computation.19 | async-start | bytes 1769472 | tf_op jit(solution)/shard_map/reduce_scatter | solution.py:486
  1093.9 231.1 %reduce-scatter.26.cloned.1.call-start = ((), (), s32[]{:S(2)}) async-start(), calls=%async_computation.21 | async-start | bytes 3538944 | tf_op jit(solution)/shard_map/reduce_scatter | solution.py:488
  1099.8 292.2 %reduce-scatter.16.cloned.1.call-start = ((), (), s32[]{:S(2)}) async-start(), calls=%async_computation.16 | async-start | bytes 1179648 | tf_op jit(solution)/shard_map/reduce_scatter | solution.py:483
  1155.0 309.6 %reduce-scatter.18.cloned.1.call-start = ((), (), s32[]{:S(2)}) async-start(), calls=%async_computation.17 | async-start | bytes 2654208 | tf_op jit(solution)/shard_map/reduce_scatter | solution.py:484
  1168.9 971.4 %reduce-scatter.24.cloned.1.call-start = ((), (), s32[]{:S(2)}) async-start(), calls=%async_computation.20 | async-start | bytes 47775744 | tf_op jit(solution)/shard_map/reduce_scatter | solution.py:487
  (200 other events, 7936.4 us)
Sparse Core Ops, SparseCore 0:
  45.5 25.9 reduce-scatter.9
  604.3 132.3 all-reduce.25
  1030.2 21.3 reduce-scatter.11
  1088.3 23.0 reduce-scatter.13
  1115.1 63.5 reduce-scatter.19
  1182.5 63.8 reduce-scatter.21
  1251.0 73.9 reduce-scatter.25
  1329.4 62.5 reduce-scatter.15
  1396.1 68.4 reduce-scatter.17
  1468.3 671.9 reduce-scatter.23
Sparse Core Ops, SparseCore 1:
  48.8 46.9 all-gather.3
  97.8 448.2 all-gather.5
  549.0 57.0 all-gather.7
where the time goes:
time: 2230 us; the launch traced here: 2220 us
  waiting for transfers between devices  1270 us (57%)
  blocking collectives  392 us (18%)
  matrix products  246 us (11%)
  local copies, waits for them, and re-layouts  123 us (6%)
  other arithmetic  91.4 us (4%)
  starting transfers between devices  62.8 us (3%)
  between operations  37.7 us (2%)
    reduce_scatter x1, waiting for transfers between devices, per_device(): lax.psum_scatter(rates_grad, 'pix', scatter_dimension=2, tiled=True)  671 us
    all_gather x1, waiting for transfers between devices, per_device(): lax.all_gather(head_rates.astype(jnp.bfloat16), 'pix', axis=2, tiled=True)  186 us
    psum x1, waiting for transfers between devices, per_device(): before = lax.psum(pre_parts, 'ch') + branch_bias[None]  99.6 us
    dot_general x27, matrix products, split_tasks_rows(): lax.dot_general(slopes.reshape(pixels, 3, -1), weight.reshape(3, -1, weig...  89.9 us
    all_gather x1, blocking collectives, per_device(): lax.all_gather(w_expand.astype(jnp.bfloat16), 'pix', axis=0, tiled=True)  80 us
    reduce_scatter x1, waiting for transfers between devices, per_device(): lax.psum_scatter(proj_grad, 'pix', scatter_dimension=1, tiled=True)  76.3 us
    dot_general x42, matrix products, contract_first(): lax.dot_general(left, right, (((0,), (0,)), ((), ())), preferred_element_...  72.2 us
    reduce_scatter x1, waiting for transfers between devices, per_device(): lax.psum_scatter(dilated_grad, 'pix', scatter_dimension=1, tiled=True)  71 us
  transfers between devices with their start and end apart: 25, of which 12 were waited for; matrix products, arithmetic and copies ran while one was open for 13% of the time, Pallas kernels for 0%

commit v1 on v0

--- a/solution.py
+++ b/solution.py
@@ -1,6 +1,8 @@
 import jax
 import jax.numpy as jnp
 from jax import lax
+from jax.experimental import pallas as pl
+from jax.experimental.pallas import tpu as pltpu
 from jax.sharding import PartitionSpec as P
 
 C = 2048
@@ -218,7 +220,7 @@
     )
 
 
-def per_device(
+def per_device_plain(
     features,
     valid_mask,
     sem_label,
@@ -574,6 +576,999 @@
     )
 
 
+MESH = pl.DeviceIdType.MESH
+BF = jnp.bfloat16
+F32 = jnp.float32
+NPIX = 8
+NCH = 4
+ROWS = 4
+WIDTH = 128
+PX = ROWS * WIDTH
+CIN = C // NCH
+COLS = 3 * HID // NPIX
+SEGS = COLS // 32
+VMEM_LIMIT = 60 * 2**20
+
+
+def row_groups():
+    groups = []
+    for rate_index, rate in enumerate(aspp_rates):
+        for step in (-1, 0, 1):
+            if abs(step) * rate // ROWS < NPIX:
+                groups.append((rate_index, step))
+    return groups
+
+
+GROUPS = row_groups()
+TAPS = 1 + 3 * len(GROUPS)
+SEG_ROWS = TAPS * 32
+
+
+def whole_vmem():
+    return pl.BlockSpec(memory_space=pltpu.VMEM)
+
+
+def slide(tile, steps):
+    lane = lax.broadcasted_iota(jnp.int32, tile.shape, 1)
+    if steps == 0:
+        return tile
+    rolled = pltpu.roll(tile, steps % WIDTH, 1)
+    if steps > 0:
+        return jnp.where(lane >= steps, rolled, 0.0)
+    return jnp.where(lane < WIDTH + steps, rolled, 0.0)
+
+
+def tanh_parts(values):
+    root = 0.7978845608028654
+    inner = jnp.tanh(root * (values + 0.044715 * values * values * values))
+    return root, inner
+
+
+def gelu_of(values):
+    _, inner = tanh_parts(values)
+    return 0.5 * values * (1.0 + inner)
+
+
+def gelu_slope(values):
+    root, inner = tanh_parts(values)
+    return 0.5 * (1.0 + inner) + 0.5 * values * (1.0 - inner * inner) * root * (
+        1.0 + 3.0 * 0.044715 * values * values
+    )
+
+
+def nt_dot(left, right):
+    return lax.dot_general(left, right, (((1,), (1,)), ((), ())), preferred_element_type=F32)
+
+
+def nn_dot(left, right):
+    return lax.dot_general(left, right, (((1,), (0,)), ((), ())), preferred_element_type=F32)
+
+
+def greet(targets):
+    barrier = pltpu.get_barrier_semaphore()
+    for target in targets:
+        pl.semaphore_signal(barrier, inc=1, device_id=target, device_id_type=MESH)
+    pl.semaphore_wait(barrier, len(targets))
+
+
+def remote(src, dst, send_sem, recv_sem, target):
+    return pltpu.make_async_remote_copy(
+        src, dst, send_sem, recv_sem, device_id=target, device_id_type=MESH
+    )
+
+
+def place():
+    p = lax.axis_index("pix")
+    c = lax.axis_index("ch")
+    return p, c, p // 2, lax.rem(p, 2), c // 2, lax.rem(c, 2)
+
+
+def heads_forward_kernel(
+    x_ref, w_ref, q_ref, xall_ref,
+    acc, y_tmp, core_buf, core_in, x_buf, x_in, row_buf, local_sem,
+    zr_send, zl_send, z_recv, y_send, y_recv, core_send, core_recv, x_send, x_recv, row_send, row_recv,
+):
+    p, c, z, y, x, core = place()
+    zcount = NPIX // 2
+    up = (2 * lax.rem(z + 1, zcount) + y, c)
+    down = (2 * lax.rem(z + zcount - 1, zcount) + y, c)
+    other_y = (2 * z + 1 - y, c)
+    other_core = (p, 2 * x + 1 - core)
+    other_x = (p, 2 * (1 - x) + core)
+    row_targets = [(lax.rem(p + d, NPIX), c) for d in range(1, NPIX)]
+    greet(row_targets + [other_core, other_x])
+
+    own = pltpu.make_async_copy(x_ref, xall_ref.at[p], local_sem.at[0])
+    own.start()
+
+    def to_up(source):
+        return remote(xall_ref.at[source], xall_ref.at[source], zr_send.at[source // 2], z_recv.at[source // 2], up)
+
+    def to_down(source):
+        return remote(xall_ref.at[source], xall_ref.at[source], zl_send.at[source // 2], z_recv.at[source // 2], down)
+
+    def to_y(source):
+        return remote(xall_ref.at[source], xall_ref.at[source], y_send.at[source // 2], y_recv.at[source // 2], other_y)
+
+    def step_of(i):
+        near = jnp.where(z == 0, i, jnp.where(z == 3, 3 - i, 0))
+        one = jnp.where(i == 0, 1, jnp.where(i == 1, 0, i))
+        two = jnp.where(i == 0, 2, jnp.where(i == 1, 3, 3 - i))
+        two = jnp.where(i == 2, 1, jnp.where(i == 3, 0, two))
+        return jnp.where(z == 1, one, jnp.where(z == 2, two, near))
+
+    acc[...] = jnp.zeros_like(acc)
+    own.wait()
+
+    def process(src):
+        xb = xall_ref[src]
+
+        def one_seg(s, carry):
+            y_tmp[...] = nt_dot(w_ref[s], xb)
+
+            def add_group(dest, branch, first_tap, taps):
+                rows = pl.ds(pl.multiple_of(branch * COLS + s * 32, 32), 32)
+                for r in range(ROWS):
+                    lanes = pl.ds(r * WIDTH, WIDTH)
+                    total = acc[dest, rows, lanes]
+                    for i, shift in enumerate(taps):
+                        tile = y_tmp[pl.ds((first_tap + i) * 32, 32), lanes]
+                        total = total + slide(tile, shift)
+                    acc[dest, rows, lanes] = total
+
+            add_group(src, 0, 0, (0,))
+            for g, (rate_index, step) in enumerate(GROUPS):
+                rate = aspp_rates[rate_index]
+                dest = src - step * (rate // ROWS)
+                shifts = (rate, 0, -rate)
+                if step == 0:
+                    add_group(dest, rate_index + 1, 1 + 3 * g, shifts)
+                else:
+
+                    @pl.when((dest >= 0) & (dest < NPIX))
+                    def _():
+                        add_group(dest, rate_index + 1, 1 + 3 * g, shifts)
+
+            return carry
+
+        lax.fori_loop(0, SEGS, one_seg, 0)
+
+    def gather_step(i, carry):
+        zs = step_of(i)
+        mine = 2 * zs + y
+        theirs = 2 * zs + 1 - y
+
+        @pl.when(i > 0)
+        def _():
+            to_up(mine).wait_recv()
+
+        @pl.when((zs <= z) & (z < zcount - 1))
+        def _():
+            to_up(mine).start()
+
+        @pl.when((zs >= z) & (z > 0))
+        def _():
+            to_down(mine).start()
+
+        to_y(mine).start()
+        process(mine)
+        to_y(theirs).wait_recv()
+        process(theirs)
+        return carry
+
+    lax.fori_loop(0, zcount, gather_step, 0)
+
+    def drain(zs, carry):
+        mine = 2 * zs + y
+
+        @pl.when((zs <= z) & (z < zcount - 1))
+        def _():
+            to_up(mine).wait_send()
+
+        @pl.when((zs >= z) & (z > 0))
+        def _():
+            to_down(mine).wait_send()
+
+        to_y(mine).wait_send()
+        return carry
+
+    lax.fori_loop(0, zcount, drain, 0)
+
+    def lanes_of(ch):
+        return pl.ds(pl.multiple_of(ch * WIDTH, WIDTH), WIDTH)
+
+    def core_copy(b):
+        return remote(core_buf.at[b], core_in.at[b], core_send.at[b], core_recv.at[b], other_core)
+
+    def x_copy(b):
+        return remote(x_buf.at[b], x_in.at[b], x_send.at[b], x_recv.at[b], other_x)
+
+    def row_copy(b, slot):
+        return remote(
+            row_buf.at[b],
+            q_ref.at[:, pl.ds(pl.multiple_of(COLS * p, 32), COLS), :],
+            row_send.at[slot],
+            row_recv.at[slot],
+            (b, c),
+        )
+
+    def core_step(d, carry):
+        b = lax.rem(p + d, NPIX)
+        for xx in range(2):
+            core_buf[b, xx] = acc[b, :, lanes_of(2 * xx + 1 - core)].astype(BF)
+        core_copy(b).start()
+        return carry
+
+    lax.fori_loop(0, NPIX, core_step, 0)
+
+    def x_step(d, carry):
+        b = lax.rem(p + d, NPIX)
+        core_copy(b).wait_recv()
+        x_buf[b] = (acc[b, :, lanes_of(2 * (1 - x) + core)] + core_in[b, 1 - x].astype(F32)).astype(BF)
+        x_copy(b).start()
+        return carry
+
+    lax.fori_loop(0, NPIX, x_step, 0)
+
+    def finish(b):
+        x_copy(b).wait_recv()
+        total = acc[b, :, lanes_of(c)] + core_in[b, x].astype(F32) + x_in[b].astype(F32)
+        return total.astype(BF).reshape(4, COLS, WIDTH)
+
+    def row_step(d, carry):
+        b = lax.rem(p + d, NPIX)
+        row_buf[b] = finish(b)
+        row_copy(b, d - 1).start()
+        return carry
+
+    lax.fori_loop(1, NPIX, row_step, 0)
+    q_ref[:, pl.ds(pl.multiple_of(COLS * p, 32), COLS), :] = finish(p)
+
+    def settle(d, carry):
+        b = lax.rem(p + d, NPIX)
+        row_copy(b, d - 1).wait()
+        return carry
+
+    lax.fori_loop(1, NPIX, settle, 0)
+
+    def settle_more(b, carry):
+        core_copy(b).wait_send()
+        x_copy(b).wait_send()
+        return carry
+
+    lax.fori_loop(0, NPIX, settle_more, 0)
+
+
+def heads_forward(block_out, w_seg):
+    dma = pltpu.SemaphoreType.DMA
+    zc = NPIX // 2
+    return pl.pallas_call(
+        heads_forward_kernel,
+        out_shape=(
+            jax.ShapeDtypeStruct((4, 3 * HID, WIDTH), BF),
+            jax.ShapeDtypeStruct((NPIX, PX, CIN), BF),
+        ),
+        in_specs=[whole_vmem()] * 2,
+        out_specs=[whole_vmem()] * 2,
+        scratch_shapes=[
+            pltpu.VMEM((NPIX, 4 * COLS, PX), F32),
+            pltpu.VMEM((SEG_ROWS, PX), F32),
+            pltpu.VMEM((NPIX, 2, 4 * COLS, WIDTH), BF),
+            pltpu.VMEM((NPIX, 2, 4 * COLS, WIDTH), BF),
+            pltpu.VMEM((NPIX, 4 * COLS, WIDTH), BF),
+            pltpu.VMEM((NPIX, 4 * COLS, WIDTH), BF),
+            pltpu.VMEM((NPIX, 4, COLS, WIDTH), BF),
+            dma((1,)),
+            dma((zc,)), dma((zc,)), dma((zc,)), dma((zc,)), dma((zc,)),
+            dma((NPIX,)), dma((NPIX,)), dma((NPIX,)), dma((NPIX,)),
+            dma((NPIX - 1,)), dma((NPIX - 1,)),
+        ],
+        compiler_params=pltpu.CompilerParams(
+            collective_id=1, has_side_effects=True, vmem_limit_bytes=VMEM_LIMIT
+        ),
+        name="heads_forward",
+    )(block_out, w_seg)
+
+
+def heads_middle_kernel(
+    q_ref, bias_ref, pbias_ref, wpt_ref, wot_ref, obias_ref, label_ref, target_ref, mask_ref, count_ref,
+    dq_ref, dwp_ref, dwo_ref, rows_ref, obg_ref,
+    hid,
+):
+    ones = jnp.ones((8, WIDTH), BF)
+    for k in range(4):
+        hid[k] = gelu_of(q_ref[k].astype(F32) + bias_ref[:, k : k + 1]).astype(BF)
+    row = lax.broadcasted_iota(jnp.int32, (32, WIDTH), 0)
+    for t in range(3):
+        cols = slice(t * HID, (t + 1) * HID)
+        zt = pbias_ref[:, t : t + 1] + jnp.zeros((HID, WIDTH), F32)
+        for k in range(4):
+            zt = zt + nn_dot(wpt_ref[t, :, k * HID : (k + 1) * HID], hid[k, cols, :])
+        ut = gelu_of(zt).astype(BF)
+        out = lax.dot_general(
+            wot_ref[t], ut, (((0,), (0,)), ((), ())), preferred_element_type=F32
+        ) + obias_ref[:, t : t + 1]
+        scale = mask_ref[t : t + 1, :] / count_ref[t : t + 1, :]
+        if t == 0:
+            live = row < NCLS
+            highest = jnp.max(jnp.where(live, out, -1e30), axis=0, keepdims=True)
+            raised = jnp.where(live, jnp.exp(jnp.minimum(out - highest, 0.0)), 0.0)
+            probs = raised / jnp.sum(raised, axis=0, keepdims=True)
+            onehot = (row == label_ref[0:1, :]).astype(F32)
+            slope = scale * (probs - onehot)
+        elif t == 1:
+            gap = out - target_ref[0:1, :]
+            slope = jnp.where(row < 1, scale * gap / jnp.sqrt(gap * gap + 1.0), 0.0)
+        else:
+            target = jnp.zeros((32, WIDTH), F32)
+            for i in range(3):
+                target = jnp.where(row == i, target_ref[1 + i : 2 + i, :], target)
+            slope = jnp.where(row < 3, scale * (out - target), 0.0)
+        ot = slope.astype(BF)
+        dwo_ref[t] = nt_dot(ot, ut)
+        obg_ref[t] = nt_dot(ones, ot)
+        dz = (nn_dot(wot_ref[t], ot) * gelu_slope(zt)).astype(BF)
+        rows_ref[4, :, cols] = nt_dot(ones, dz)
+        for k in range(4):
+            part = hid[k, cols, :]
+            dwp_ref[t, k * HID : (k + 1) * HID, :] = nt_dot(part, dz)
+            dcat = lax.dot_general(
+                wpt_ref[t, :, k * HID : (k + 1) * HID], dz, (((0,), (0,)), ((), ())),
+                preferred_element_type=F32,
+            )
+            before = q_ref[k, cols, :].astype(F32) + bias_ref[cols, k : k + 1]
+            dq_ref[k, cols, :] = (dcat * gelu_slope(before)).astype(BF)
+    for k in range(4):
+        rows_ref[k] = nt_dot(ones, dq_ref[k])
+
+
+def heads_middle(q, bias, pbias, wpt, wot, obias, label, target, mask, count):
+    return pl.pallas_call(
+        heads_middle_kernel,
+        out_shape=(
+            jax.ShapeDtypeStruct((4, 3 * HID, WIDTH), BF),
+            jax.ShapeDtypeStruct((3, 4 * HID, HID), F32),
+            jax.ShapeDtypeStruct((3, 32, HID), F32),
+            jax.ShapeDtypeStruct((5, 8, 3 * HID), F32),
+            jax.ShapeDtypeStruct((3, 8, 32), F32),
+        ),
+        in_specs=[whole_vmem()] * 10,
+        out_specs=[whole_vmem()] * 5,
+        scratch_shapes=[pltpu.VMEM((4, 3 * HID, WIDTH), BF)],
+        compiler_params=pltpu.CompilerParams(vmem_limit_bytes=VMEM_LIMIT),
+        name="heads_middle",
+    )(q, bias, pbias, wpt, wot, obias, label, target, mask, count)
+
+
+def low_task(zplane):
+    return (2 * zplane * COLS) // HID
+
+
+def heads_backward_kernel(
+    dq_ref, xall_ref, w_ref, dw_ref, gz_ref,
+    dq_all, wt, dcol, parts, y_in, z_buf, z_in, gram_own, gram_ch, gram_px, gsum,
+    local_sem, row_send, row_recv, x_send, x_recv, ca_send, ca_recv, cb_send, cb_recv,
+    y_send, y_recv, z_send, z_recv, gc_send, gc_recv, gp_send, gp_recv,
+):
+    p, c, z, y, x, core = place()
+    zcount = NPIX // 2
+    other_y = (2 * z + 1 - y, c)
+    other_core = (p, 2 * x + 1 - core)
+    other_x = (p, 2 * (1 - x) + core)
+    pix_targets = [(lax.rem(p + d, NPIX), c) for d in range(1, NPIX)]
+    ch_targets = [(p, lax.rem(c + d, NCH)) for d in range(1, NCH)]
+    greet(pix_targets + ch_targets)
+
+    def cols_of(b):
+        return pl.ds(pl.multiple_of(COLS * b, 32), COLS)
+
+    def row_copy(d):
+        b = lax.rem(p + d, NPIX)
+        return remote(dq_ref.at[:, cols_of(b), :], dq_all.at[p, c], row_send.at[d - 1], row_recv.at[d - 1], (b, c))
+
+    for d in range(1, NPIX):
+        row_copy(d).start()
+    own = pltpu.make_async_copy(dq_ref.at[:, cols_of(p), :], dq_all.at[p, c], local_sem.at[0])
+    own.start()
+    for s in range(SEGS):
+        wt[s] = jnp.transpose(w_ref[s].astype(F32)).astype(BF)
+    dw_ref[...] = jnp.zeros_like(dw_ref)
+    own.wait()
+
+    def x_copy(d, b, ch):
+        return remote(dq_all.at[b, ch], dq_all.at[b, ch], x_send.at[d], x_recv.at[d], other_x)
+
+    def ca_copy(d, b, ch):
+        return remote(dq_all.at[b, ch], dq_all.at[b, ch], ca_send.at[d], ca_recv.at[d], other_core)
+
+    def cb_copy(d, b, ch):
+        return remote(dq_all.at[b, ch], dq_all.at[b, ch], cb_send.at[d], cb_recv.at[d], other_core)
+
+    far = 2 * (1 - x) + core
+    for d in range(NPIX):
+        b = lax.rem(p + NPIX - d, NPIX)
+        if d > 0:
+            row_copy(d).wait_recv()
+        x_copy(d, b, c).start()
+        ca_copy(d, b, c).start()
+    for d in range(NPIX):
+        b = lax.rem(p + NPIX - d, NPIX)
+        x_copy(d, b, far).wait_recv()
+        cb_copy(d, b, far).start()
+    for d in range(NPIX):
+        b = lax.rem(p + NPIX - d, NPIX)
+        ca_copy(d, b, 2 * x + 1 - core).wait_recv()
+        cb_copy(d, b, 2 * (1 - x) + 1 - core).wait_recv()
+
+    def task_of(pixel_device, s):
+        return (SEGS * pixel_device + s) // (HID // 32)
+
+    in_low = [task_of(p, s) == low_task(z) for s in range(SEGS)]
+    other_p = 2 * z + 1 - y
+
+    def has_low(device):
+        return task_of(device, 0) == low_task(z)
+
+    def has_high(device):
+        return task_of(device, SEGS - 1) != low_task(z)
+
+    def y_copy(zz, slot):
+        return remote(
+            parts.at[2 * zz + 1 - y, slot], y_in.at[zz, slot],
+            y_send.at[zz, slot], y_recv.at[zz, slot], other_y,
+        )
+
+    def block_step(i, carry):
+        zz = lax.rem(i, zcount)
+        b = jnp.where(i < zcount, 2 * zz + 1 - y, 2 * zz + y)
+
+        def fill(source, branch, first_tap, shifts):
+            for r in range(ROWS):
+                lanes = pl.ds(r * WIDTH, WIDTH)
+                tile = dq_all[source, r, branch].astype(F32)
+                for t, shift in enumerate(shifts):
+                    moved = slide(tile, shift).astype(BF)
+                    for s in range(SEGS):
+                        dcol[s, pl.ds((first_tap + t) * 32, 32), lanes] = moved[s * 32 : (s + 1) * 32]
+
+        fill(b, 0, 0, (0,))
+        for g, (rate_index, step) in enumerate(GROUPS):
+            rate = aspp_rates[rate_index]
+            source = b - step * (rate // ROWS)
+            shifts = (-rate, 0, rate)
+            if step == 0:
+                fill(source, rate_index + 1, 1 + 3 * g, shifts)
+            else:
+                inside = (source >= 0) & (source < NPIX)
+
+                @pl.when(inside)
+                def _():
+                    fill(source, rate_index + 1, 1 + 3 * g, shifts)
+
+                @pl.when(jnp.logical_not(inside))
+                def _():
+                    for s in range(SEGS):
+                        dcol[s, pl.ds((1 + 3 * g) * 32, 96), :] = jnp.zeros((96, PX), BF)
+
+        def product_rows(m, inner):
+            rows = pl.ds(pl.multiple_of(m * 128, 128), 128)
+            low = jnp.zeros((128, PX), F32)
+            high = jnp.zeros((128, PX), F32)
+            for s in range(SEGS):
+                value = nn_dot(wt[s, rows, :], dcol[s])
+                low = low + jnp.where(in_low[s], value, 0.0)
+                high = high + jnp.where(in_low[s], 0.0, value)
+            parts[b, 0, rows, :] = low.astype(BF)
+            parts[b, 1, rows, :] = high.astype(BF)
+            return inner
+
+        lax.fori_loop(0, CIN // 128, product_rows, 0)
+
+        @pl.when((i < zcount) & has_low(p))
+        def _():
+            y_copy(zz, 0).start()
+
+        @pl.when((i < zcount) & has_high(p))
+        def _():
+            y_copy(zz, 1).start()
+
+        def weight_rows(m, inner):
+            s = m // 2
+            rows = pl.ds(pl.multiple_of(lax.rem(m, 2) * (SEG_ROWS // 2), 32), SEG_ROWS // 2)
+            dw_ref[s, rows, :] += nn_dot(dcol[s, rows, :], xall_ref[b])
+            return inner
+
+        lax.fori_loop(0, 2 * SEGS, weight_rows, 0)
+        return carry
+
+    lax.fori_loop(0, NPIX, block_step, 0)
+
+    def z_copy(d, slot):
+        zz = lax.rem(z + d, zcount)
+        return remote(
+            z_buf.at[zz, slot], z_in.at[z, slot],
+            z_send.at[d - 1, slot], z_recv.at[d - 1, slot], (2 * zz + y, c),
+        )
+
+    pair_high = (z == 1) | (z == 2)
+    for d in (1, 2, 3, 0):
+        zz = lax.rem(z + d, zcount)
+        for slot in range(2):
+            theirs = has_low(other_p) if slot == 0 else has_high(other_p)
+            there = pair_high if slot else (z >= 0)
+
+            @pl.when(theirs)
+            def _():
+                y_copy(zz, slot).wait_recv()
+                z_buf[zz, slot] = (
+                    parts[2 * zz + y, slot].astype(F32) + y_in[zz, slot].astype(F32)
+                ).astype(BF)
+
+            @pl.when(jnp.logical_not(theirs))
+            def _():
+                z_buf[zz, slot] = parts[2 * zz + y, slot]
+
+            if d > 0:
+
+                @pl.when(there)
+                def _():
+                    z_copy(d, slot).start()
+
+    for slot in range(2):
+        z_in[z, slot] = z_buf[z, slot]
+    for d in range(1, zcount):
+        source = lax.rem(z + zcount - d, zcount)
+        for slot in range(2):
+            has = (source == 1) | (source == 2) if slot else (source >= 0)
+
+            @pl.when(has)
+            def _():
+                z_copy(d, slot).wait_recv()
+
+    def task_grads(rows):
+        first = z_in[0, 0, rows, :].astype(F32) + z_in[1, 0, rows, :].astype(F32)
+        second = z_in[1, 1, rows, :].astype(F32) + z_in[2, 0, rows, :].astype(F32)
+        third = z_in[2, 1, rows, :].astype(F32) + z_in[3, 0, rows, :].astype(F32)
+        return first, second, third
+
+    pairs = ((0, 0), (0, 1), (0, 2), (1, 1), (1, 2), (2, 2))
+    gram_own[...] = jnp.zeros_like(gram_own)
+
+    def gram_rows(m, carry):
+        rows = pl.ds(pl.multiple_of(m * 32, 32), 32)
+        grads = task_grads(rows)
+        for i, (a, b) in enumerate(pairs):
+            product = grads[a] * grads[b]
+            gram_own[i] += fold(product)
+        return carry
+
+    def fold(product):
+        total = product[0:8, 0:128]
+        for r in range(4):
+            for l in range(4):
+                if r or l:
+                    total = total + product[8 * r : 8 * r + 8, 128 * l : 128 * l + 128]
+        return total
+
+    lax.fori_loop(0, CIN // 32, gram_rows, 0)
+
+    def gc_copy(d):
+        return remote(gram_own, gram_ch.at[d - 1], gc_send.at[d - 1], gc_recv.at[d - 1], ch_targets[d - 1])
+
+    for d in range(1, NCH):
+        gc_copy(d).start()
+    for d in range(1, NCH):
+        gc_copy(d).wait()
+    gsum[...] = gram_own[...] + gram_ch[0] + gram_ch[1] + gram_ch[2]
+
+    def gp_copy(d):
+        return remote(gsum, gram_px.at[d - 1], gp_send.at[d - 1], gp_recv.at[d - 1], pix_targets[d - 1])
+
+    for d in range(1, NPIX):
+        gp_copy(d).start()
+    for d in range(1, NPIX):
+        gp_copy(d).wait()
+    entry = {}
+    for i, (a, b) in enumerate(pairs):
+        total = gsum[i]
+        for d in range(NPIX - 1):
+            total = total + gram_px[d, i]
+        value = jnp.sum(total, axis=0, keepdims=True)
+        value = jnp.sum(value, axis=1, keepdims=True)
+        entry[(a, b)] = value
+        entry[(b, a)] = value
+    lengths = [jnp.sqrt(entry[(t, t)] + 1e-12) for t in range(3)]
+
+    def pairing(row_task, col_task):
+        return (
+            entry[(0, 0)] / lengths[0]
+            - entry[(0, col_task)] / lengths[col_task]
+            - entry[(row_task, 0)] / lengths[0]
+            + entry[(row_task, col_task)] / lengths[col_task]
+        )
+
+    right_one = entry[(0, 0)] / lengths[0] - entry[(0, 1)] / lengths[1]
+    right_two = entry[(0, 0)] / lengths[0] - entry[(0, 2)] / lengths[2]
+    upper_left, upper_right = pairing(1, 1), pairing(1, 2)
+    lower_left, lower_right = pairing(2, 1), pairing(2, 2)
+    determinant = upper_left * lower_right - upper_right * lower_left
+    alpha_one = (right_one * lower_right - right_two * lower_left) / determinant
+    alpha_two = (right_two * upper_left - right_one * upper_right) / determinant
+    alpha_zero = 1.0 - alpha_one - alpha_two
+
+    for m in range(CIN // 128):
+        first, second, third = task_grads(pl.ds(m * 128, 128))
+        mixed = alpha_zero * first + alpha_one * second + alpha_two * third
+        gz_ref[:, m * 128 : (m + 1) * 128] = jnp.transpose(mixed)
+
+    for d in range(1, NPIX):
+        row_copy(d).wait_send()
+    for d in range(NPIX):
+        b = lax.rem(p + NPIX - d, NPIX)
+        x_copy(d, b, c).wait_send()
+        ca_copy(d, b, c).wait_send()
+        cb_copy(d, b, far).wait_send()
+    for zz in range(zcount):
+
+        @pl.when(has_low(p))
+        def _():
+            y_copy(zz, 0).wait_send()
+
+        @pl.when(has_high(p))
+        def _():
+            y_copy(zz, 1).wait_send()
+
+    for d in range(1, zcount):
+        z_copy(d, 0).wait_send()
+
+        @pl.when(pair_high)
+        def _():
+            z_copy(d, 1).wait_send()
+
+
+def heads_backward(dq, xall, w_seg):
+    dma = pltpu.SemaphoreType.DMA
+    zc = NPIX // 2
+    return pl.pallas_call(
+        heads_backward_kernel,
+        out_shape=(
+            jax.ShapeDtypeStruct((SEGS, SEG_ROWS, CIN), F32),
+            jax.ShapeDtypeStruct((PX, CIN), F32),
+        ),
+        in_specs=[whole_vmem()] * 3,
+        out_specs=[whole_vmem()] * 2,
+        scratch_shapes=[
+            pltpu.VMEM((NPIX, NCH, 4, COLS, WIDTH), BF),
+            pltpu.VMEM((SEGS, CIN, SEG_ROWS), BF),
+            pltpu.VMEM((SEGS, SEG_ROWS, PX), BF),
+            pltpu.VMEM((NPIX, 2, CIN, PX), BF),
+            pltpu.VMEM((zc, 2, CIN, PX), BF),
+            pltpu.VMEM((zc, 2, CIN, PX), BF),
+            pltpu.VMEM((zc, 2, CIN, PX), BF),
+            pltpu.VMEM((6, 8, 128), F32),
+            pltpu.VMEM((NCH - 1, 6, 8, 128), F32),
+            pltpu.VMEM((NPIX - 1, 6, 8, 128), F32),
+            pltpu.VMEM((6, 8, 128), F32),
+            dma((1,)),
+            dma((NPIX - 1,)), dma((NPIX - 1,)),
+            dma((NPIX,)), dma((NPIX,)), dma((NPIX,)), dma((NPIX,)), dma((NPIX,)), dma((NPIX,)),
+            dma((zc, 2)), dma((zc, 2)),
+            dma((zc - 1, 2)), dma((zc - 1, 2)),
+            dma((NCH - 1,)), dma((NCH - 1,)),
+            dma((NPIX - 1,)), dma((NPIX - 1,)),
+        ],
+        compiler_params=pltpu.CompilerParams(
+            collective_id=2, has_side_effects=True, vmem_limit_bytes=VMEM_LIMIT
+        ),
+        name="heads_backward",
+    )(dq, xall, w_seg)
+
+
+def tap_weights(head_weight, head_rates):
+    rates = head_rates.astype(BF)
+    pieces = [jnp.transpose(head_weight.astype(BF))[None]]
+    for rate_index, step in GROUPS:
+        pieces.append(rates[rate_index, 3 * (step + 1) : 3 * (step + 2)])
+    taps = jnp.concatenate(pieces, axis=0)
+    taps = taps.reshape(TAPS, SEGS, 32, CIN).transpose(1, 0, 2, 3)
+    return taps.reshape(SEGS, SEG_ROWS, CIN)
+
+
+def tap_grads(dw):
+    taps = dw.reshape(SEGS, TAPS, 32, CIN).transpose(1, 0, 2, 3).reshape(TAPS, COLS, CIN)
+    head = jnp.transpose(taps[0])
+    rates = []
+    for rate_index in range(3):
+        for step in (-1, 0, 1):
+            if (rate_index, step) in GROUPS:
+                g = GROUPS.index((rate_index, step))
+                rates.append(taps[1 + 3 * g : 4 + 3 * g])
+            else:
+                rates.append(jnp.zeros((3, COLS, CIN), F32))
+    return head, jnp.stack(rates).reshape(3, 9, COLS, CIN)
+
+
+def per_device_rows(
+    features,
+    valid_mask,
+    sem_label,
+    depth_target,
+    normal_target,
+    label_mask,
+    w_reduce,
+    m_reduce,
+    v_reduce,
+    w_dilated,
+    m_dilated,
+    v_dilated,
+    w_expand,
+    m_expand,
+    v_expand,
+    head_weight,
+    m_head,
+    v_head,
+    head_rates,
+    m_rates,
+    v_rates,
+    head_proj,
+    m_proj,
+    v_proj,
+    norm_params,
+    norm_m,
+    norm_v,
+    head_small,
+    small_m,
+    small_v,
+):
+    rows_per_shard, columns_per_shard, wide_dev = features.shape
+    pixels = rows_per_shard * columns_per_shard
+    groups = lax.axis_size("ch")
+    block_id = lax.axis_index("ch")
+    pix_devices = lax.axis_size("pix")
+    middle_per_shard = M // groups
+    count_all = float(pixels * pix_devices)
+    flat_in = features.reshape(pixels, wide_dev)
+    mask_flat = valid_mask.reshape(pixels).astype(jnp.float32)
+    gains = norm_params[0]
+    shifts = norm_params[1]
+
+    def owned(vector, offset, width):
+        return lax.dynamic_slice_in_dim(vector, offset + block_id * width, width)
+
+    reduce_w, dilated_w, expand_w = (
+        lax.all_gather(w_reduce.astype(jnp.bfloat16), "pix", axis=1, tiled=True),
+        lax.all_gather(w_dilated.astype(jnp.bfloat16), "pix", axis=1, tiled=True),
+        lax.all_gather(w_expand.astype(jnp.bfloat16), "pix", axis=0, tiled=True),
+    )
+    reduced = lax.psum_scatter(
+        jnp.dot(flat_in, reduce_w, preferred_element_type=jnp.float32),
+        "ch",
+        scatter_dimension=1,
+        tiled=True,
+    )
+    local_counts = jnp.sum(label_mask.astype(jnp.float32), axis=(1, 2))
+    reduced_sum = jnp.sum(reduced, axis=0)
+    reduced_sq = jnp.sum(reduced * reduced, axis=0)
+    reduced_sum, reduced_sq = lax.psum((reduced_sum, reduced_sq), "pix")
+    task_counts = lax.psum(local_counts, "pix")
+    task_counts = jnp.maximum(task_counts, 1.0)
+    gain_one = owned(gains, 0, middle_per_shard)
+    norm_one, hat_one, scale_one = forward_norm(
+        reduced, reduced_sum, reduced_sq, count_all, gain_one, owned(shifts, 0, middle_per_shard)
+    )
+    first = (smooth(norm_one) * mask_flat[:, None]).astype(jnp.bfloat16)
+    first_gathered = channel_gather(first).reshape(rows_per_shard, columns_per_shard, M)
+    bordered_input = with_halo(first_gathered, (("pix", 0),), DILATION_RATE)
+    bordered_input = jnp.pad(bordered_input, ((0, 0), (DILATION_RATE, DILATION_RATE), (0, 0)))
+    middle = jnp.zeros((pixels, middle_per_shard), jnp.float32)
+    for tap_index in range(9):
+        kernel_row, kernel_column = divmod(tap_index, 3)
+        sliding_patch = bordered_input[
+            kernel_row * DILATION_RATE : kernel_row * DILATION_RATE + rows_per_shard,
+            kernel_column * DILATION_RATE : kernel_column * DILATION_RATE + columns_per_shard,
+        ].reshape(pixels, M)
+        middle = middle + jnp.dot(
+            sliding_patch, dilated_w[tap_index], preferred_element_type=jnp.float32
+        )
+    gain_two = owned(gains, M, middle_per_shard)
+    middle_sum, middle_sq = pixel_sums(jnp.sum(middle, axis=0), jnp.sum(middle * middle, axis=0))
+    norm_two, hat_two, scale_two = forward_norm(
+        middle, middle_sum, middle_sq, count_all, gain_two, owned(shifts, M, middle_per_shard)
+    )
+    second = smooth(norm_two).astype(jnp.bfloat16)
+    second_all = channel_gather(second)
+    expanded = jnp.dot(second_all, expand_w, preferred_element_type=jnp.float32)
+    gain_three = owned(gains, 2 * M, wide_dev)
+    expand_sum, expand_sq = pixel_sums(
+        jnp.sum(expanded, axis=0), jnp.sum(expanded * expanded, axis=0)
+    )
+    norm_three, hat_three, scale_three = forward_norm(
+        expanded, expand_sum, expand_sq, count_all, gain_three, owned(shifts, 2 * M, wide_dev)
+    )
+    summed_in = norm_three + flat_in.astype(jnp.float32)
+    shared = smooth(summed_in).astype(jnp.bfloat16)
+    branch_bias, proj_bias, sem_w, depth_w, normal_w, sem_b, depth_b, normal_b = unpack_small(
+        head_small
+    )
+    out_weights = (
+        sem_w.astype(jnp.bfloat16),
+        depth_w.astype(jnp.bfloat16),
+        normal_w.astype(jnp.bfloat16),
+    )
+    own_row = lambda array, axis: lax.dynamic_slice_in_dim(array, block_id, 1, axis=axis)
+    w_seg = tap_weights(head_weight, head_rates)
+    q_rows, shared_all = heads_forward(shared, w_seg)
+    proj_t = lax.all_gather(
+        jnp.transpose(head_proj.astype(jnp.bfloat16), (0, 2, 1)), "pix", axis=2, tiled=True
+    )
+    out_stack = jnp.stack(
+        [jnp.pad(weight, ((0, 0), (0, 32 - weight.shape[1]))) for weight in out_weights]
+    )
+    out_bias = jnp.stack(
+        [jnp.pad(bias, (0, 32 - bias.shape[0])) for bias in (sem_b, depth_b, normal_b)], axis=1
+    )
+    targets = jnp.concatenate([own_row(depth_target, 0), own_row(normal_target, 1)[:, 0]], axis=0)
+    pre_grad, proj_grad, out_grad, bias_rows, out_bias_rows = heads_middle(
+        q_rows,
+        branch_bias.T,
+        proj_bias.T,
+        proj_t,
+        out_stack,
+        out_bias,
+        own_row(sem_label, 0),
+        targets,
+        own_row(label_mask, 1)[:, 0].astype(jnp.float32),
+        jnp.broadcast_to(task_counts[:, None], (3, columns_per_shard)),
+    )
+    small_term = pack_small(
+        [bias_rows[:4, 0], bias_rows[4, 0]]
+        + [out_grad[0, :NCLS].T, out_grad[1, :1].T, out_grad[2, :3].T]
+        + [out_bias_rows[0, 0, :NCLS], out_bias_rows[1, 0, :1], out_bias_rows[2, 0, :3]]
+    )
+    tap_sums, combined = heads_backward(pre_grad, shared_all, w_seg)
+    head_shard, rates_shard = tap_grads(tap_sums)
+    shared_slope = combined * smooth_slope(summed_in)
+    expand_up, gain_three_grad, shift_three_grad = backward_norm(
+        shared_slope, hat_three, scale_three, count_all, gain_three
+    )
+    expand_back = expand_up.astype(jnp.bfloat16)
+    expand_grad = contract_first(second_all, expand_back)
+    second_back = channel_parts(contract_last(expand_back, expand_w))
+    middle_up, gain_two_grad, shift_two_grad = backward_norm(
+        second_back * smooth_slope(norm_two), hat_two, scale_two, count_all, gain_two
+    )
+    middle_gradient = middle_up.astype(jnp.bfloat16)
+    dilated_list = []
+    for tap_index in range(9):
+        kernel_row, kernel_column = divmod(tap_index, 3)
+        sliding_patch = bordered_input[
+            kernel_row * DILATION_RATE : kernel_row * DILATION_RATE + rows_per_shard,
+            kernel_column * DILATION_RATE : kernel_column * DILATION_RATE + columns_per_shard,
+        ].reshape(pixels, M)
+        dilated_list.append(contract_first(sliding_patch, middle_gradient))
+    dilated_grad = jnp.stack(dilated_list)
+    canvas_gradient = with_halo(
+        middle_gradient.reshape(rows_per_shard, columns_per_shard, middle_per_shard),
+        (("pix", 0),),
+        DILATION_RATE,
+    )
+    canvas_gradient = jnp.pad(canvas_gradient, ((0, 0), (DILATION_RATE, DILATION_RATE), (0, 0)))
+    first_part = jnp.zeros((pixels, M), jnp.float32)
+    for tap_index in range(9):
+        kernel_row, kernel_column = divmod(tap_index, 3)
+        sliding_patch = canvas_gradient[
+            (2 - kernel_row) * DILATION_RATE : (2 - kernel_row) * DILATION_RATE + rows_per_shard,
+            (2 - kernel_column) * DILATION_RATE : (2 - kernel_column) * DILATION_RATE
+            + columns_per_shard,
+        ].reshape(pixels, middle_per_shard)
+        first_part = first_part + contract_last(sliding_patch, dilated_w[tap_index])
+    first_back = channel_parts(first_part) * mask_flat[:, None] * smooth_slope(norm_one)
+    reduce_up, gain_one_grad, shift_one_grad = backward_norm(
+        first_back, hat_one, scale_one, count_all, gain_one
+    )
+    reduce_all = channel_gather(reduce_up.astype(jnp.bfloat16))
+    reduce_grad = contract_first(flat_in, reduce_all)
+    input_grad = contract_last(reduce_all, reduce_w) + shared_slope
+    reduce_shard, dilated_shard, expand_shard, proj_shard = (
+        lax.psum_scatter(reduce_grad, "pix", scatter_dimension=1, tiled=True),
+        lax.psum_scatter(dilated_grad, "pix", scatter_dimension=1, tiled=True),
+        lax.psum_scatter(expand_grad, "pix", scatter_dimension=0, tiled=True),
+        lax.psum_scatter(lax.psum(proj_grad, "ch"), "pix", scatter_dimension=1, tiled=True),
+    )
+    norm_local = jnp.zeros((2, 2 * M + C), jnp.float32)
+    for offset, width, gain_grad, shift_grad in (
+        (0, middle_per_shard, gain_one_grad, shift_one_grad),
+        (M, middle_per_shard, gain_two_grad, shift_two_grad),
+        (2 * M, wide_dev, gain_three_grad, shift_three_grad),
+    ):
+        norm_local = lax.dynamic_update_slice(
+            norm_local, jnp.stack([gain_grad, shift_grad]), (0, offset + block_id * width)
+        )
+    big_local = (
+        jnp.sum(reduce_shard * reduce_shard)
+        + jnp.sum(dilated_shard * dilated_shard)
+        + jnp.sum(expand_shard * expand_shard)
+        + jnp.sum(head_shard * head_shard)
+        + jnp.sum(rates_shard * rates_shard)
+        + jnp.sum(proj_shard * proj_shard) / groups
+    )
+    big_squares, norm_grad, small_grad = lax.psum(
+        (big_local, norm_local / pix_devices, small_term), ("pix", "ch")
+    )
+    grad_norm = jnp.sqrt(
+        big_squares + jnp.sum(norm_grad * norm_grad) + jnp.sum(small_grad * small_grad)
+    )
+    factor = jnp.minimum(1.0, CLIP_NORM / (grad_norm + 1e-06))
+    reduce_new, reduce_first, reduce_second = adam_step(
+        w_reduce, m_reduce, v_reduce, reduce_shard * factor, RATE_MATRIX, DECAY
+    )
+    dilated_new, dilated_first, dilated_second = adam_step(
+        w_dilated, m_dilated, v_dilated, dilated_shard * factor, RATE_MATRIX, DECAY
+    )
+    expand_new, expand_first, expand_second = adam_step(
+        w_expand, m_expand, v_expand, expand_shard * factor, RATE_MATRIX, DECAY
+    )
+    head_new, head_first, head_second = adam_step(
+        head_weight, m_head, v_head, head_shard * factor, RATE_MATRIX, DECAY
+    )
+    rates_new, rates_first, rates_second = adam_step(
+        head_rates, m_rates, v_rates, rates_shard * factor, RATE_MATRIX, DECAY
+    )
+    proj_new, proj_first, proj_second = adam_step(
+        head_proj, m_proj, v_proj, proj_shard * factor, RATE_MATRIX, DECAY
+    )
+    norm_new, norm_first, norm_second = adam_step(
+        norm_params, norm_m, norm_v, norm_grad * factor, RATE_SMALL, 0.0
+    )
+    small_new, small_first, small_second = adam_step(
+        head_small, small_m, small_v, small_grad * factor, RATE_SMALL, 0.0
+    )
+    depth_bias_grad = small_grad[small_grad.shape[0] - 4]
+    return (
+        shared.reshape(rows_per_shard, columns_per_shard, wide_dev),
+        input_grad.reshape(rows_per_shard, columns_per_shard, wide_dev),
+        grad_norm,
+        reduce_new,
+        reduce_first,
+        reduce_second,
+        reduce_new.astype(jnp.bfloat16),
+        dilated_new,
+        dilated_first,
+        dilated_second,
+        dilated_new.astype(jnp.bfloat16),
+        expand_new,
+        expand_first,
+        expand_second,
+        expand_new.astype(jnp.bfloat16),
+        head_new,
+        head_first,
+        head_second,
+        head_new.astype(jnp.bfloat16),
+        rates_new,
+        rates_first,
+        rates_second,
+        rates_new.astype(jnp.bfloat16),
+        proj_new,
+        proj_first,
+        proj_second,
+        proj_new.astype(jnp.bfloat16),
+        norm_new,
+        norm_first,
+        norm_second,
+        small_new,
+        small_first,
+        small_second,
+        depth_bias_grad,
+    )
+
+
+def per_device(features, *rest):
+    sizes = (lax.axis_size("pix"), lax.axis_size("ch"))
+    if sizes == (NPIX, NCH) and features.shape == (ROWS, WIDTH, CIN):
+        return per_device_rows(features, *rest)
+    return per_device_plain(features, *rest)
+
+
 def solution(mesh):
     placed = (
         P("pix", None, "ch"),

time: 2230 us -> 1020 us (0.46)
  waiting for transfers between devices: 1270 us -> 308 us
  Pallas kernels: 0 us -> 286 us
  matrix products: 246 us -> 31.6 us
  blocking collectives: 392 us -> 252 us
  local copies, waits for them, and re-layouts: 123 us -> 44 us
  starting transfers between devices: 62.8 us -> 13.3 us
  other arithmetic: 91.4 us -> 54.7 us
    reduce_scatter x7 -> x5, waiting for transfers between devices: 927 us -> 218 us  [the longest x1 71.2 us: per_device_rows(): lax.psum_scatter(dilated_grad, 'pix', scatter_dimension=1, tiled=True)]
    pallas_call x0 -> x3, Pallas kernels: none -> 286 us  [the longest x1 184 us: heads_backward(): pl.pallas_call(heads_backward_kernel, out_shape=(jax.ShapeDtypeStruct((SE...]
    all_gather x3 -> x2, waiting for transfers between devices: 188 us -> 0.05 us  [the longest x1 0.03 us: per_device_rows(): lax.all_gather(w_dilated.astype(jnp.bfloat16), 'pix', axis=1, tiled=True)]
    dot_general x46 -> x11, matrix products: 107 us -> 7.8 us  [the longest x9 4.83 us: per_device_rows(): jnp.dot(sliding_patch, dilated_w[tap_index], preferred_element_type=jnp.f...]
    all_gather x3 -> x2, blocking collectives: 146 us -> 66.7 us  [the longest x1 33.7 us: per_device_rows(): lax.all_gather(w_expand.astype(jnp.bfloat16), 'pix', axis=0, tiled=True)]
    psum x1, waiting for transfers between devices: 99.6 us -> 32.5 us  [per_device_rows(): lax.psum(proj_grad, 'ch')]
    dot_general x42 -> x11, matrix products: 72.2 us -> 14.4 us  [contract_first(): lax.dot_general(left, right, (((0,), (0,)), ((), ())), preferred_element_...]
    dot_general x43 -> x11, matrix products: 67 us -> 9.42 us  [contract_last(): lax.dot_general(left, right, (((1,), (1,)), ((), ())), preferred_element_...]
  transfers between devices with their start and end apart: 25 -> 14, of which waited for: 12 -> 11; matrix products, arithmetic and copies ran while one was open for 13% -> 8% of each run, Pallas kernels for 0% -> 9%
where the time goes in v1:
time: 1020 us; the launch traced here: 1010 us
  waiting for transfers between devices  308 us (30%)
  Pallas kernels  286 us (28%)
  blocking collectives  252 us (25%)
  other arithmetic  54.7 us (5%)
  local copies, waits for them, and re-layouts  44 us (4%)
  matrix products  31.6 us (3%)
  between operations  24.4 us (2%)
  starting transfers between devices  13.3 us (1%)
    pallas_call x1, Pallas kernels, heads_backward(): pl.pallas_call(heads_backward_kernel, out_shape=(jax.ShapeDtypeStruct((SE...  184 us
    pallas_call x1, Pallas kernels, heads_forward(): pl.pallas_call(heads_forward_kernel, out_shape=(jax.ShapeDtypeStruct((4,...  95.5 us
    reduce_scatter x1, waiting for transfers between devices, per_device_rows(): lax.psum_scatter(dilated_grad, 'pix', scatter_dimension=1, tiled=True)  71.2 us
    psum x3, blocking collectives, back_pair(): return lax.psum((first, second), 'pix')  65 us
    reduce_scatter x1, waiting for transfers between devices, per_device_rows(): lax.psum_scatter(reduce_grad, 'pix', scatter_dimension=1, tiled=True)  64.7 us
    reduce_scatter x1, waiting for transfers between devices, per_device_rows(): lax.psum_scatter(expand_grad, 'pix', scatter_dimension=0, tiled=True)  43.8 us
    reduce_scatter x2, waiting for transfers between devices, channel_parts(): return lax.psum_scatter(partial_sum, 'ch', scatter_dimension=1, tiled=True)  41.1 us
    psum x1, blocking collectives, per_device_rows(): lax.psum((big_local, norm_local / pix_devices, small_term), ('pix', 'ch'))  40.5 us
  transfers between devices with their start and end apart: 14, of which 11 were waited for; matrix products, arithmetic and copies ran while one was open for 8% of the time, Pallas kernels for 9%

profile of v1, /device:TPU:0, one launch (start us, length us, event | category | flops | bytes accessed | tf_op | source)
XLA Modules:
  0.0 1014.4 jit_solution(9216340109361709366)
XLA Ops:
  9.1 33.0 %all_gather.21 = bf16[512,512]{0,1:T(8,128)(2,1)S(1)} all-gather(bf16[512,64]{0,1:T(8,128)(2,1)S(1)} %convert_element_type.103), channel_id=1, replica_groups=mesh['pix'=8,'ch'=4] {'pix'}, dimensions={1}, use_global_device_ids=true | all-gather | bytes 589824 | tf_op jit(solution)/shard_map/all_gather | solution.py:1339
  49.1 33.7 %all_gather.25 = bf16[512,512]{1,0:T(8,128)(2,1)} all-gather(bf16[64,512]{1,0:T(8,128)(2,1)S(1)} %convert_element_type.109), channel_id=1, replica_groups=mesh['pix'=8,'ch'=4] {'pix'}, dimensions={0}, use_global_device_ids=true | all-gather | bytes 589824 | tf_op jit(solution)/shard_map/all_gather | solution.py:1341
  99.9 22.4 %all-reduce.14 = (f32[128]{0:T(128)S(1)}, f32[128]{0:T(128)S(1)}) all-reduce(f32[128]{0:T(128)S(1)} %get-tuple-element.63, f32[128]{0:T(128)S(1)} %get-tuple-element.62), channel_id=1, replica_groups=mesh['pix'=8,'ch'=4] {'pix'}, use_global_device_ids=true, to_apply=%region_4.0 | all-reduce | flops 256 | bytes 2048 | tf_op jit(solution)/shard_map/psum | solution.py:1352
  124.6 7.1 all_gather.22
  147.8 10.3 %collective-permute-done = bf16[4,128,512]{2,1,0:T(8,128)(2,1)} collective-permute-done((bf16[4,128,512]{2,1,0:T(8,128)(2,1)S(1)}, bf16[4,128,512]{2,1,0:T(8,128)(2,1)}, u32[]{:S(2)}, u32[]{:S(2)}) %collective-permute-start) | collective-permute-done | bytes 524320 | tf_op jit(solution)/shard_map/ppermute | solution.py:41
  164.6 19.8 %all-reduce.13 = (f32[128]{0:T(128)S(1)}, f32[128]{0:T(128)S(1)}) all-reduce(f32[128]{0:T(128)S(1)} %get-tuple-element.61, f32[128]{0:T(128)S(1)} %get-tuple-element.60), channel_id=1, replica_groups=mesh['pix'=8,'ch'=4] {'pix'}, use_global_device_ids=true, to_apply=%region_8.9 | all-reduce | flops 256 | bytes 2048 | tf_op jit(solution)/shard_map/psum | solution.py:173
  186.1 6.8 all_gather.24
  194.2 17.5 %all-reduce.12 = (f32[512]{0:T(512)S(1)}, f32[512]{0:T(512)S(1)}, f32[3]{0:T(128)S(1)}) all-reduce(f32[512]{0:T(512)S(1)} %get-tuple-element.55, f32[512]{0:T(512)S(1)} %get-tuple-element.54, f32[3]{0:T(128)S(1)} %copy-done.76), channel_id=1, replica_groups=mesh['pix'=8,'ch'=4] {'pix'}, use_global_device_ids=true, to_apply=%region_12.13 | all-reduce | flops 1027 | bytes 8216 | tf_op jit(solution)/shard_map/psum | solution.py:173
  213.1 95.5 %heads_forward.1 = (bf16[4,768,128]{2,1,0:T(8,128)(2,1)}, bf16[8,512,512]{2,1,0:T(8,128)(2,1)}) custom-call(bf16[512,512]{1,0:T(8,128)(2,1)} %multiply_convert_fusion.1.x_ref, bf16[3,704,512]{2,1,0:T(8,128)(2,1)} %bitcast.257), custom_call_target="tpu_custom_call" | custom-call | tf_op jit(solution)/shard_map/heads_forward/pallas_call | solution.py:845
  309.3 7.1 heads_middle.1
  316.4 183.7 %heads_backward.1 = (f32[3,704,512]{2,1,0:T(8,128)}, f32[512,512]{1,0:T(8,128)}) custom-call(bf16[4,768,128]{2,1,0:T(8,128)(2,1)} %get-tuple-element.44.dq_ref, bf16[8,512,512]{2,1,0:T(8,128)(2,1)} %get-tuple-element.45.xall_ref, bf16[3,704,512]{2,1,0:T(8,128)(2,1)} %bitcast.258), custom_call_target="tpu_custom_call" | custom-call | tf_op jit(solution)/shard_map/heads_backward/pallas_call | solution.py:1232
  502.3 21.6 %all-reduce.11 = (f32[512]{0:T(512)S(1)}, f32[512]{0:T(512)S(1)}) all-reduce(f32[512]{0:T(512)S(1)} %get-tuple-element.53, f32[512]{0:T(512)S(1)} %get-tuple-element.52), channel_id=1, replica_groups=mesh['pix'=8,'ch'=4] {'pix'}, use_global_device_ids=true, to_apply=%region_18.19 | all-reduce | flops 1024 | bytes 8192 | tf_op jit(solution)/shard_map/psum | solution.py:177
  526.6 21.4 %reduce-scatter.10.cloned.1.call-done = f32[512,128]{1,0:T(8,128)} async-done(((f32[512,512]{1,0:T(8,128)}), f32[512,128]{1,0:T(8,128)}) %reduce-scatter.10.cloned.1.call-update) | async-done | bytes 262160 | tf_op jit(solution)/shard_map/reduce_scatter | solution.py:185
  549.2 21.3 %all-reduce.10 = (f32[128]{0:T(128)S(1)}, f32[128]{0:T(128)S(1)}) all-reduce(f32[128]{0:T(128)S(1)} %get-tuple-element.59, f32[128]{0:T(128)S(1)} %get-tuple-element.58), channel_id=1, replica_groups=mesh['pix'=8,'ch'=4] {'pix'}, use_global_device_ids=true, to_apply=%region_23.24 | all-reduce | flops 256 | bytes 2048 | tf_op jit(solution)/shard_map/psum | solution.py:177
  589.1 19.7 %reduce-scatter.12.cloned.1.call-done = f32[512,128]{1,0:T(8,128)} async-done(((f32[512,512]{1,0:T(8,128)}), f32[512,128]{1,0:T(8,128)}) %reduce-scatter.12.cloned.1.call-update) | async-done | bytes 262160 | tf_op jit(solution)/shard_map/reduce_scatter | solution.py:185
  610.0 22.0 %all-reduce.9 = (f32[128]{0:T(128)S(1)}, f32[128]{0:T(128)S(1)}) all-reduce(f32[128]{0:T(128)S(1)} %get-tuple-element.57, f32[128]{0:T(128)S(1)} %get-tuple-element.56), channel_id=1, replica_groups=mesh['pix'=8,'ch'=4] {'pix'}, use_global_device_ids=true, to_apply=%region_28.29 | all-reduce | flops 256 | bytes 2048 | tf_op jit(solution)/shard_map/psum | solution.py:177
  632.1 6.5 all_gather.27
  650.4 37.9 %reduce-scatter.20.cloned.1.call-done = f32[3,128,256]{2,1,0:T(8,128)} async-done(((f32[3,1024,256]{2,1,0:T(8,128)}), f32[3,128,256]{2,1,0:T(8,128)}) %reduce-scatter.20.cloned.1.call-update) | async-done | bytes 393232 | tf_op jit(solution)/shard_map/reduce_scatter | solution.py:1476
  711.7 43.8 %reduce-scatter.18.cloned.1.call-done = f32[64,512]{1,0:T(8,128)} async-done(((f32[512,512]{1,0:T(8,128)}), f32[64,512]{1,0:T(8,128)}) %reduce-scatter.18.cloned.1.call-update) | async-done | bytes 131088 | tf_op jit(solution)/shard_map/reduce_scatter | solution.py:1475
  757.2 64.7 %reduce-scatter.14.cloned.1.call-done = f32[512,64]{0,1:T(8,128)} async-done(((f32[512,512]{0,1:T(8,128)}), f32[512,64]{0,1:T(8,128)}) %reduce-scatter.14.cloned.1.call-update) | async-done | bytes 131088 | tf_op jit(solution)/shard_map/reduce_scatter | solution.py:1473
  823.4 32.5 %all-reduce.17.cloned.1.call-done = f32[3,128,256]{2,1,0:T(8,128)} async-done(((f32[3,128,256]{2,1,0:T(8,128)}), f32[3,128,256]{2,1,0:T(8,128)}) %all-reduce.17.cloned.1.call-update) | async-done | bytes 393232 | tf_op jit(solution)/shard_map/psum | solution.py:1476
  858.3 71.2 %reduce-scatter.16.cloned.1.call-done = f32[9,64,128]{2,1,0:T(8,128)} async-done(((f32[9,512,128]{2,1,0:T(8,128)}), f32[9,64,128]{2,1,0:T(8,128)}) %reduce-scatter.16.cloned.1.call-update) | async-done | bytes 294928 | tf_op jit(solution)/shard_map/reduce_scatter | solution.py:1474
  937.0 40.5 %all-reduce.8 = (f32[]{:T(128)}, f32[2,3072]{1,0:T(2,128)S(1)}, f32[9751]{0:T(1024)S(1)}) all-reduce(f32[]{:T(128)S(6)} %add.413, f32[2,3072]{1,0:T(2,128)S(1)} %broadcast_multiply_fusion.1, f32[9751]{0:T(1024)S(1)} %concatenate.44), channel_id=1, replica_groups=mesh['pix'=8,'ch'=4] {'pix','ch'}, use_global_device_ids=true, to_apply=%region_40.41 | all-reduce | flops 15896 | bytes 127168 | tf_op jit(solution)/shard_map/psum | solution.py:1495
  988.6 10.3 %fusion.84 = (bf16[3,9,96,512]{3,2,1,0:T(8,128)(2,1)}, f32[3,9,96,512]{3,2,1,0:T(8,128)}, f32[3,9,96,512]{3,2,1,0:T(8,128)}, f32[3,9,96,512]{3,2,1,0:T(8,128)}) fusion(f32[3,9,96,512]{3,2,1,0:T(8,128)S(1)} %bitcast.249, f32[3,9,96,512]{3,2,1,0:T(8,128)S(1)} %bitcast.265, f32[3,9,96,512]{3,2,1,0:T(8,128)} %param.50, f32[3,9,96,512]{3,2,1,0:T(8,128)S(1)} %bitcast.250), kind=kLoop, calls=%fused_computation.235 | loop fusion | flops 21233664 | bytes 39813120 | tf_op jit(solution)/shard_map/convert_element_type | solution.py:1550
  (366 shorter events, 139.3 us)
Async XLA Ops:
  8.0 81.7 %copy-start = (f32[3,4,128]{2,1,0:T(4,128)S(1)}, f32[3,4,128]{2,1,0:T(4,128)}, u32[]{:S(2)}) copy-start(f32[3,4,128]{2,1,0:T(4,128)} %param.34) | copy-start | bytes 18436
  8.1 90.8 %reduce-scatter.8.cloned.1.call-start = ((), (), s32[]{:S(2)}) async-start(), calls=%async_computation.7 | async-start | bytes 1310720 | tf_op jit(solution)/shard_map/reduce_scatter | solution.py:1343
  45.4 98.3 %all-gather.3.cloned.1.call-start = ((), (), s32[]{:S(2)}) async-start(), calls=%async_computation.8 | async-start | bytes 1327104 | tf_op jit(solution)/shard_map/all_gather | solution.py:1340
  46.2 262.4 %all-gather.5.cloned.1.call-start = ((), (), s32[]{:S(2)}) async-start(), calls=%async_computation.9 | async-start | bytes 1769472 | tf_op jit(solution)/shard_map/all_gather | solution.py:1401
  47.1 500.9 %reduce-scatter.10.cloned.1.call-start = ((), (), s32[]{:S(2)}) async-start(), calls=%async_computation.10 | async-start | bytes 1310720 | tf_op jit(solution)/shard_map/reduce_scatter | solution.py:185
  131.8 16.1 %collective-permute-start.1 = (bf16[4,128,512]{2,1,0:T(8,128)(2,1)S(1)}, bf16[4,128,512]{2,1,0:T(8,128)(2,1)S(1)}, u32[]{:S(2)}, u32[]{:S(2)}) collective-permute-start(bf16[4,128,512]{2,1,0:T(8,128)(2,1)S(1)} %bitcast.259), channel_id=1, source_target_pairs={{4,0},{8,4},{12,8},{16,12},{20,16},{24,20},{28,24},{5,1},{9,5},{13... | collective-permute-start | bytes 1572872 | tf_op jit(solution)/shard_map/ppermute | solution.py:43
  133.0 25.1 %collective-permute-start = (bf16[4,128,512]{2,1,0:T(8,128)(2,1)S(1)}, bf16[4,128,512]{2,1,0:T(8,128)(2,1)}, u32[]{:S(2)}, u32[]{:S(2)}) collective-permute-start(bf16[4,128,512]{2,1,0:T(8,128)(2,1)S(1)} %bitcast.260), channel_id=1, source_target_pairs={{0,4},{4,8},{8,12},{12,16},{16,20},{20,24},{24,28},{1,5},{5,9},{9,... | collective-permute-start | bytes 1572872 | tf_op jit(solution)/shard_map/ppermute | solution.py:41
  164.6 47.2 %copy-start.4 = (bf16[4,128,512]{2,1,0:T(8,128)(2,1)S(1)}, bf16[4,128,512]{2,1,0:T(8,128)(2,1)}, u32[]{:S(2)}) copy-start(bf16[4,128,512]{2,1,0:T(8,128)(2,1)} %param.30) | copy-start | bytes 1572868
  525.1 46.0 %copy-start.63 = (f32[128]{0:T(128)S(1)}, f32[128]{0:T(128)}, u32[]{:S(2)}) copy-start(f32[128]{0:T(128)} %copy-done.61) | copy-start | bytes 1540
  525.1 46.0 %copy-start.66 = (f32[128]{0:T(128)S(1)}, f32[128]{0:T(128)}, u32[]{:S(2)}) copy-start(f32[128]{0:T(128)} %copy-done.64) | copy-start | bytes 1540
  525.1 46.0 %copy-start.78 = (f32[128]{0:T(128)S(1)}, f32[128]{0:T(128)}, u32[]{:S(2)}) copy-start(f32[128]{0:T(128)} %get-tuple-element.113) | copy-start | bytes 1540
  526.6 82.2 %reduce-scatter.12.cloned.1.call-start = ((), (), s32[]{:S(2)}) async-start(), calls=%async_computation.11 | async-start | bytes 1310720 | tf_op jit(solution)/shard_map/reduce_scatter | solution.py:185
  571.2 7.0 collective-permute-start.3
  572.6 7.1 collective-permute-start.2
  585.5 102.9 %reduce-scatter.20.cloned.1.call-start = ((), (), s32[]{:S(2)}) async-start(), calls=%async_computation.15 | async-start | bytes 3538944 | tf_op jit(solution)/shard_map/reduce_scatter | solution.py:1476
  586.1 45.9 %copy-start.77 = (f32[128]{0:T(128)S(1)}, f32[128]{0:T(128)}, u32[]{:S(2)}) copy-start(f32[128]{0:T(128)} %get-tuple-element.110) | copy-start | bytes 1540
  586.1 169.4 %reduce-scatter.18.cloned.1.call-start = ((), (), s32[]{:S(2)}) async-start(), calls=%async_computation.14 | async-start | bytes 1179648 | tf_op jit(solution)/shard_map/reduce_scatter | solution.py:1475
  589.0 232.9 %reduce-scatter.14.cloned.1.call-start = ((), (), s32[]{:S(2)}) async-start(), calls=%async_computation.12 | async-start | bytes 1179648 | tf_op jit(solution)/shard_map/reduce_scatter | solution.py:1473
  640.9 215.1 %all-reduce.17.cloned.1.call-start = ((), (), s32[]{:S(2)}) async-start(), calls=%async_computation.16 | async-start | bytes 786432 | tf_op jit(solution)/shard_map/psum | solution.py:1476
  688.4 241.1 %reduce-scatter.16.cloned.1.call-start = ((), (), s32[]{:S(2)}) async-start(), calls=%async_computation.13 | async-start | bytes 2654208 | tf_op jit(solution)/shard_map/reduce_scatter | solution.py:1474
  709.7 47.4 %copy-start.80 = (f32[128]{0:T(128)S(1)}, f32[128]{0:T(128)}, u32[]{:S(2)}) copy-start(f32[128]{0:T(128)} %copy-done.79) | copy-start | bytes 1540
  709.7 47.4 %copy-start.82 = (f32[128]{0:T(128)S(1)}, f32[128]{0:T(128)}, u32[]{:S(2)}) copy-start(f32[128]{0:T(128)} %copy-done.81) | copy-start | bytes 1540
  709.7 224.7 %copy-start.22 = (bf16[512,512]{1,0:T(8,128)(2,1)S(1)}, bf16[512,512]{1,0:T(8,128)(2,1)}, u32[]{:S(2)}) copy-start(bf16[512,512]{1,0:T(8,128)(2,1)} %copy-done.21) | copy-start | bytes 1572868
  934.4 54.1 %slice-start.2 = ((s8[5308416]{0:T(1024)(128)(4,1)}), s8[1114112]{0:T(1024)(128)(4,1)S(1)}, s32[]{:S(2)}) async-start(s8[5308416]{0:T(1024)(128)(4,1)} %bitcast.264), calls=%async_computation.19 | async-start | bytes 2228224
  (80 other events, 968.4 us)
Sparse Core Ops, SparseCore 0:
  45.6 26.0 reduce-scatter.7
  526.7 21.3 reduce-scatter.9
  585.6 23.0 reduce-scatter.11
  613.2 75.1 reduce-scatter.19
  692.6 62.8 reduce-scatter.17
  759.3 62.4 reduce-scatter.13
  824.3 31.5 all-reduce.16
  860.0 69.4 reduce-scatter.15
Sparse Core Ops, SparseCore 1:
  48.9 43.5 all-gather.2
  95.1 46.2 all-gather.4

commit v2 on v1

--- a/solution.py
+++ b/solution.py
@@ -940,12 +940,22 @@
     )(q, bias, pbias, wpt, wot, obias, label, target, mask, count)
 
 
+def fold(values):
+    rows, lanes = values.shape
+    total = values[0:8, 0:128]
+    for r in range(rows // 8):
+        for l in range(lanes // 128):
+            if r or l:
+                total = total + values[8 * r : 8 * r + 8, 128 * l : 128 * l + 128]
+    return total
+
+
 def low_task(zplane):
     return (2 * zplane * COLS) // HID
 
 
 def heads_backward_kernel(
-    dq_ref, xall_ref, w_ref, dw_ref, gz_ref,
+    dq_ref, xall_ref, w_ref, dw_ref, gz_ref, square_ref,
     dq_all, wt, dcol, parts, y_in, z_buf, z_in, gram_own, gram_ch, gram_px, gsum,
     local_sem, row_send, row_recv, x_send, x_recv, ca_send, ca_recv, cb_send, cb_recv,
     y_send, y_recv, z_send, z_recv, gc_send, gc_recv, gp_send, gp_recv,
@@ -1083,6 +1093,14 @@
 
     lax.fori_loop(0, NPIX, block_step, 0)
 
+    square_ref[...] = jnp.zeros_like(square_ref)
+
+    def square_rows(m, carry):
+        s = m // TAPS
+        part = dw_ref[s, pl.ds(pl.multiple_of(lax.rem(m, TAPS) * 32, 32), 32), :]
+        square_ref[...] += fold(part * part)
+        return carry
+
     def z_copy(d, slot):
         zz = lax.rem(z + d, zcount)
         return remote(
@@ -1114,6 +1132,7 @@
                 def _():
                     z_copy(d, slot).start()
 
+    lax.fori_loop(0, SEGS * TAPS, square_rows, 0)
     for slot in range(2):
         z_in[z, slot] = z_buf[z, slot]
     for d in range(1, zcount):
@@ -1141,14 +1160,6 @@
             product = grads[a] * grads[b]
             gram_own[i] += fold(product)
         return carry
-
-    def fold(product):
-        total = product[0:8, 0:128]
-        for r in range(4):
-            for l in range(4):
-                if r or l:
-                    total = total + product[8 * r : 8 * r + 8, 128 * l : 128 * l + 128]
-        return total
 
     lax.fori_loop(0, CIN // 32, gram_rows, 0)
 
@@ -1234,9 +1245,10 @@
         out_shape=(
             jax.ShapeDtypeStruct((SEGS, SEG_ROWS, CIN), F32),
             jax.ShapeDtypeStruct((PX, CIN), F32),
+            jax.ShapeDtypeStruct((8, 128), F32),
         ),
         in_specs=[whole_vmem()] * 3,
-        out_specs=[whole_vmem()] * 2,
+        out_specs=[whole_vmem()] * 3,
         scratch_shapes=[
             pltpu.VMEM((NPIX, NCH, 4, COLS, WIDTH), BF),
             pltpu.VMEM((SEGS, CIN, SEG_ROWS), BF),
@@ -1286,6 +1298,642 @@
             else:
                 rates.append(jnp.zeros((3, COLS, CIN), F32))
     return head, jnp.stack(rates).reshape(3, 9, COLS, CIN)
+
+
+MID = M // NCH
+WPART = M // NPIX
+TAP_LANES = 9 * MID
+W_REDUCE = slice(0, CIN)
+W_DILATED = slice(CIN, CIN + TAP_LANES)
+W_EXPAND = slice(CIN + TAP_LANES, 2 * CIN + TAP_LANES)
+W_LANES = 2 * CIN + TAP_LANES
+SMALL_ROWS = 80
+
+
+def slide_rows(tile, steps):
+    if steps == 0:
+        return tile
+    line = lax.broadcasted_iota(jnp.int32, (WIDTH, tile.shape[1]), 0)
+    keep = line >= steps if steps > 0 else line < WIDTH + steps
+    pieces = []
+    for r in range(ROWS):
+        rolled = pltpu.roll(tile[r * WIDTH : (r + 1) * WIDTH], steps % WIDTH, 0)
+        pieces.append(jnp.where(keep, rolled, 0.0))
+    return jnp.concatenate(pieces, axis=0)
+
+
+def column_sums(values):
+    return jnp.sum(values, axis=0, keepdims=True)
+
+
+def pix_copies(inbox, send_sem, recv_sem):
+    p, c = lax.axis_index("pix"), lax.axis_index("ch")
+    return [
+        remote(inbox.at[p], inbox.at[p], send_sem.at[d - 1], recv_sem.at[d - 1], (lax.rem(p + d, NPIX), c))
+        for d in range(1, NPIX)
+    ]
+
+
+def ch_copies(source, inbox, send_sem, recv_sem):
+    p, c = lax.axis_index("pix"), lax.axis_index("ch")
+    copies = []
+    for d in range(1, NCH):
+        other = lax.rem(c + d, NCH)
+        copies.append(remote(source(other), inbox.at[c], send_sem.at[d - 1], recv_sem.at[d - 1], (p, other)))
+    return copies
+
+
+def start_all(copies):
+    for copy in copies:
+        copy.start()
+
+
+def wait_all(copies):
+    for copy in copies:
+        copy.wait()
+
+
+def add_up(inbox):
+    total = inbox[0]
+    for i in range(1, inbox.shape[0]):
+        total = total + inbox[i]
+    return total
+
+
+def block_forward_kernel(
+    x_ref, mask_ref, w_ref, proj_ref, narrow_ref, wide_ref,
+    out_ref, hat_one_ref, hat_two_ref, hat_three_ref, wall_ref, first_ref, second_ref, stats_ref, stats_wide_ref, wpt_ref,
+    work, ch_buf, ch_in, halo_buf, halo_in, stat_one, stat_two, stat_three,
+    local_sem, wz_send, wz_recv, wy_send, wy_recv, c_send, c_recv, s_send, s_recv, h_send, h_recv,
+):
+    p, c, z, y, x, core = place()
+    zcount = NPIX // 2
+    other_y = (2 * z + 1 - y, c)
+    pix_targets = [(lax.rem(p + d, NPIX), c) for d in range(1, NPIX)]
+    ch_targets = [(p, lax.rem(c + d, NCH)) for d in range(1, NCH)]
+    greet(pix_targets + ch_targets)
+    parts = (pl.ds(0, CIN), pl.ds(CIN, TAP_LANES), pl.ds(CIN + TAP_LANES, CIN))
+
+    def shard(part):
+        return w_ref.at[:, parts[part]] if part < 3 else proj_ref
+
+    def spot(part, source):
+        if part < 3:
+            return wall_ref.at[source, :, parts[part]]
+        return wpt_ref.at[:, :, pl.ds(pl.multiple_of(source * 128, 128), 128)]
+
+    def wz_copy(part, d):
+        target = (2 * lax.rem(z + d, zcount) + y, c)
+        return remote(
+            shard(part), spot(part, p),
+            wz_send.at[part, d - 1], wz_recv.at[part, d - 1], target,
+        )
+
+    def wy_copy(part, d):
+        source = 2 * lax.rem(z + zcount - d, zcount) + y
+        src = shard(part) if d == 0 else spot(part, source)
+        return remote(
+            src, spot(part, source), wy_send.at[part, d], wy_recv.at[part, d], other_y
+        )
+
+    for part in range(4):
+        wy_copy(part, 0).start()
+        for d in range(1, zcount):
+            wz_copy(part, d).start()
+    own = pltpu.make_async_copy(w_ref, wall_ref.at[p], local_sem.at[0])
+    own.start()
+    own_proj = pltpu.make_async_copy(proj_ref, spot(3, p), local_sem.at[1])
+    own_proj.start()
+    own.wait()
+    own_proj.wait()
+
+    def forward_part(part):
+        for d in range(1, zcount):
+            wz_copy(part, d).wait_recv()
+            wy_copy(part, d).start()
+
+    def receive_part(part):
+        for d in range(zcount):
+            wy_copy(part, d).wait_recv()
+
+    def weights(lanes):
+        return wall_ref[:, :, lanes].reshape(M, lanes.stop - lanes.start)
+
+    def stat_round(index, inbox, values):
+        if index > 0:
+            inbox[p] = jnp.zeros_like(inbox[p])
+        inbox[p, 0:1, :] = column_sums(values)
+        inbox[p, 1:2, :] = column_sums(values * values)
+        copies = pix_copies(inbox, s_send.at[index], s_recv.at[index])
+        start_all(copies)
+        wait_all(copies)
+        return add_up(inbox)
+
+    count_all = float(NPIX * PX)
+
+    def norm_of(values, sums, gain, shift):
+        mean = sums[0:1] / count_all
+        scale = lax.rsqrt(sums[1:2] / count_all - mean * mean + EPS_NORM)
+        hat = (values - mean) * scale
+        return hat, hat * gain + shift, scale
+
+    forward_part(0)
+    receive_part(0)
+    for m in range(NCH):
+        wanted = wall_ref[2 * m : 2 * m + 2, :, W_REDUCE].reshape(MID, CIN)
+        value = nt_dot(x_ref[...], wanted)
+        ch_buf[0, m] = value.astype(BF)
+
+        @pl.when(m == c)
+        def _():
+            work[...] = value
+
+    reduce_copies = ch_copies(lambda other: ch_buf.at[0, other], ch_in, c_send.at[0], c_recv.at[0])
+    start_all(reduce_copies)
+    wait_all(reduce_copies)
+    reduced = work[...]
+    for d in range(1, NCH):
+        reduced = reduced + ch_in[lax.rem(c + d, NCH)].astype(F32)
+    stat_one[p] = jnp.zeros((8, MID), F32)
+    stat_one[p, 2:3, :] = narrow_ref[4:5, :]
+    sums = stat_round(0, stat_one, reduced)
+    hat, normed, scale = norm_of(reduced, sums, narrow_ref[0:1, :], narrow_ref[1:2, :])
+    hat_one_ref[...] = hat
+    stats_ref[...] = jnp.zeros_like(stats_ref)
+    stats_ref[0:1, :] = scale
+    stats_ref[2:3, :] = jnp.maximum(sums[2:3], 1.0)
+
+    def own_lanes():
+        return pl.ds(pl.multiple_of(c * MID, MID), MID)
+
+    def gather_copies(ref, index):
+        copies = []
+        for d in range(1, NCH):
+            copies.append(
+                remote(
+                    ref.at[:, own_lanes()], ref.at[:, own_lanes()],
+                    c_send.at[index, d - 1], c_recv.at[index, d - 1], ch_targets[d - 1],
+                )
+            )
+        return copies
+
+    first_ref[:, own_lanes()] = (gelu_of(normed) * mask_ref[...]).astype(BF)
+    copies = gather_copies(first_ref, 1)
+    start_all(copies)
+    forward_part(1)
+    wait_all(copies)
+    receive_part(1)
+
+    def row_part(step):
+        total = jnp.zeros((PX, MID), F32)
+        for col in range(3):
+            tap = 3 * (step + 1) + col
+            lanes = slice(CIN + tap * MID, CIN + (tap + 1) * MID)
+            total = total + slide_rows(nn_dot(first_ref[...], weights(lanes)), -DILATION_RATE * (col - 1))
+        return total
+
+    def halo_copy(side):
+        target = (p - 1, c) if side == 0 else (p + 1, c)
+        return remote(halo_buf.at[side], halo_in.at[side], h_send.at[side], h_recv.at[side], target)
+
+    halo_buf[0] = row_part(1).astype(BF)
+
+    @pl.when(p > 0)
+    def _():
+        halo_copy(0).start()
+
+    halo_buf[1] = row_part(-1).astype(BF)
+
+    @pl.when(p < NPIX - 1)
+    def _():
+        halo_copy(1).start()
+
+    work[...] = row_part(0)
+
+    @pl.when(p < NPIX - 1)
+    def _():
+        halo_copy(0).wait_recv()
+        work[...] += halo_in[0].astype(F32)
+
+    @pl.when(p > 0)
+    def _():
+        halo_copy(1).wait_recv()
+        work[...] += halo_in[1].astype(F32)
+
+    forward_part(2)
+    middle = work[...]
+    sums = stat_round(1, stat_two, middle)
+    hat, normed, scale = norm_of(middle, sums, narrow_ref[2:3, :], narrow_ref[3:4, :])
+    hat_two_ref[...] = hat
+    stats_ref[1:2, :] = scale
+    second_ref[:, own_lanes()] = gelu_of(normed).astype(BF)
+    copies = gather_copies(second_ref, 2)
+    start_all(copies)
+    wait_all(copies)
+
+    receive_part(2)
+    hat_three_ref[...] = nn_dot(second_ref[...], weights(W_EXPAND))
+    expanded = hat_three_ref[...]
+    forward_part(3)
+    sums = stat_round(2, stat_three, expanded)
+    hat, normed, scale = norm_of(expanded, sums, wide_ref[0:1, :], wide_ref[1:2, :])
+    hat_three_ref[...] = hat
+    stats_wide_ref[...] = jnp.broadcast_to(scale, stats_wide_ref.shape)
+    out_ref[...] = gelu_of(normed + x_ref[...].astype(F32)).astype(BF)
+    receive_part(3)
+
+    for part in range(4):
+        for d in range(zcount):
+            wy_copy(part, d).wait_send()
+        for d in range(1, zcount):
+            wz_copy(part, d).wait_send()
+
+    @pl.when(p > 0)
+    def _():
+        halo_copy(0).wait_send()
+
+    @pl.when(p < NPIX - 1)
+    def _():
+        halo_copy(1).wait_send()
+
+
+def block_forward(flat_in, mask, w_shard, proj_shard, narrow, wide):
+    dma = pltpu.SemaphoreType.DMA
+    zc = NPIX // 2
+    shape = jax.ShapeDtypeStruct
+    return pl.pallas_call(
+        block_forward_kernel,
+        out_shape=(
+            shape((PX, CIN), BF),
+            shape((PX, MID), F32),
+            shape((PX, MID), F32),
+            shape((PX, CIN), F32),
+            shape((NPIX, WPART, W_LANES), BF),
+            shape((PX, M), BF),
+            shape((PX, M), BF),
+            shape((8, MID), F32),
+            shape((8, CIN), F32),
+            shape((3, HID, 4 * HID), BF),
+        ),
+        in_specs=[whole_vmem()] * 6,
+        out_specs=[whole_vmem()] * 10,
+        scratch_shapes=[
+            pltpu.VMEM((PX, MID), F32),
+            pltpu.VMEM((1, NCH, PX, MID), BF),
+            pltpu.VMEM((NCH, PX, MID), BF),
+            pltpu.VMEM((2, PX, MID), BF),
+            pltpu.VMEM((2, PX, MID), BF),
+            pltpu.VMEM((NPIX, 8, MID), F32),
+            pltpu.VMEM((NPIX, 8, MID), F32),
+            pltpu.VMEM((NPIX, 8, CIN), F32),
+            dma((2,)),
+            dma((4, zc - 1)), dma((4, zc - 1)), dma((4, zc)), dma((4, zc)),
+            dma((3, NCH - 1)), dma((3, NCH - 1)),
+            dma((3, NPIX - 1)), dma((3, NPIX - 1)),
+            dma((2,)), dma((2,)),
+        ],
+        compiler_params=pltpu.CompilerParams(
+            collective_id=0, has_side_effects=True, vmem_limit_bytes=VMEM_LIMIT
+        ),
+        name="block_forward",
+    )(flat_in, mask, w_shard, proj_shard, narrow, wide)
+
+
+def block_backward_kernel(
+    gz_ref, x_ref, mask_ref, wall_ref, hat_one_ref, hat_two_ref, hat_three_ref, first_ref, second_ref,
+    narrow_ref, wide_ref, stats_ref, stats_wide_ref, dwp_ref, small_ref, square_ref,
+    ingrad_ref, wgrad_ref, pgrad_ref, sgrad_ref, ngrad_ref, ngrad_wide_ref, total_ref,
+    ds, ds_low, turned, ch_buf, ch_in, halo_in, taps, back_t, stat_three, stat_two, stat_one,
+    we_buf, we_in, wd_buf, wd_in, wr_buf, wr_in, pc_buf, pc_in, pr_buf, pr_in, pg_in,
+    small_ch, small_px, sq_ch, sq_px, norm_in, norm_wide_in,
+    c_send, c_recv, s_send, s_recv, h_send, h_recv, g_send, g_recv,
+    pc_send, pc_recv, pg_send, pg_recv, t_send, t_recv, u_send, u_recv, n_send, n_recv,
+):
+    p, c, z, y, x, core = place()
+    pix_targets = [(lax.rem(p + d, NPIX), c) for d in range(1, NPIX)]
+    ch_targets = [(p, lax.rem(c + d, NCH)) for d in range(1, NCH)]
+    greet(pix_targets + ch_targets)
+    count_all = float(NPIX * PX)
+
+    def weights(lanes):
+        return wall_ref[:, :, lanes].reshape(M, lanes.stop - lanes.start)
+
+    def own_lanes():
+        return pl.ds(pl.multiple_of(c * MID, MID), MID)
+
+    def stat_round(index, inbox, upstream, hat):
+        inbox[p] = jnp.zeros_like(inbox[p])
+        inbox[p, 0:1, :] = column_sums(upstream)
+        inbox[p, 1:2, :] = column_sums(upstream * hat)
+        copies = pix_copies(inbox, s_send.at[index], s_recv.at[index])
+        start_all(copies)
+        return copies
+
+    def stat_end(copies, inbox):
+        wait_all(copies)
+        return add_up(inbox)
+
+    def norm_back(upstream, hat, sums, gain, scale):
+        return gain * scale * (upstream - sums[0:1] / count_all - hat * (sums[1:2] / count_all))
+
+    def own_ch_copies(ref, inbox_index):
+        copies = []
+        for d in range(1, NCH):
+            copies.append(
+                remote(ref.at[c], ref.at[c], n_send.at[inbox_index, d - 1], n_recv.at[inbox_index, d - 1], ch_targets[d - 1])
+            )
+        return copies
+
+    small_ch[c] = small_ref[...]
+    small_copies = own_ch_copies(small_ch, 0)
+    start_all(small_copies)
+
+    for other in range(NCH):
+        for t in range(3):
+            for b in range(NPIX):
+                start = b * 128 + other * 32
+                pc_buf[other, t, b] = dwp_ref[t, start : start + 32, :].astype(BF)
+    proj_copies = ch_copies(lambda other: pc_buf.at[other], pc_in, pc_send, pc_recv)
+
+    wide_rows = 64
+
+    def expand_rows(m, carry):
+        rows = pl.ds(pl.multiple_of(m * wide_rows, wide_rows), wide_rows)
+        summed = hat_three_ref[rows, :] * wide_ref[0:1, :] + wide_ref[1:2, :] + x_ref[rows, :].astype(F32)
+        ds[rows, :] = gz_ref[rows, :] * gelu_slope(summed)
+        return carry
+
+    lax.fori_loop(0, PX // wide_rows, expand_rows, 0)
+    copies = stat_round(0, stat_three, ds[...], hat_three_ref[...])
+    start_all(proj_copies)
+    turned[0] = jnp.transpose(second_ref[...].astype(F32)).astype(BF)
+    turned[1] = jnp.transpose(first_ref[...].astype(F32)).astype(BF)
+    sums = stat_end(copies, stat_three)
+    norm_wide_in[c] = sums
+    ds_low[...] = norm_back(ds[...], hat_three_ref[...], sums, wide_ref[0:1, :], stats_wide_ref[0:1, :]).astype(BF)
+
+    def scatter_ch(index, product):
+        for m in range(NCH):
+            value = product(m)
+            ch_buf[index, m] = value.astype(BF)
+        copies = ch_copies(lambda other: ch_buf.at[index, other], ch_in.at[index], c_send.at[index], c_recv.at[index])
+        start_all(copies)
+        return copies
+
+    def scatter_end(index, copies):
+        wait_all(copies)
+        total = ch_buf[index, c].astype(F32)
+        for d in range(1, NCH):
+            total = total + ch_in[index, lax.rem(c + d, NCH)].astype(F32)
+        return total
+
+    def grad_copies(index, buf, inbox):
+        copies = []
+        for d in range(1, NPIX):
+            b = lax.rem(p + d, NPIX)
+            copies.append(
+                remote(buf.at[b], inbox.at[d - 1], g_send.at[index, d - 1], g_recv.at[index, d - 1], (b, c))
+            )
+        return copies
+
+    def expand_back(m):
+        wanted = wall_ref[2 * m : 2 * m + 2, :, W_EXPAND].reshape(MID, CIN)
+        return nt_dot(ds_low[...], wanted)
+
+    copies = scatter_ch(0, expand_back)
+    we_buf[...] = nn_dot(turned[0], ds_low[...]).astype(BF).reshape(NPIX, WPART, CIN)
+    we_copies = grad_copies(0, we_buf, we_in)
+    start_all(we_copies)
+    hat = hat_two_ref[...]
+    slope = gelu_slope(hat * narrow_ref[2:3, :] + narrow_ref[3:4, :])
+    upstream = scatter_end(0, copies) * slope
+    copies = stat_round(1, stat_two, upstream, hat)
+    wait_all(proj_copies)
+    for t in range(3):
+        total = pc_buf[c, t].astype(F32)
+        for d in range(1, NCH):
+            total = total + pc_in[lax.rem(c + d, NCH), t].astype(F32)
+        pr_buf[:, t] = total.astype(BF)
+    wait_all(small_copies)
+    small_px[p] = add_up(small_ch)
+    sums = stat_end(copies, stat_two)
+    norm_in[c, 2:4, :] = sums[0:2]
+
+    def halo_copy(side):
+        target = (p - 1, c) if side == 0 else (p + 1, c)
+        return remote(back_t.at[0], halo_in.at[side], h_send.at[side], h_recv.at[side], target)
+
+    gradient = norm_back(upstream, hat, sums, narrow_ref[2:3, :], stats_ref[1:2, :])
+    back_t[0] = gradient.astype(BF)
+
+    @pl.when(p > 0)
+    def _():
+        halo_copy(0).start()
+
+    @pl.when(p < NPIX - 1)
+    def _():
+        halo_copy(1).start()
+
+    def fill_taps(step, source):
+        for col in range(3):
+            tap = 3 * (step + 1) + col
+            moved = slide_rows(source.astype(F32), DILATION_RATE * (col - 1))
+            taps[:, tap * MID : (tap + 1) * MID] = moved.astype(BF)
+
+    fill_taps(0, back_t[0])
+
+    @pl.when(p < NPIX - 1)
+    def _():
+        halo_copy(0).wait_recv()
+
+    @pl.when(p == NPIX - 1)
+    def _():
+        halo_in[0] = jnp.zeros((PX, MID), BF)
+
+    fill_taps(-1, halo_in[0])
+
+    @pl.when(p > 0)
+    def _():
+        halo_copy(1).wait_recv()
+
+    @pl.when(p == 0)
+    def _():
+        halo_in[1] = jnp.zeros((PX, MID), BF)
+
+    fill_taps(1, halo_in[1])
+
+    def dilated_back(m):
+        wanted = wall_ref[2 * m : 2 * m + 2, :, W_DILATED].reshape(MID, TAP_LANES)
+        return nt_dot(taps[...], wanted)
+
+    copies = scatter_ch(1, dilated_back)
+    proj_rows = grad_copies(3, pr_buf, pr_in)
+    start_all(proj_rows)
+    for m in range(NPIX):
+        wd_buf[m] = nn_dot(turned[1, m * WPART : (m + 1) * WPART, :], taps[...]).astype(BF)
+    wd_copies = grad_copies(1, wd_buf, wd_in)
+    start_all(wd_copies)
+    hat = hat_one_ref[...]
+    slope = gelu_slope(hat * narrow_ref[0:1, :] + narrow_ref[1:2, :]) * mask_ref[...]
+    upstream = scatter_end(1, copies) * slope
+    copies = stat_round(2, stat_one, upstream, hat)
+    small_rows = [
+        remote(small_px.at[p], small_px.at[p], t_send.at[d - 1], t_recv.at[d - 1], pix_targets[d - 1])
+        for d in range(1, NPIX)
+    ]
+    start_all(small_rows)
+    sums = stat_end(copies, stat_one)
+    norm_in[c, 0:2, :] = sums[0:2]
+    norm_in[c, 4:8, :] = jnp.zeros((4, MID), F32)
+    gradient = norm_back(upstream, hat, sums, narrow_ref[0:1, :], stats_ref[0:1, :])
+
+    own_rows = pl.ds(pl.multiple_of(c * MID, MID), MID)
+    turned[2, own_rows, :] = jnp.transpose(gradient).astype(BF)
+    copies = [
+        remote(
+            turned.at[2, own_rows, :], turned.at[2, own_rows, :],
+            c_send.at[2, d - 1], c_recv.at[2, d - 1], ch_targets[d - 1],
+        )
+        for d in range(1, NCH)
+    ]
+    start_all(copies)
+    norm_copies = own_ch_copies(norm_in, 1) + own_ch_copies(norm_wide_in, 2)
+    start_all(norm_copies)
+    wait_all(copies)
+    wr_buf[...] = nn_dot(turned[2], x_ref[...]).astype(BF).reshape(NPIX, WPART, CIN)
+    wr_copies = grad_copies(2, wr_buf, wr_in)
+    start_all(wr_copies)
+    full = jnp.transpose(turned[2].astype(F32)).astype(BF)
+    ingrad_ref[...] = nn_dot(full, weights(W_REDUCE)) + ds[...]
+    wait_all(proj_rows)
+    for t in range(3):
+        total = pr_buf[p, t].astype(F32)
+        for d in range(NPIX - 1):
+            total = total + pr_in[d, t].astype(F32)
+        pg_in[c, t] = total
+    pg_copies = [
+        remote(pg_in.at[c], pg_in.at[c], pg_send.at[d - 1], pg_recv.at[d - 1], ch_targets[d - 1])
+        for d in range(1, NCH)
+    ]
+    start_all(pg_copies)
+
+    def grad_end(copies, buf, inbox, lanes):
+        wait_all(copies)
+        total = buf[p].astype(F32)
+        for d in range(NPIX - 1):
+            total = total + inbox[d].astype(F32)
+        wgrad_ref[:, lanes] = total
+        return fold(total * total)
+
+    squares = square_ref[...] + grad_end(we_copies, we_buf, we_in, W_EXPAND)
+    squares = squares + grad_end(wd_copies, wd_buf, wd_in, W_DILATED)
+    wait_all(pg_copies)
+    for t in range(3):
+        for other in range(NCH):
+            pgrad_ref[t, other * 32 : (other + 1) * 32, :] = pg_in[other, t]
+        squares = squares + fold(pg_in[c, t] * pg_in[c, t])
+    wait_all(small_rows)
+    sgrad_ref[...] = add_up(small_px)
+    wait_all(norm_copies)
+    ngrad_ref[...] = norm_in[...]
+    ngrad_wide_ref[...] = norm_wide_in[...]
+    shared = fold(sgrad_ref[...] * sgrad_ref[...])
+    for other in range(NCH):
+        shared = shared + fold(norm_in[other] * norm_in[other])
+        piece = norm_wide_in[other]
+        shared = shared + fold(piece * piece)
+    squares = squares + grad_end(wr_copies, wr_buf, wr_in, W_REDUCE)
+    sq_ch[c] = squares
+    copies = [
+        remote(sq_ch.at[c], sq_ch.at[c], u_send.at[0, d - 1], u_recv.at[0, d - 1], ch_targets[d - 1])
+        for d in range(1, NCH)
+    ]
+    start_all(copies)
+    wait_all(copies)
+    sq_px[p] = add_up(sq_ch)
+    copies = [
+        remote(sq_px.at[p], sq_px.at[p], u_send.at[1, d - 1], u_recv.at[1, d - 1], pix_targets[d - 1])
+        for d in range(1, NPIX)
+    ]
+    start_all(copies)
+    wait_all(copies)
+    everything = add_up(sq_px) + shared
+    total = jnp.sum(jnp.sum(everything, axis=0, keepdims=True), axis=1, keepdims=True)
+    norm = jnp.sqrt(total)
+    factor = jnp.minimum(1.0, CLIP_NORM / (norm + 1e-06))
+    line = lax.broadcasted_iota(jnp.int32, (8, 128), 0)
+    total_ref[...] = jnp.where(line == 0, norm, factor)
+
+    @pl.when(p > 0)
+    def _():
+        halo_copy(0).wait_send()
+
+    @pl.when(p < NPIX - 1)
+    def _():
+        halo_copy(1).wait_send()
+
+
+def block_backward(*operands):
+    dma = pltpu.SemaphoreType.DMA
+    shape = jax.ShapeDtypeStruct
+    vmem = pltpu.VMEM
+    return pl.pallas_call(
+        block_backward_kernel,
+        out_shape=(
+            shape((PX, CIN), F32),
+            shape((WPART, W_LANES), F32),
+            shape((3, 128, HID), F32),
+            shape((SMALL_ROWS, 128), F32),
+            shape((NCH, 8, MID), F32),
+            shape((NCH, 8, CIN), F32),
+            shape((8, 128), F32),
+        ),
+        in_specs=[whole_vmem()] * 16,
+        out_specs=[whole_vmem()] * 7,
+        scratch_shapes=[
+            vmem((PX, CIN), F32),
+            vmem((PX, CIN), BF),
+            vmem((3, M, PX), BF),
+            vmem((2, NCH, PX, MID), BF),
+            vmem((2, NCH, PX, MID), BF),
+            vmem((2, PX, MID), BF),
+            vmem((PX, TAP_LANES), BF),
+            vmem((1, PX, MID), BF),
+            vmem((NPIX, 8, CIN), F32),
+            vmem((NPIX, 8, MID), F32),
+            vmem((NPIX, 8, MID), F32),
+            vmem((NPIX, WPART, CIN), BF),
+            vmem((NPIX - 1, WPART, CIN), BF),
+            vmem((NPIX, WPART, TAP_LANES), BF),
+            vmem((NPIX - 1, WPART, TAP_LANES), BF),
+            vmem((NPIX, WPART, CIN), BF),
+            vmem((NPIX - 1, WPART, CIN), BF),
+            vmem((NCH, 3, NPIX, 32, HID), BF),
+            vmem((NCH, 3, NPIX, 32, HID), BF),
+            vmem((NPIX, 3, 32, HID), BF),
+            vmem((NPIX - 1, 3, 32, HID), BF),
+            vmem((NCH, 3, 32, HID), F32),
+            vmem((NCH, SMALL_ROWS, 128), F32),
+            vmem((NPIX, SMALL_ROWS, 128), F32),
+            vmem((NCH, 8, 128), F32),
+            vmem((NPIX, 8, 128), F32),
+            vmem((NCH, 8, MID), F32),
+            vmem((NCH, 8, CIN), F32),
+            dma((3, NCH - 1)), dma((3, NCH - 1)),
+            dma((3, NPIX - 1)), dma((3, NPIX - 1)),
+            dma((2,)), dma((2,)),
+            dma((4, NPIX - 1)), dma((4, NPIX - 1)),
+            dma((NCH - 1,)), dma((NCH - 1,)),
+            dma((NCH - 1,)), dma((NCH - 1,)),
+            dma((NPIX - 1,)), dma((NPIX - 1,)),
+            dma((2, NPIX - 1)), dma((2, NPIX - 1)),
+            dma((3, NCH - 1)), dma((3, NCH - 1)),
+        ],
+        compiler_params=pltpu.CompilerParams(
+            collective_id=3, has_side_effects=True, vmem_limit_bytes=VMEM_LIMIT
+        ),
+        name="block_backward",
+    )(*operands)
 
 
 def per_device_rows(
@@ -1320,95 +1968,50 @@
     small_m,
     small_v,
 ):
-    rows_per_shard, columns_per_shard, wide_dev = features.shape
-    pixels = rows_per_shard * columns_per_shard
-    groups = lax.axis_size("ch")
+
     block_id = lax.axis_index("ch")
-    pix_devices = lax.axis_size("pix")
-    middle_per_shard = M // groups
-    count_all = float(pixels * pix_devices)
-    flat_in = features.reshape(pixels, wide_dev)
-    mask_flat = valid_mask.reshape(pixels).astype(jnp.float32)
+    flat_in = features.reshape(PX, CIN)
+    mask_column = valid_mask.reshape(PX, 1).astype(F32)
     gains = norm_params[0]
     shifts = norm_params[1]
 
     def owned(vector, offset, width):
         return lax.dynamic_slice_in_dim(vector, offset + block_id * width, width)
 
-    reduce_w, dilated_w, expand_w = (
-        lax.all_gather(w_reduce.astype(jnp.bfloat16), "pix", axis=1, tiled=True),
-        lax.all_gather(w_dilated.astype(jnp.bfloat16), "pix", axis=1, tiled=True),
-        lax.all_gather(w_expand.astype(jnp.bfloat16), "pix", axis=0, tiled=True),
-    )
-    reduced = lax.psum_scatter(
-        jnp.dot(flat_in, reduce_w, preferred_element_type=jnp.float32),
-        "ch",
-        scatter_dimension=1,
-        tiled=True,
-    )
-    local_counts = jnp.sum(label_mask.astype(jnp.float32), axis=(1, 2))
-    reduced_sum = jnp.sum(reduced, axis=0)
-    reduced_sq = jnp.sum(reduced * reduced, axis=0)
-    reduced_sum, reduced_sq = lax.psum((reduced_sum, reduced_sq), "pix")
-    task_counts = lax.psum(local_counts, "pix")
-    task_counts = jnp.maximum(task_counts, 1.0)
-    gain_one = owned(gains, 0, middle_per_shard)
-    norm_one, hat_one, scale_one = forward_norm(
-        reduced, reduced_sum, reduced_sq, count_all, gain_one, owned(shifts, 0, middle_per_shard)
-    )
-    first = (smooth(norm_one) * mask_flat[:, None]).astype(jnp.bfloat16)
-    first_gathered = channel_gather(first).reshape(rows_per_shard, columns_per_shard, M)
-    bordered_input = with_halo(first_gathered, (("pix", 0),), DILATION_RATE)
-    bordered_input = jnp.pad(bordered_input, ((0, 0), (DILATION_RATE, DILATION_RATE), (0, 0)))
-    middle = jnp.zeros((pixels, middle_per_shard), jnp.float32)
-    for tap_index in range(9):
-        kernel_row, kernel_column = divmod(tap_index, 3)
-        sliding_patch = bordered_input[
-            kernel_row * DILATION_RATE : kernel_row * DILATION_RATE + rows_per_shard,
-            kernel_column * DILATION_RATE : kernel_column * DILATION_RATE + columns_per_shard,
-        ].reshape(pixels, M)
-        middle = middle + jnp.dot(
-            sliding_patch, dilated_w[tap_index], preferred_element_type=jnp.float32
-        )
-    gain_two = owned(gains, M, middle_per_shard)
-    middle_sum, middle_sq = pixel_sums(jnp.sum(middle, axis=0), jnp.sum(middle * middle, axis=0))
-    norm_two, hat_two, scale_two = forward_norm(
-        middle, middle_sum, middle_sq, count_all, gain_two, owned(shifts, M, middle_per_shard)
-    )
-    second = smooth(norm_two).astype(jnp.bfloat16)
-    second_all = channel_gather(second)
-    expanded = jnp.dot(second_all, expand_w, preferred_element_type=jnp.float32)
-    gain_three = owned(gains, 2 * M, wide_dev)
-    expand_sum, expand_sq = pixel_sums(
-        jnp.sum(expanded, axis=0), jnp.sum(expanded * expanded, axis=0)
-    )
-    norm_three, hat_three, scale_three = forward_norm(
-        expanded, expand_sum, expand_sq, count_all, gain_three, owned(shifts, 2 * M, wide_dev)
-    )
-    summed_in = norm_three + flat_in.astype(jnp.float32)
-    shared = smooth(summed_in).astype(jnp.bfloat16)
+    def own_row(array, axis):
+        return lax.dynamic_slice_in_dim(array, block_id, 1, axis=axis)
+
+    w_shard = jnp.concatenate(
+        [w_reduce.T, w_dilated.transpose(1, 0, 2).reshape(WPART, TAP_LANES), w_expand], axis=1
+    ).astype(BF)
+    w_seg = tap_weights(head_weight, head_rates)
+    local_counts = jnp.sum(label_mask.astype(F32), axis=(1, 2))
+    narrow = jnp.stack(
+        [
+            owned(gains, 0, MID),
+            owned(shifts, 0, MID),
+            owned(gains, M, MID),
+            owned(shifts, M, MID),
+            jnp.pad(local_counts, (0, MID - 3)),
+        ]
+        + [jnp.zeros((MID,), F32)] * 3
+    )
+    wide = jnp.stack([owned(gains, 2 * M, CIN), owned(shifts, 2 * M, CIN)] + [jnp.zeros((CIN,), F32)] * 6)
+    shared, hat_one, hat_two, hat_three, w_all, first, second, stats, stats_wide, proj_t = block_forward(
+        flat_in, mask_column, w_shard, jnp.transpose(head_proj, (0, 2, 1)).astype(BF), narrow, wide
+    )
     branch_bias, proj_bias, sem_w, depth_w, normal_w, sem_b, depth_b, normal_b = unpack_small(
         head_small
     )
-    out_weights = (
-        sem_w.astype(jnp.bfloat16),
-        depth_w.astype(jnp.bfloat16),
-        normal_w.astype(jnp.bfloat16),
-    )
-    own_row = lambda array, axis: lax.dynamic_slice_in_dim(array, block_id, 1, axis=axis)
-    w_seg = tap_weights(head_weight, head_rates)
-    q_rows, shared_all = heads_forward(shared, w_seg)
-    proj_t = lax.all_gather(
-        jnp.transpose(head_proj.astype(jnp.bfloat16), (0, 2, 1)), "pix", axis=2, tiled=True
-    )
     out_stack = jnp.stack(
-        [jnp.pad(weight, ((0, 0), (0, 32 - weight.shape[1]))) for weight in out_weights]
+        [jnp.pad(weight.astype(BF), ((0, 0), (0, 32 - weight.shape[1]))) for weight in (sem_w, depth_w, normal_w)]
     )
     out_bias = jnp.stack(
         [jnp.pad(bias, (0, 32 - bias.shape[0])) for bias in (sem_b, depth_b, normal_b)], axis=1
     )
+    q_rows, shared_all = heads_forward(shared, w_seg)
     targets = jnp.concatenate([own_row(depth_target, 0), own_row(normal_target, 1)[:, 0]], axis=0)
-    pre_grad, proj_grad, out_grad, bias_rows, out_bias_rows = heads_middle(
+    pre_grad, proj_part, out_grad, bias_rows, out_bias_rows = heads_middle(
         q_rows,
         branch_bias.T,
         proj_bias.T,
@@ -1417,88 +2020,34 @@
         out_bias,
         own_row(sem_label, 0),
         targets,
-        own_row(label_mask, 1)[:, 0].astype(jnp.float32),
-        jnp.broadcast_to(task_counts[:, None], (3, columns_per_shard)),
+        own_row(label_mask, 1)[:, 0].astype(F32),
+        jnp.broadcast_to(stats[2, :3][:, None], (3, WIDTH)),
     )
     small_term = pack_small(
         [bias_rows[:4, 0], bias_rows[4, 0]]
         + [out_grad[0, :NCLS].T, out_grad[1, :1].T, out_grad[2, :3].T]
         + [out_bias_rows[0, 0, :NCLS], out_bias_rows[1, 0, :1], out_bias_rows[2, 0, :3]]
     )
-    tap_sums, combined = heads_backward(pre_grad, shared_all, w_seg)
+    small_count = small_term.shape[0]
+    small_term = jnp.pad(small_term, (0, SMALL_ROWS * 128 - small_count)).reshape(SMALL_ROWS, 128)
+    tap_sums, combined, squares = heads_backward(pre_grad, shared_all, w_seg)
     head_shard, rates_shard = tap_grads(tap_sums)
-    shared_slope = combined * smooth_slope(summed_in)
-    expand_up, gain_three_grad, shift_three_grad = backward_norm(
-        shared_slope, hat_three, scale_three, count_all, gain_three
-    )
-    expand_back = expand_up.astype(jnp.bfloat16)
-    expand_grad = contract_first(second_all, expand_back)
-    second_back = channel_parts(contract_last(expand_back, expand_w))
-    middle_up, gain_two_grad, shift_two_grad = backward_norm(
-        second_back * smooth_slope(norm_two), hat_two, scale_two, count_all, gain_two
-    )
-    middle_gradient = middle_up.astype(jnp.bfloat16)
-    dilated_list = []
-    for tap_index in range(9):
-        kernel_row, kernel_column = divmod(tap_index, 3)
-        sliding_patch = bordered_input[
-            kernel_row * DILATION_RATE : kernel_row * DILATION_RATE + rows_per_shard,
-            kernel_column * DILATION_RATE : kernel_column * DILATION_RATE + columns_per_shard,
-        ].reshape(pixels, M)
-        dilated_list.append(contract_first(sliding_patch, middle_gradient))
-    dilated_grad = jnp.stack(dilated_list)
-    canvas_gradient = with_halo(
-        middle_gradient.reshape(rows_per_shard, columns_per_shard, middle_per_shard),
-        (("pix", 0),),
-        DILATION_RATE,
-    )
-    canvas_gradient = jnp.pad(canvas_gradient, ((0, 0), (DILATION_RATE, DILATION_RATE), (0, 0)))
-    first_part = jnp.zeros((pixels, M), jnp.float32)
-    for tap_index in range(9):
-        kernel_row, kernel_column = divmod(tap_index, 3)
-        sliding_patch = canvas_gradient[
-            (2 - kernel_row) * DILATION_RATE : (2 - kernel_row) * DILATION_RATE + rows_per_shard,
-            (2 - kernel_column) * DILATION_RATE : (2 - kernel_column) * DILATION_RATE
-            + columns_per_shard,
-        ].reshape(pixels, middle_per_shard)
-        first_part = first_part + contract_last(sliding_patch, dilated_w[tap_index])
-    first_back = channel_parts(first_part) * mask_flat[:, None] * smooth_slope(norm_one)
-    reduce_up, gain_one_grad, shift_one_grad = backward_norm(
-        first_back, hat_one, scale_one, count_all, gain_one
-    )
-    reduce_all = channel_gather(reduce_up.astype(jnp.bfloat16))
-    reduce_grad = contract_first(flat_in, reduce_all)
-    input_grad = contract_last(reduce_all, reduce_w) + shared_slope
-    reduce_shard, dilated_shard, expand_shard, proj_shard = (
-        lax.psum_scatter(reduce_grad, "pix", scatter_dimension=1, tiled=True),
-        lax.psum_scatter(dilated_grad, "pix", scatter_dimension=1, tiled=True),
-        lax.psum_scatter(expand_grad, "pix", scatter_dimension=0, tiled=True),
-        lax.psum_scatter(lax.psum(proj_grad, "ch"), "pix", scatter_dimension=1, tiled=True),
-    )
-    norm_local = jnp.zeros((2, 2 * M + C), jnp.float32)
-    for offset, width, gain_grad, shift_grad in (
-        (0, middle_per_shard, gain_one_grad, shift_one_grad),
-        (M, middle_per_shard, gain_two_grad, shift_two_grad),
-        (2 * M, wide_dev, gain_three_grad, shift_three_grad),
-    ):
-        norm_local = lax.dynamic_update_slice(
-            norm_local, jnp.stack([gain_grad, shift_grad]), (0, offset + block_id * width)
-        )
-    big_local = (
-        jnp.sum(reduce_shard * reduce_shard)
-        + jnp.sum(dilated_shard * dilated_shard)
-        + jnp.sum(expand_shard * expand_shard)
-        + jnp.sum(head_shard * head_shard)
-        + jnp.sum(rates_shard * rates_shard)
-        + jnp.sum(proj_shard * proj_shard) / groups
-    )
-    big_squares, norm_grad, small_grad = lax.psum(
-        (big_local, norm_local / pix_devices, small_term), ("pix", "ch")
-    )
-    grad_norm = jnp.sqrt(
-        big_squares + jnp.sum(norm_grad * norm_grad) + jnp.sum(small_grad * small_grad)
-    )
-    factor = jnp.minimum(1.0, CLIP_NORM / (grad_norm + 1e-06))
+    input_grad, w_grad, proj_shard, small_sum, norm_narrow, norm_wide, totals = block_backward(
+        combined, flat_in, mask_column, w_all, hat_one, hat_two, hat_three, first, second,
+        narrow, wide, stats, stats_wide, proj_part, small_term, squares,
+    )
+    reduce_shard = w_grad[:, W_REDUCE].T
+    dilated_shard = w_grad[:, W_DILATED].reshape(WPART, 9, MID).transpose(1, 0, 2)
+    expand_shard = w_grad[:, W_EXPAND]
+    small_grad = small_sum.reshape(-1)[:small_count]
+    norm_grad = jnp.stack(
+        [
+            jnp.concatenate([norm_narrow[:, 1].reshape(-1), norm_narrow[:, 3].reshape(-1), norm_wide[:, 1].reshape(-1)]),
+            jnp.concatenate([norm_narrow[:, 0].reshape(-1), norm_narrow[:, 2].reshape(-1), norm_wide[:, 0].reshape(-1)]),
+        ]
+    )
+    grad_norm = totals[0, 0]
+    factor = totals[1, 0]
     reduce_new, reduce_first, reduce_second = adam_step(
         w_reduce, m_reduce, v_reduce, reduce_shard * factor, RATE_MATRIX, DECAY
     )
@@ -1523,10 +2072,10 @@
     small_new, small_first, small_second = adam_step(
         head_small, small_m, small_v, small_grad * factor, RATE_SMALL, 0.0
     )
-    depth_bias_grad = small_grad[small_grad.shape[0] - 4]
+    depth_bias_grad = small_grad[small_count - 4]
     return (
-        shared.reshape(rows_per_shard, columns_per_shard, wide_dev),
-        input_grad.reshape(rows_per_shard, columns_per_shard, wide_dev),
+        shared.reshape(ROWS, WIDTH, CIN),
+        input_grad.reshape(ROWS, WIDTH, CIN),
         grad_norm,
         reduce_new,
         reduce_first,

time: 1020 us -> 590 us (0.58)
  waiting for transfers between devices: 308 us -> 0 us
  blocking collectives: 252 us -> 0 us
  Pallas kernels: 286 us -> 515 us
  matrix products: 31.6 us -> 0 us
  between operations: 24.4 us -> 1.35 us
  other arithmetic: 54.7 us -> 38.8 us
  starting transfers between devices: 13.3 us -> 0 us
  local copies, waits for them, and re-layouts: 44 us -> 33.5 us
    reduce_scatter x7 -> x0, waiting for transfers between devices: 259 us -> none  [the longest x1 71.2 us: per_device_rows(): lax.psum_scatter(dilated_grad, 'pix', scatter_dimension=1, tiled=True)]
    pallas_call x0 -> x2, Pallas kernels: none -> 216 us  [the longest x1 115 us: block_backward(): pl.pallas_call(block_backward_kernel, out_shape=(shape((PX, CIN), F32), s...]
    psum x7 -> x0, blocking collectives: 165 us -> none  [the longest x3 65 us: back_pair(): return lax.psum((first, second), 'pix')]
    all_gather x5 -> x0, blocking collectives: 87.2 us -> none  [the longest x1 33.7 us: per_device_rows(): lax.all_gather(w_expand.astype(jnp.bfloat16), 'pix', axis=0, tiled=True)]
    psum x1 -> x0, waiting for transfers between devices: 32.5 us -> none  [per_device_rows(): lax.psum(proj_grad, 'ch')]
    dot_general x33 -> x0, matrix products: 31.6 us -> none  [the longest x11 14.4 us: contract_first(): lax.dot_general(left, right, (((0,), (0,)), ((), ())), preferred_element_...]
    reduce_sum x13 -> x1, other arithmetic: 17.5 us -> 0.8 us  [per_device_rows(): local_counts = jnp.sum(label_mask.astype(F32), axis=(1, 2))]
    ppermute x4 -> x0, waiting for transfers between devices: 15.5 us -> none  [the longest x2 11.8 us: with_halo(): lax.ppermute(tail, axis, [(i, (i + 1) % count) for i in range(ends)])]
  transfers between devices with their start and end apart: 14 -> 0, of which waited for: 11 -> 0; matrix products, arithmetic and copies ran while one was open for 8% -> 0% of each run, Pallas kernels for 9% -> 0%
where the time goes in v2:
time: 590 us; the launch traced here: 589 us
  Pallas kernels  515 us (87%)
  other arithmetic  38.8 us (7%)
  local copies, waits for them, and re-layouts  33.5 us (6%)
    pallas_call x1, Pallas kernels, heads_backward(): pl.pallas_call(heads_backward_kernel, out_shape=(jax.ShapeDtypeStruct((SE...  192 us
    pallas_call x1, Pallas kernels, block_backward(): pl.pallas_call(block_backward_kernel, out_shape=(shape((PX, CIN), F32), s...  115 us
    pallas_call x1, Pallas kernels, block_forward(): pl.pallas_call(block_forward_kernel, out_shape=(shape((PX, CIN), BF), sha...  101 us
    pallas_call x1, Pallas kernels, heads_forward(): pl.pallas_call(heads_forward_kernel, out_shape=(jax.ShapeDtypeStruct((4,...  99.9 us

profile of v2, /device:TPU:0, one launch (start us, length us, event | category | flops | bytes accessed | tf_op | source)
XLA Modules:
  0.0 588.6 jit_solution(9489711036298530401)
XLA Ops:
  3.2 1.0 copy_bitcast_fusion.1
  5.8 1.8 copy.168
  10.7 100.5 %block_forward.1 = (bf16[512,512]{1,0:T(8,128)(2,1)}, f32[512,128]{1,0:T(8,128)}, f32[512,128]{1,0:T(8,128)}, f32[512,512]{1,0:T(8,128)}, bf16[8,64,2176]{2,1,0:...) custom-call(bf16[512,512]{1,0:T(8,128)(2,1)} %bitcast.156, ...), custom_call_target="tpu_custom_call" | custom-call | tf_op jit(solution)/shard_map/block_forward/pallas_call | solution.py:1564
  112.2 2.9 convert_element_type.77
  115.6 1.3 copy-done.2
  116.9 99.9 %heads_forward.1 = (bf16[4,768,128]{2,1,0:T(8,128)(2,1)}, bf16[8,512,512]{2,1,0:T(8,128)(2,1)}) custom-call(bf16[512,512]{1,0:T(8,128)(2,1)} %get-tuple-element.61.x_ref, bf16[3,704,512]{2,1,0:T(8,128)(2,1)} %bitcast.144), custom_call_target="tpu_custom_call" | custom-call | tf_op jit(solution)/shard_map/heads_forward/pallas_call | solution.py:845
  222.0 1.2 constant_dynamic-slice_fusion.3.label_ref
  227.1 7.1 %heads_middle.1 = (bf16[4,768,128]{2,1,0:T(8,128)(2,1)}, f32[3,1024,256]{2,1,0:T(8,128)}, f32[3,32,256]{2,1,0:T(8,128)}, f32[5,8,768]{2,1,0:T(8,128)}, f32[3,8,32]{2,1,0:T(8,128)}) custom-call(bf16[4,768,128]{2,1,0:T(8,128)(2,1)} %get-tuple-element.62.q_ref, f32[768,4]{1,0:T(8,128)} %bitcast.159, f32[256,3]{1,0:T(8,128)} %bitcast.169, ...), custom_call_target="tpu_custom_call" | custom-call | tf_op jit(solution)/shard_map/heads_middle/pallas_call | solution.py:926
  234.2 192.4 %heads_backward.1 = (f32[3,704,512]{2,1,0:T(8,128)}, f32[512,512]{1,0:T(8,128)}, f32[8,128]{1,0:T(8,128)}) custom-call(bf16[4,768,128]{2,1,0:T(8,128)(2,1)} %get-tuple-element.65.dq_ref, bf16[8,512,512]{2,1,0:T(8,128)(2,1)} %get-tuple-element.66.xall_ref, bf16[3,704,512]{2,1,0:T(8,128)(2,1)} %bitcast.145), custom_call_target="tpu_custom_call" | custom-call | tf_op jit(solution)/shard_map/heads_backward/pallas_call | solution.py:1243
  431.7 1.2 slice.177
  435.0 115.2 %block_backward.1 = (f32[512,512]{1,0:T(8,128)}, f32[64,2176]{1,0:T(8,128)}, f32[3,128,256]{2,1,0:T(8,128)}, f32[80,128]{1,0:T(8,128)}, f32[4,8,128]{2,1,0:T(8,1...) custom-call(f32[512,512]{1,0:T(8,128)} %get-tuple-element.67.gz_ref, bf16[512,512]{1,0:T(8,128)(2,1)} %bitcast.157, ...), custom_call_target="tpu_custom_call" | custom-call | tf_op jit(solution)/shard_map/block_backward/pallas_call | solution.py:1880
  550.2 1.3 fusion.37
  551.5 2.4 fusion.29
  553.9 2.7 fusion.26
  556.6 2.4 fusion.24
  559.1 2.7 copy.209
  564.6 1.8 broadcast_multiply_fusion
  566.5 1.0 slice-done
  567.8 10.3 %fusion.18 = (bf16[3,9,96,512]{3,2,1,0:T(8,128)(2,1)}, f32[3,9,96,512]{3,2,1,0:T(8,128)}, f32[3,9,96,512]{3,2,1,0:T(8,128)}, f32[3,9,96,512]{3,2,1,0:T(8,128)}) fusion(f32[3,9,96,512]{3,2,1,0:T(8,128)S(1)} %bitcast.140, f32[3,9,96,512]{3,2,1,0:T(8,128)S(1)} %bitcast.147, f32[3,9,96,512]{3,2,1,0:T(8,128)} %param.50, f32[3,9,96,512]{3,2,1,0:T(8,128)S(1)} %bitcast.141), kind=kLoop, calls=%fused_computation.102 | loop fusion | flops 21233664 | bytes 39813120 | tf_op jit(solution)/shard_map/convert_element_type | solution.py:2099
  578.1 3.4 fusion.16
  582.5 1.4 multiply_subtract_fusion.7
  583.9 1.3 multiply_subtract_fusion.6
  585.7 1.9 copy.228
  587.6 1.0 copy.229
  (147 shorter events, 29.3 us)
Async XLA Ops:
  0.7 222.5 %copy-start = (f32[3,4,128]{2,1,0:T(4,128)S(1)}, f32[3,4,128]{2,1,0:T(4,128)}, u32[]{:S(2)}) copy-start(f32[3,4,128]{2,1,0:T(4,128)} %param.34) | copy-start | bytes 18436
  115.1 101.6 %slice-start.4 = ((f32[9751]{0:T(1024)}), f32[3072]{0:T(1024)S(1)}, s32[]{:S(2)}) async-start(f32[9751]{0:T(1024)} %param.57), calls=%async_computation.4 | async-start | bytes 24576 | tf_op jit(solution)/shard_map/slice | solution.py:95
  115.1 102.6 %slice-start.5 = ((f32[9751]{0:T(1024)}), f32[768]{0:T(1024)S(1)}, s32[]{:S(2)}) async-start(f32[9751]{0:T(1024)} %param.57), calls=%async_computation.5 | async-start | bytes 8192 | tf_op jit(solution)/shard_map/slice | solution.py:95
  115.1 103.4 %copy-start.10 = (f32[9751]{0:T(1024)S(1)}, f32[9751]{0:T(1024)}, u32[]{:S(2)}) copy-start(f32[9751]{0:T(1024)} %param.57) | copy-start | bytes 117016
  429.0 122.5 %copy-start.6 = (f32[512,64]{0,1:T(8,128)S(1)}, f32[512,64]{0,1:T(8,128)}, u32[]{:S(2)}) copy-start(f32[512,64]{0,1:T(8,128)} %param.36) | copy-start | bytes 393220
  429.0 122.5 %copy-start.13 = (f32[512,64]{0,1:T(8,128)S(1)}, f32[512,64]{0,1:T(8,128)}, u32[]{:S(2)}) copy-start(f32[512,64]{0,1:T(8,128)} %param.37) | copy-start | bytes 393220
  429.0 122.4 %copy-start.14 = (f32[512,64]{0,1:T(8,128)S(1)}, f32[512,64]{0,1:T(8,128)}, u32[]{:S(2)}) copy-start(f32[512,64]{0,1:T(8,128)} %param.38) | copy-start | bytes 393220
  434.9 118.9 %copy-start.3 = (f32[9,64,128]{2,1,0:T(8,128)S(1)}, f32[9,64,128]{2,1,0:T(8,128)}, u32[]{:S(2)}) copy-start(f32[9,64,128]{2,1,0:T(8,128)} %param.39) | copy-start | bytes 884740
  434.9 118.9 %copy-start.8 = (f32[9,64,128]{2,1,0:T(8,128)S(1)}, f32[9,64,128]{2,1,0:T(8,128)}, u32[]{:S(2)}) copy-start(f32[9,64,128]{2,1,0:T(8,128)} %param.40) | copy-start | bytes 884740
  434.9 118.9 %copy-start.9 = (f32[9,64,128]{2,1,0:T(8,128)S(1)}, f32[9,64,128]{2,1,0:T(8,128)}, u32[]{:S(2)}) copy-start(f32[9,64,128]{2,1,0:T(8,128)} %param.41) | copy-start | bytes 884740
  434.9 121.7 %copy-start.7 = (f32[64,512]{1,0:T(8,128)S(1)}, f32[64,512]{1,0:T(8,128)}, u32[]{:S(2)}) copy-start(f32[64,512]{1,0:T(8,128)} %param.42) | copy-start | bytes 393220
  435.0 121.7 %copy-start.15 = (f32[64,512]{1,0:T(8,128)S(1)}, f32[64,512]{1,0:T(8,128)}, u32[]{:S(2)}) copy-start(f32[64,512]{1,0:T(8,128)} %param.43) | copy-start | bytes 393220
  435.0 121.7 %copy-start.16 = (f32[64,512]{1,0:T(8,128)S(1)}, f32[64,512]{1,0:T(8,128)}, u32[]{:S(2)}) copy-start(f32[64,512]{1,0:T(8,128)} %param.44) | copy-start | bytes 393220
  556.6 5.9 %copy-start.11 = (f32[512,96]{0,1:T(8,128)S(1)}, f32[512,96]{0,1:T(8,128)}, u32[]{:S(2)}) copy-start(f32[512,96]{0,1:T(8,128)} %param.46) | copy-start | bytes 589828
  556.6 5.9 %copy-start.12 = (f32[512,96]{0,1:T(8,128)S(1)}, f32[512,96]{0,1:T(8,128)}, u32[]{:S(2)}) copy-start(f32[512,96]{0,1:T(8,128)} %param.47) | copy-start | bytes 589828
  567.7 14.6 %copy-start.23 = (f32[4,8,128]{2,1,0:T(8,128)S(1)}, f32[4,8,128]{2,1,0:T(8,128)}, u32[]{:S(2)}) copy-start(f32[4,8,128]{2,1,0:T(8,128)} %get-tuple-element.85) | copy-start | bytes 49156
  567.7 14.7 %copy-start.17 = (f32[2,3072]{1,0:T(2,128)S(1)}, f32[2,3072]{1,0:T(2,128)}, u32[]{:S(2)}) copy-start(f32[2,3072]{1,0:T(2,128)} %param.54) | copy-start | bytes 73732
  567.8 14.7 %copy-start.21 = (f32[2,3072]{1,0:T(2,128)S(1)}, f32[2,3072]{1,0:T(2,128)}, u32[]{:S(2)}) copy-start(f32[2,3072]{1,0:T(2,128)} %param.55) | copy-start | bytes 73732
  567.8 14.7 %copy-start.22 = (f32[2,3072]{1,0:T(2,128)S(1)}, f32[2,3072]{1,0:T(2,128)}, u32[]{:S(2)}) copy-start(f32[2,3072]{1,0:T(2,128)} %param.56) | copy-start | bytes 73732
  567.8 16.1 %copy-start.18 = (f32[9751]{0:T(1024)S(1)}, f32[9751]{0:T(1024)}, u32[]{:S(2)}) copy-start(f32[9751]{0:T(1024)} %param.58) | copy-start | bytes 117016
  567.8 16.1 %copy-start.19 = (f32[9751]{0:T(1024)S(1)}, f32[9751]{0:T(1024)}, u32[]{:S(2)}) copy-start(f32[9751]{0:T(1024)} %param.59) | copy-start | bytes 117016
  567.8 16.1 %copy-start.20 = (f32[80,128]{1,0:T(8,128)S(1)}, f32[80,128]{1,0:T(8,128)}, u32[]{:S(2)}) copy-start(f32[80,128]{1,0:T(8,128)} %get-tuple-element.87) | copy-start | bytes 122884
  567.8 20.8 %copy-start.1 = (f32[3,4,128]{2,1,0:T(4,128)S(1)}, f32[3,4,128]{2,1,0:T(4,128)}, u32[]{:S(2)}) copy-start(f32[3,4,128]{2,1,0:T(4,128)} %param.34) | copy-start | bytes 18436
  578.1 9.5 %copy-start.4 = (f32[512,512]{1,0:T(8,128)S(1)}, f32[512,512]{1,0:T(8,128)}, u32[]{:S(2)}) copy-start(f32[512,512]{1,0:T(8,128)} %get-tuple-element.80) | copy-start | bytes 3145732
  (6 other events, 18.5 us)

commit v3 on v2

--- a/solution.py
+++ b/solution.py
@@ -590,18 +590,31 @@
 VMEM_LIMIT = 60 * 2**20
 
 
-def row_groups():
+REACH = tuple(rate // ROWS for rate in aspp_rates)
+
+
+def tap_groups():
     groups = []
-    for rate_index, rate in enumerate(aspp_rates):
-        for step in (-1, 0, 1):
-            if abs(step) * rate // ROWS < NPIX:
-                groups.append((rate_index, step))
+    first = 0
+    for rate_index, step in ((1, -1), (0, -1), (None, 0), (0, 0), (1, 0), (2, 0), (0, 1), (1, 1)):
+        if rate_index is None:
+            groups.append((0, first, 0, 0, (0,)))
+            first += 1
+        else:
+            rate = aspp_rates[rate_index]
+            groups.append((rate_index + 1, first, step, REACH[rate_index], (rate, 0, -rate)))
+            first += 3
     return groups
 
 
-GROUPS = row_groups()
-TAPS = 1 + 3 * len(GROUPS)
+TAP_GROUPS = tap_groups()
+TAPS = 22
 SEG_ROWS = TAPS * 32
+WINDOW = 16 * 32
+
+
+def window_of(block):
+    return jnp.where(block < NPIX - REACH[1], 0, jnp.where(block >= REACH[1], 2, 1))
 
 
 def whole_vmem():
@@ -664,9 +677,10 @@
 
 
 def heads_forward_kernel(
-    x_ref, w_ref, q_ref, xall_ref,
+    x_ref, w_ref, proj_ref, q_ref, xall_ref, wpt_ref,
     acc, y_tmp, core_buf, core_in, x_buf, x_in, row_buf, local_sem,
     zr_send, zl_send, z_recv, y_send, y_recv, core_send, core_recv, x_send, x_recv, row_send, row_recv,
+    pj_send, pj_recv,
 ):
     p, c, z, y, x, core = place()
     zcount = NPIX // 2
@@ -676,10 +690,18 @@
     other_core = (p, 2 * x + 1 - core)
     other_x = (p, 2 * (1 - x) + core)
     row_targets = [(lax.rem(p + d, NPIX), c) for d in range(1, NPIX)]
-    greet(row_targets + [other_core, other_x])
+    ch_targets = [(p, lax.rem(c + d, NCH)) for d in range(1, NCH)]
+    greet(row_targets + ch_targets)
 
     own = pltpu.make_async_copy(x_ref, xall_ref.at[p], local_sem.at[0])
     own.start()
+    wpt_ref[c] = proj_ref[...]
+    proj_copies = [
+        remote(proj_ref, wpt_ref.at[c], pj_send.at[d - 1], pj_recv.at[d - 1], ch_targets[d - 1])
+        for d in range(1, NCH)
+    ]
+    for copy in proj_copies:
+        copy.start()
 
     def to_up(source):
         return remote(xall_ref.at[source], xall_ref.at[source], zr_send.at[source // 2], z_recv.at[source // 2], up)
@@ -703,31 +725,30 @@
     def process(src):
         xb = xall_ref[src]
 
+        first_row = pl.multiple_of(window_of(src) * 96, 32)
+
         def one_seg(s, carry):
-            y_tmp[...] = nt_dot(w_ref[s], xb)
-
-            def add_group(dest, branch, first_tap, taps):
+            y_tmp[pl.ds(first_row, WINDOW), :] = nt_dot(w_ref[s, pl.ds(first_row, WINDOW), :], xb)
+
+            def add_group(dest, branch, first_tap, shifts):
                 rows = pl.ds(pl.multiple_of(branch * COLS + s * 32, 32), 32)
                 for r in range(ROWS):
                     lanes = pl.ds(r * WIDTH, WIDTH)
                     total = acc[dest, rows, lanes]
-                    for i, shift in enumerate(taps):
+                    for i, shift in enumerate(shifts):
                         tile = y_tmp[pl.ds((first_tap + i) * 32, 32), lanes]
                         total = total + slide(tile, shift)
                     acc[dest, rows, lanes] = total
 
-            add_group(src, 0, 0, (0,))
-            for g, (rate_index, step) in enumerate(GROUPS):
-                rate = aspp_rates[rate_index]
-                dest = src - step * (rate // ROWS)
-                shifts = (rate, 0, -rate)
+            for branch, first_tap, step, reach, shifts in TAP_GROUPS:
+                dest = src - step * reach
                 if step == 0:
-                    add_group(dest, rate_index + 1, 1 + 3 * g, shifts)
+                    add_group(dest, branch, first_tap, shifts)
                 else:
 
                     @pl.when((dest >= 0) & (dest < NPIX))
                     def _():
-                        add_group(dest, rate_index + 1, 1 + 3 * g, shifts)
+                        add_group(dest, branch, first_tap, shifts)
 
             return carry
 
@@ -837,9 +858,11 @@
         return carry
 
     lax.fori_loop(0, NPIX, settle_more, 0)
-
-
-def heads_forward(block_out, w_seg):
+    for copy in proj_copies:
+        copy.wait()
+
+
+def heads_forward(block_out, w_seg, proj_own):
     dma = pltpu.SemaphoreType.DMA
     zc = NPIX // 2
     return pl.pallas_call(
@@ -847,9 +870,10 @@
         out_shape=(
             jax.ShapeDtypeStruct((4, 3 * HID, WIDTH), BF),
             jax.ShapeDtypeStruct((NPIX, PX, CIN), BF),
+            jax.ShapeDtypeStruct((NCH, 3, HID // NCH, 4 * HID), BF),
         ),
-        in_specs=[whole_vmem()] * 2,
-        out_specs=[whole_vmem()] * 2,
+        in_specs=[whole_vmem()] * 3,
+        out_specs=[whole_vmem()] * 3,
         scratch_shapes=[
             pltpu.VMEM((NPIX, 4 * COLS, PX), F32),
             pltpu.VMEM((SEG_ROWS, PX), F32),
@@ -862,12 +886,13 @@
             dma((zc,)), dma((zc,)), dma((zc,)), dma((zc,)), dma((zc,)),
             dma((NPIX,)), dma((NPIX,)), dma((NPIX,)), dma((NPIX,)),
             dma((NPIX - 1,)), dma((NPIX - 1,)),
+            dma((NCH - 1,)), dma((NCH - 1,)),
         ],
         compiler_params=pltpu.CompilerParams(
             collective_id=1, has_side_effects=True, vmem_limit_bytes=VMEM_LIMIT
         ),
         name="heads_forward",
-    )(block_out, w_seg)
+    )(block_out, w_seg, proj_own)
 
 
 def heads_middle_kernel(
@@ -881,9 +906,10 @@
     row = lax.broadcasted_iota(jnp.int32, (32, WIDTH), 0)
     for t in range(3):
         cols = slice(t * HID, (t + 1) * HID)
+        wpt = wpt_ref[:, t].reshape(HID, 4 * HID)
         zt = pbias_ref[:, t : t + 1] + jnp.zeros((HID, WIDTH), F32)
         for k in range(4):
-            zt = zt + nn_dot(wpt_ref[t, :, k * HID : (k + 1) * HID], hid[k, cols, :])
+            zt = zt + nn_dot(wpt[:, k * HID : (k + 1) * HID], hid[k, cols, :])
         ut = gelu_of(zt).astype(BF)
         out = lax.dot_general(
             wot_ref[t], ut, (((0,), (0,)), ((), ())), preferred_element_type=F32
@@ -913,7 +939,7 @@
             part = hid[k, cols, :]
             dwp_ref[t, k * HID : (k + 1) * HID, :] = nt_dot(part, dz)
             dcat = lax.dot_general(
-                wpt_ref[t, :, k * HID : (k + 1) * HID], dz, (((0,), (0,)), ((), ())),
+                wpt[:, k * HID : (k + 1) * HID], dz, (((0,), (0,)), ((), ())),
                 preferred_element_type=F32,
             )
             before = q_ref[k, cols, :].astype(F32) + bias_ref[cols, k : k + 1]
@@ -950,15 +976,30 @@
     return total
 
 
-def low_task(zplane):
-    return (2 * zplane * COLS) // HID
+def moved_segments():
+    moves = []
+    for pair in range(NPIX // 2):
+        tasks = [[(SEGS * (2 * pair + side) + s) * 32 // HID for s in range(SEGS)] for side in range(2)]
+        low, high = tasks[0][0], tasks[1][-1]
+        if low == high:
+            continue
+        for side, keeps in ((0, low), (1, high)):
+            for s in range(SEGS):
+                if tasks[side][s] != keeps:
+                    moves.append((2 * pair + side, s, 2 * pair + 1 - side))
+    return moves
+
+
+MOVES = moved_segments()
 
 
 def heads_backward_kernel(
     dq_ref, xall_ref, w_ref, dw_ref, gz_ref, square_ref,
-    dq_all, wt, dcol, parts, y_in, z_buf, z_in, gram_own, gram_ch, gram_px, gsum,
+    dq_all, dq_more, w_more, wt, dcol, dcol_more, work, buf, z_out, oi_in, ac_in, grads,
+    gram_own, gram_ch, gram_px, gsum,
     local_sem, row_send, row_recv, x_send, x_recv, ca_send, ca_recv, cb_send, cb_recv,
-    y_send, y_recv, z_send, z_recv, gc_send, gc_recv, gp_send, gp_recv,
+    more_send, more_recv, fan_send, fan_recv, wm_send, wm_recv,
+    y_send, y_recv, oi_send, oi_recv, ac_send, ac_recv, gc_send, gc_recv, gp_send, gp_recv,
 ):
     p, c, z, y, x, core = place()
     zcount = NPIX // 2
@@ -968,6 +1009,7 @@
     pix_targets = [(lax.rem(p + d, NPIX), c) for d in range(1, NPIX)]
     ch_targets = [(p, lax.rem(c + d, NCH)) for d in range(1, NCH)]
     greet(pix_targets + ch_targets)
+    far = 2 * (1 - x) + core
 
     def cols_of(b):
         return pl.ds(pl.multiple_of(COLS * b, 32), COLS)
@@ -975,14 +1017,48 @@
     def row_copy(d):
         b = lax.rem(p + d, NPIX)
         return remote(dq_ref.at[:, cols_of(b), :], dq_all.at[p, c], row_send.at[d - 1], row_recv.at[d - 1], (b, c))
+
+    def more_copy(i, source):
+        giver, s, receiver = MOVES[i]
+        start = giver * COLS + s * 32
+        return remote(
+            dq_ref.at[:, start : start + 32, :], dq_more.at[source, c],
+            more_send.at[i], more_recv.at[source], (receiver, c),
+        )
+
+    def weight_copy(i):
+        return remote(w_ref.at[MOVES[i][1]], w_more, wm_send.at[0], wm_recv.at[0], other_y)
+
+    def fan_copy(i, ch, target):
+        return remote(dq_more.at[:, ch], dq_more.at[:, ch], fan_send.at[i], fan_recv.at[i], target)
+
+    def any_of(flags):
+        total = flags[0]
+        for flag in flags[1:]:
+            total = total | flag
+        return total
+
+    receives = any_of([p == move[2] for move in MOVES])
 
     for d in range(1, NPIX):
         row_copy(d).start()
     own = pltpu.make_async_copy(dq_ref.at[:, cols_of(p), :], dq_all.at[p, c], local_sem.at[0])
     own.start()
-    for s in range(SEGS):
-        wt[s] = jnp.transpose(w_ref[s].astype(F32)).astype(BF)
-    dw_ref[...] = jnp.zeros_like(dw_ref)
+    for i, (giver, s, receiver) in enumerate(MOVES):
+        start = giver * COLS + s * 32
+
+        @pl.when(p == receiver)
+        def _():
+            dq_more[p, c] = dq_ref[:, start : start + 32, :]
+
+        @pl.when(p != receiver)
+        def _():
+            more_copy(i, p).start()
+
+        @pl.when(p == giver)
+        def _():
+            weight_copy(i).start()
+
     own.wait()
 
     def x_copy(d, b, ch):
@@ -994,105 +1070,231 @@
     def cb_copy(d, b, ch):
         return remote(dq_all.at[b, ch], dq_all.at[b, ch], cb_send.at[d], cb_recv.at[d], other_core)
 
-    far = 2 * (1 - x) + core
+    def turn(win, s):
+        value = jnp.transpose(w_ref[s, win * 96 : win * 96 + WINDOW, :].astype(F32)).astype(BF)
+        lanes = slice(s * WINDOW, (s + 1) * WINDOW)
+        givers = [move[0] for move in MOVES if move[1] == s]
+        if givers:
+            given = any_of([p == giver for giver in givers])
+            wt[win, :, lanes] = jnp.where(given, jnp.zeros_like(value), value)
+        else:
+            wt[win, :, lanes] = value
+
+    pieces = [(win, s) for win in range(3) for s in range(SEGS)]
     for d in range(NPIX):
         b = lax.rem(p + NPIX - d, NPIX)
         if d > 0:
             row_copy(d).wait_recv()
         x_copy(d, b, c).start()
         ca_copy(d, b, c).start()
+        if d > 0:
+            turn(*pieces[d - 1])
+    for piece in pieces[NPIX - 1 :]:
+        turn(*piece)
+
+    @pl.when(receives)
+    def _():
+        for source in range(NPIX):
+
+            @pl.when(p != source)
+            def _():
+                more_copy(0, source).wait_recv()
+
+        fan_copy(0, c, other_x).start()
+        fan_copy(1, c, other_core).start()
+
     for d in range(NPIX):
         b = lax.rem(p + NPIX - d, NPIX)
         x_copy(d, b, far).wait_recv()
         cb_copy(d, b, far).start()
+    dw_ref[...] = jnp.zeros_like(dw_ref)
+
+    @pl.when(receives)
+    def _():
+        weight_copy(0).wait_recv()
+        for win in range(3):
+            wt[win, :, SEGS * WINDOW :] = jnp.transpose(
+                w_more[win * 96 : win * 96 + WINDOW, :].astype(F32)
+            ).astype(BF)
+        fan_copy(0, far, other_x).wait_recv()
+        fan_copy(2, far, other_core).start()
+
     for d in range(NPIX):
         b = lax.rem(p + NPIX - d, NPIX)
         ca_copy(d, b, 2 * x + 1 - core).wait_recv()
         cb_copy(d, b, 2 * (1 - x) + 1 - core).wait_recv()
 
-    def task_of(pixel_device, s):
-        return (SEGS * pixel_device + s) // (HID // 32)
-
-    in_low = [task_of(p, s) == low_task(z) for s in range(SEGS)]
-    other_p = 2 * z + 1 - y
-
-    def has_low(device):
-        return task_of(device, 0) == low_task(z)
-
-    def has_high(device):
-        return task_of(device, SEGS - 1) != low_task(z)
-
-    def y_copy(zz, slot):
-        return remote(
-            parts.at[2 * zz + 1 - y, slot], y_in.at[zz, slot],
-            y_send.at[zz, slot], y_recv.at[zz, slot], other_y,
-        )
-
-    def block_step(i, carry):
-        zz = lax.rem(i, zcount)
-        b = jnp.where(i < zcount, 2 * zz + 1 - y, 2 * zz + y)
-
-        def fill(source, branch, first_tap, shifts):
+    @pl.when(receives)
+    def _():
+        fan_copy(1, 2 * x + 1 - core, other_core).wait_recv()
+        fan_copy(2, 2 * (1 - x) + 1 - core, other_core).wait_recv()
+
+    def one_block(b):
+        win = window_of(b)
+
+        def each_group(visit, clear):
+            for branch, first_tap, step, reach, shifts in TAP_GROUPS:
+                first_row = first_tap * 32 - win * 96
+                source = b - step * reach
+                if step == 0:
+                    visit(source, branch, first_row, shifts)
+                else:
+                    in_window = win <= 1 if step < 0 else win >= 1
+                    if reach == REACH[1]:
+                        in_window = win == 1 + step
+                    inside = (source >= 0) & (source < NPIX)
+
+                    @pl.when(inside)
+                    def _():
+                        visit(source, branch, first_row, shifts)
+
+                    @pl.when(in_window & jnp.logical_not(inside))
+                    def _():
+                        clear(first_row)
+
+        def visit(source, branch, first_row, shifts):
             for r in range(ROWS):
                 lanes = pl.ds(r * WIDTH, WIDTH)
                 tile = dq_all[source, r, branch].astype(F32)
                 for t, shift in enumerate(shifts):
-                    moved = slide(tile, shift).astype(BF)
+                    moved = slide(tile, -shift).astype(BF)
                     for s in range(SEGS):
-                        dcol[s, pl.ds((first_tap + t) * 32, 32), lanes] = moved[s * 32 : (s + 1) * 32]
-
-        fill(b, 0, 0, (0,))
-        for g, (rate_index, step) in enumerate(GROUPS):
-            rate = aspp_rates[rate_index]
-            source = b - step * (rate // ROWS)
-            shifts = (-rate, 0, rate)
-            if step == 0:
-                fill(source, rate_index + 1, 1 + 3 * g, shifts)
-            else:
-                inside = (source >= 0) & (source < NPIX)
-
-                @pl.when(inside)
-                def _():
-                    fill(source, rate_index + 1, 1 + 3 * g, shifts)
-
-                @pl.when(jnp.logical_not(inside))
-                def _():
-                    for s in range(SEGS):
-                        dcol[s, pl.ds((1 + 3 * g) * 32, 96), :] = jnp.zeros((96, PX), BF)
-
-        def product_rows(m, inner):
-            rows = pl.ds(pl.multiple_of(m * 128, 128), 128)
-            low = jnp.zeros((128, PX), F32)
-            high = jnp.zeros((128, PX), F32)
+                        rows = pl.ds(pl.multiple_of(s * WINDOW + first_row + t * 32, 32), 32)
+                        dcol[b, rows, lanes] = moved[s * 32 : (s + 1) * 32]
+
+        def clear(first_row):
             for s in range(SEGS):
-                value = nn_dot(wt[s, rows, :], dcol[s])
-                low = low + jnp.where(in_low[s], value, 0.0)
-                high = high + jnp.where(in_low[s], 0.0, value)
-            parts[b, 0, rows, :] = low.astype(BF)
-            parts[b, 1, rows, :] = high.astype(BF)
-            return inner
-
-        lax.fori_loop(0, CIN // 128, product_rows, 0)
-
-        @pl.when((i < zcount) & has_low(p))
+                rows = pl.ds(pl.multiple_of(s * WINDOW + first_row, 32), 96)
+                dcol[b, rows, :] = jnp.zeros((96, PX), BF)
+
+        def visit_more(source, branch, first_row, shifts):
+            for r in range(ROWS):
+                lanes = pl.ds(r * WIDTH, WIDTH)
+                tile = dq_more[source, r, branch].astype(F32)
+                for t, shift in enumerate(shifts):
+                    rows = pl.ds(pl.multiple_of(first_row + t * 32, 32), 32)
+                    dcol_more[rows, lanes] = slide(tile, -shift).astype(BF)
+
+        def clear_more(first_row):
+            dcol_more[pl.ds(pl.multiple_of(first_row, 32), 96), :] = jnp.zeros((96, PX), BF)
+
+        each_group(visit, clear)
+        work[...] = nn_dot(wt[win, :, : SEGS * WINDOW], dcol[b])
+
+        @pl.when(receives)
         def _():
-            y_copy(zz, 0).start()
-
-        @pl.when((i < zcount) & has_high(p))
+            each_group(visit_more, clear_more)
+            work[...] += nn_dot(wt[win, :, SEGS * WINDOW :], dcol_more[...])
+
+        buf[b] = work[...].astype(BF)
+
+    mirrored = z >= 2
+    outer = (z == 0) | (z == zcount - 1)
+    inner = jnp.logical_not(outer)
+    has_near = y == z - 1
+
+    def true_z(e):
+        return jnp.where(mirrored, zcount - 1 - e, e)
+
+    def block_at(e):
+        return 2 * true_z(e) + y
+
+    def arrived_at(e):
+        return NPIX + true_z(e)
+
+    def near_at(e):
+        return jnp.where(has_near, block_at(e), arrived_at(e))
+
+    def mid_at(e):
+        return jnp.where(has_near, arrived_at(e), block_at(e))
+
+    def y_copy(zz):
+        return remote(buf.at[2 * zz + 1 - y], buf.at[NPIX + zz], y_send.at[zz], y_recv.at[zz], other_y)
+
+    oi_z = jnp.where(z == 0, 1, jnp.where(z == 1, 0, jnp.where(z == 2, 3, 2)))
+
+    def oi_copy(i, source):
+        return remote(source, oi_in.at[i], oi_send.at[i], oi_recv.at[i], (2 * oi_z + y, c))
+
+    def ac_copy(i, source):
+        return remote(source, ac_in.at[i], ac_send.at[i], ac_recv.at[i], (2 * (zcount - 1 - z) + y, c))
+
+    def order(i):
+        last = jnp.where(outer, zcount - 1 - i, i - 2)
+        return jnp.where(i < 2, zcount - 1 - i, last)
+
+    def sum_of(first, second):
+        return (first.astype(F32) + second.astype(F32)).astype(BF)
+
+    def block_pair(i, carry):
+        zz = true_z(order(i))
+
+        def either(j, inner_carry):
+            one_block(2 * zz + jnp.where(j == 0, 1 - y, y))
+
+            @pl.when(j == 0)
+            def _():
+                y_copy(zz).start()
+
+            return inner_carry
+
+        lax.fori_loop(0, 2, either, 0)
+
+        @pl.when(i > 0)
         def _():
-            y_copy(zz, 1).start()
-
-        def weight_rows(m, inner):
-            s = m // 2
-            rows = pl.ds(pl.multiple_of(lax.rem(m, 2) * (SEG_ROWS // 2), 32), SEG_ROWS // 2)
-            dw_ref[s, rows, :] += nn_dot(dcol[s, rows, :], xall_ref[b])
-            return inner
-
-        lax.fori_loop(0, 2 * SEGS, weight_rows, 0)
+            y_copy(true_z(order(i - 1))).wait_recv()
+
+        for step in range(1, zcount):
+
+            @pl.when((i == step) & outer)
+            def _():
+                e = zcount - step
+                z_out[step - 1] = sum_of(buf[block_at(e)], buf[arrived_at(e)])
+                oi_copy(step - 1, z_out.at[step - 1]).start()
+
+        @pl.when((i == 1) & inner)
+        def _():
+            ac_copy(0, buf.at[mid_at(3)]).start()
+
+        @pl.when((i == 2) & inner)
+        def _():
+            ac_copy(1, buf.at[mid_at(2)]).start()
+            oi_copy(0, z_out.at[0]).wait_recv()
+            z_out[0] = sum_of(oi_in[0], buf[near_at(3)])
+            ac_copy(2, z_out.at[0]).start()
+
+        @pl.when((i == 3) & inner)
+        def _():
+            oi_copy(0, buf.at[near_at(0)]).start()
+            oi_copy(1, z_out.at[0]).wait_recv()
+            z_out[1] = sum_of(oi_in[1], buf[near_at(2)])
+            ac_copy(3, z_out.at[1]).start()
+
         return carry
 
-    lax.fori_loop(0, NPIX, block_step, 0)
-
+    lax.fori_loop(0, zcount, block_pair, 0)
+
+    def weight_block(b, carry):
+        first_row = pl.multiple_of(window_of(b) * 96, 32)
+
+        def one_seg(s, inner_carry):
+            rows = pl.ds(pl.multiple_of(s * WINDOW, WINDOW), WINDOW)
+            dw_ref[s, pl.ds(first_row, WINDOW), :] += nn_dot(dcol[b, rows, :], xall_ref[b])
+            return inner_carry
+
+        return lax.fori_loop(0, SEGS, one_seg, carry)
+
+    lax.fori_loop(0, NPIX // 2, weight_block, 0)
+
+    @pl.when(inner)
+    def _():
+        ac_copy(0, z_out.at[0]).wait_recv()
+        z_out[2] = sum_of(ac_in[0], buf[mid_at(0)])
+        oi_copy(1, z_out.at[2]).start()
+        ac_copy(2, z_out.at[0]).wait_recv()
+        oi_copy(2, ac_in.at[2]).start()
+
+    lax.fori_loop(NPIX // 2, NPIX, weight_block, 0)
     square_ref[...] = jnp.zeros_like(square_ref)
 
     def square_rows(m, carry):
@@ -1101,64 +1303,39 @@
         square_ref[...] += fold(part * part)
         return carry
 
-    def z_copy(d, slot):
-        zz = lax.rem(z + d, zcount)
-        return remote(
-            z_buf.at[zz, slot], z_in.at[z, slot],
-            z_send.at[d - 1, slot], z_recv.at[d - 1, slot], (2 * zz + y, c),
+    lax.fori_loop(0, SEGS * TAPS, square_rows, 0)
+
+    near_task = jnp.where(mirrored, 2, 0)
+    far_task = jnp.where(mirrored, 0, 2)
+    y_copy(true_z(order(zcount - 1))).wait_recv()
+
+    @pl.when(outer)
+    def _():
+        for i in range(3):
+            oi_copy(i, z_out.at[0]).wait_recv()
+        grads[near_task] = (
+            buf[block_at(0)].astype(F32) + buf[arrived_at(0)].astype(F32) + oi_in[0].astype(F32)
         )
-
-    pair_high = (z == 1) | (z == 2)
-    for d in (1, 2, 3, 0):
-        zz = lax.rem(z + d, zcount)
-        for slot in range(2):
-            theirs = has_low(other_p) if slot == 0 else has_high(other_p)
-            there = pair_high if slot else (z >= 0)
-
-            @pl.when(theirs)
-            def _():
-                y_copy(zz, slot).wait_recv()
-                z_buf[zz, slot] = (
-                    parts[2 * zz + y, slot].astype(F32) + y_in[zz, slot].astype(F32)
-                ).astype(BF)
-
-            @pl.when(jnp.logical_not(theirs))
-            def _():
-                z_buf[zz, slot] = parts[2 * zz + y, slot]
-
-            if d > 0:
-
-                @pl.when(there)
-                def _():
-                    z_copy(d, slot).start()
-
-    lax.fori_loop(0, SEGS * TAPS, square_rows, 0)
-    for slot in range(2):
-        z_in[z, slot] = z_buf[z, slot]
-    for d in range(1, zcount):
-        source = lax.rem(z + zcount - d, zcount)
-        for slot in range(2):
-            has = (source == 1) | (source == 2) if slot else (source >= 0)
-
-            @pl.when(has)
-            def _():
-                z_copy(d, slot).wait_recv()
-
-    def task_grads(rows):
-        first = z_in[0, 0, rows, :].astype(F32) + z_in[1, 0, rows, :].astype(F32)
-        second = z_in[1, 1, rows, :].astype(F32) + z_in[2, 0, rows, :].astype(F32)
-        third = z_in[2, 1, rows, :].astype(F32) + z_in[3, 0, rows, :].astype(F32)
-        return first, second, third
+        grads[1] = oi_in[1].astype(F32)
+        grads[far_task] = oi_in[2].astype(F32)
+
+    @pl.when(inner)
+    def _():
+        oi_copy(2, z_out.at[0]).wait_recv()
+        ac_copy(1, z_out.at[0]).wait_recv()
+        ac_copy(3, z_out.at[0]).wait_recv()
+        grads[near_task] = oi_in[2].astype(F32) + buf[near_at(1)].astype(F32)
+        grads[1] = buf[mid_at(1)].astype(F32) + ac_in[1].astype(F32)
+        grads[far_task] = ac_in[3].astype(F32)
 
     pairs = ((0, 0), (0, 1), (0, 2), (1, 1), (1, 2), (2, 2))
     gram_own[...] = jnp.zeros_like(gram_own)
 
     def gram_rows(m, carry):
         rows = pl.ds(pl.multiple_of(m * 32, 32), 32)
-        grads = task_grads(rows)
+        tasks = [grads[t, rows, :] for t in range(3)]
         for i, (a, b) in enumerate(pairs):
-            product = grads[a] * grads[b]
-            gram_own[i] += fold(product)
+            gram_own[i] += fold(tasks[a] * tasks[b])
         return carry
 
     lax.fori_loop(0, CIN // 32, gram_rows, 0)
@@ -1208,8 +1385,8 @@
     alpha_zero = 1.0 - alpha_one - alpha_two
 
     for m in range(CIN // 128):
-        first, second, third = task_grads(pl.ds(m * 128, 128))
-        mixed = alpha_zero * first + alpha_one * second + alpha_two * third
+        rows = pl.ds(m * 128, 128)
+        mixed = alpha_zero * grads[0, rows, :] + alpha_one * grads[1, rows, :] + alpha_two * grads[2, rows, :]
         gz_ref[:, m * 128 : (m + 1) * 128] = jnp.transpose(mixed)
 
     for d in range(1, NPIX):
@@ -1219,22 +1396,31 @@
         x_copy(d, b, c).wait_send()
         ca_copy(d, b, c).wait_send()
         cb_copy(d, b, far).wait_send()
-    for zz in range(zcount):
-
-        @pl.when(has_low(p))
+    for i, (giver, s, receiver) in enumerate(MOVES):
+
+        @pl.when(p != receiver)
         def _():
-            y_copy(zz, 0).wait_send()
-
-        @pl.when(has_high(p))
+            more_copy(i, p).wait_send()
+
+        @pl.when(p == giver)
         def _():
-            y_copy(zz, 1).wait_send()
-
-    for d in range(1, zcount):
-        z_copy(d, 0).wait_send()
-
-        @pl.when(pair_high)
-        def _():
-            z_copy(d, 1).wait_send()
+            weight_copy(i).wait_send()
+
+    @pl.when(receives)
+    def _():
+        fan_copy(0, c, other_x).wait_send()
+        fan_copy(1, c, other_core).wait_send()
+        fan_copy(2, far, other_core).wait_send()
+
+    for i in range(zcount):
+        y_copy(i).wait_send()
+    for i in range(3):
+        oi_copy(i, z_out.at[0]).wait_send()
+
+    @pl.when(inner)
+    def _():
+        for i in range(4):
+            ac_copy(i, z_out.at[0]).wait_send()
 
 
 def heads_backward(dq, xall, w_seg):
@@ -1251,12 +1437,17 @@
         out_specs=[whole_vmem()] * 3,
         scratch_shapes=[
             pltpu.VMEM((NPIX, NCH, 4, COLS, WIDTH), BF),
-            pltpu.VMEM((SEGS, CIN, SEG_ROWS), BF),
-            pltpu.VMEM((SEGS, SEG_ROWS, PX), BF),
-            pltpu.VMEM((NPIX, 2, CIN, PX), BF),
-            pltpu.VMEM((zc, 2, CIN, PX), BF),
-            pltpu.VMEM((zc, 2, CIN, PX), BF),
-            pltpu.VMEM((zc, 2, CIN, PX), BF),
+            pltpu.VMEM((NPIX, NCH, 4, 32, WIDTH), BF),
+            pltpu.VMEM((SEG_ROWS, CIN), BF),
+            pltpu.VMEM((3, CIN, (SEGS + 1) * WINDOW), BF),
+            pltpu.VMEM((NPIX, SEGS * WINDOW, PX), BF),
+            pltpu.VMEM((WINDOW, PX), BF),
+            pltpu.VMEM((CIN, PX), F32),
+            pltpu.VMEM((NPIX + zc, CIN, PX), BF),
+            pltpu.VMEM((3, CIN, PX), BF),
+            pltpu.VMEM((3, CIN, PX), BF),
+            pltpu.VMEM((4, CIN, PX), BF),
+            pltpu.VMEM((3, CIN, PX), F32),
             pltpu.VMEM((6, 8, 128), F32),
             pltpu.VMEM((NCH - 1, 6, 8, 128), F32),
             pltpu.VMEM((NPIX - 1, 6, 8, 128), F32),
@@ -1264,8 +1455,8 @@
             dma((1,)),
             dma((NPIX - 1,)), dma((NPIX - 1,)),
             dma((NPIX,)), dma((NPIX,)), dma((NPIX,)), dma((NPIX,)), dma((NPIX,)), dma((NPIX,)),
-            dma((zc, 2)), dma((zc, 2)),
-            dma((zc - 1, 2)), dma((zc - 1, 2)),
+            dma((len(MOVES),)), dma((NPIX,)), dma((3,)), dma((3,)), dma((1,)), dma((1,)),
+            dma((zc,)), dma((zc,)), dma((3,)), dma((3,)), dma((4,)), dma((4,)),
             dma((NCH - 1,)), dma((NCH - 1,)),
             dma((NPIX - 1,)), dma((NPIX - 1,)),
         ],
@@ -1278,9 +1469,12 @@
 
 def tap_weights(head_weight, head_rates):
     rates = head_rates.astype(BF)
-    pieces = [jnp.transpose(head_weight.astype(BF))[None]]
-    for rate_index, step in GROUPS:
-        pieces.append(rates[rate_index, 3 * (step + 1) : 3 * (step + 2)])
+    pieces = []
+    for branch, first, step, reach, shifts in TAP_GROUPS:
+        if branch == 0:
+            pieces.append(jnp.transpose(head_weight.astype(BF))[None])
+        else:
+            pieces.append(rates[branch - 1, 3 * (step + 1) : 3 * (step + 2)])
     taps = jnp.concatenate(pieces, axis=0)
     taps = taps.reshape(TAPS, SEGS, 32, CIN).transpose(1, 0, 2, 3)
     return taps.reshape(SEGS, SEG_ROWS, CIN)
@@ -1288,15 +1482,13 @@
 
 def tap_grads(dw):
     taps = dw.reshape(SEGS, TAPS, 32, CIN).transpose(1, 0, 2, 3).reshape(TAPS, COLS, CIN)
-    head = jnp.transpose(taps[0])
+    at = {(group[0], group[2]): group[1] for group in TAP_GROUPS}
+    head = jnp.transpose(taps[at[(0, 0)]])
     rates = []
     for rate_index in range(3):
         for step in (-1, 0, 1):
-            if (rate_index, step) in GROUPS:
-                g = GROUPS.index((rate_index, step))
-                rates.append(taps[1 + 3 * g : 4 + 3 * g])
-            else:
-                rates.append(jnp.zeros((3, COLS, CIN), F32))
+            first = at.get((rate_index + 1, step))
+            rates.append(jnp.zeros((3, COLS, CIN), F32) if first is None else taps[first : first + 3])
     return head, jnp.stack(rates).reshape(3, 9, COLS, CIN)
 
 
@@ -1573,7 +1765,7 @@
             shape((PX, M), BF),
             shape((8, MID), F32),
             shape((8, CIN), F32),
-            shape((3, HID, 4 * HID), BF),
+            shape((3, HID // NCH, 4 * HID), BF),
         ),
         in_specs=[whole_vmem()] * 6,
         out_specs=[whole_vmem()] * 10,
@@ -1997,8 +2189,11 @@
         + [jnp.zeros((MID,), F32)] * 3
     )
     wide = jnp.stack([owned(gains, 2 * M, CIN), owned(shifts, 2 * M, CIN)] + [jnp.zeros((CIN,), F32)] * 6)
-    shared, hat_one, hat_two, hat_three, w_all, first, second, stats, stats_wide, proj_t = block_forward(
-        flat_in, mask_column, w_shard, jnp.transpose(head_proj, (0, 2, 1)).astype(BF), narrow, wide
+    proj_shard_t = jnp.transpose(
+        lax.dynamic_slice_in_dim(head_proj, block_id * (HID // NCH), HID // NCH, axis=2), (0, 2, 1)
+    ).astype(BF)
+    shared, hat_one, hat_two, hat_three, w_all, first, second, stats, stats_wide, proj_own = block_forward(
+        flat_in, mask_column, w_shard, proj_shard_t, narrow, wide
     )
     branch_bias, proj_bias, sem_w, depth_w, normal_w, sem_b, depth_b, normal_b = unpack_small(
         head_small
@@ -2009,7 +2204,7 @@
     out_bias = jnp.stack(
         [jnp.pad(bias, (0, 32 - bias.shape[0])) for bias in (sem_b, depth_b, normal_b)], axis=1
     )
-    q_rows, shared_all = heads_forward(shared, w_seg)
+    q_rows, shared_all, proj_t = heads_forward(shared, w_seg, proj_own)
     targets = jnp.concatenate([own_row(depth_target, 0), own_row(normal_target, 1)[:, 0]], axis=0)
     pre_grad, proj_part, out_grad, bias_rows, out_bias_rows = heads_middle(
         q_rows,

time: 590 us -> 505 us (0.86)
  Pallas kernels: 515 us -> 431 us
    pallas_call x1, Pallas kernels: 192 us -> 131 us  [heads_backward(): pl.pallas_call(heads_backward_kernel, out_shape=(jax.ShapeDtypeStruct((SE...]
    pallas_call x1, Pallas kernels: 101 us -> 78 us  [block_forward(): pl.pallas_call(block_forward_kernel, out_shape=(shape((PX, CIN), BF), sha...]
where the time goes in v3:
time: 505 us; the launch traced here: 504 us
  Pallas kernels  431 us (85%)
  other arithmetic  37.9 us (8%)
  local copies, waits for them, and re-layouts  33.4 us (7%)
    pallas_call x1, Pallas kernels, heads_backward(): pl.pallas_call(heads_backward_kernel, out_shape=(jax.ShapeDtypeStruct((SE...  131 us
    pallas_call x1, Pallas kernels, block_backward(): pl.pallas_call(block_backward_kernel, out_shape=(shape((PX, CIN), F32), s...  117 us
    pallas_call x1, Pallas kernels, heads_forward(): pl.pallas_call(heads_forward_kernel, out_shape=(jax.ShapeDtypeStruct((4,...  98.4 us
    pallas_call x1, Pallas kernels, block_forward(): pl.pallas_call(block_forward_kernel, out_shape=(shape((PX, CIN), BF), sha...  78 us
    convert_element_type x1, other arithmetic, per_device_rows(): rates_new.astype(jnp.bfloat16)  10.3 us

profile of v3, /device:TPU:0, one launch (start us, length us, event | category | flops | bytes accessed | tf_op | source)
XLA Modules:
  0.0 503.5 jit_solution(5608290429356923297)
XLA Ops:
  3.2 1.0 copy_bitcast_fusion.1
  5.8 1.0 constant_dynamic-slice_fusion.10
  10.7 78.0 %block_forward.1 = (bf16[512,512]{1,0:T(8,128)(2,1)}, f32[512,128]{1,0:T(8,128)}, f32[512,128]{1,0:T(8,128)}, f32[512,512]{1,0:T(8,128)}, bf16[8,64,2176]{2,1,0:...) custom-call(bf16[512,512]{1,0:T(8,128)(2,1)} %bitcast.156, ...), custom_call_target="tpu_custom_call" | custom-call | tf_op jit(solution)/shard_map/block_forward/pallas_call | solution.py:1756
  88.6 2.9 convert_element_type.76
  92.1 1.3 copy-done.2
  93.4 98.4 %heads_forward.1 = (bf16[4,768,128]{2,1,0:T(8,128)(2,1)}, bf16[8,512,512]{2,1,0:T(8,128)(2,1)}, bf16[4,3,64,1024]{3,2,1,0:T(8,128)(2,1)}) custom-call(bf16[512,512]{1,0:T(8,128)(2,1)} %get-tuple-element.62.x_ref, bf16[3,704,512]{2,1,0:T(8,128)(2,1)} %bitcast.144, bf16[3,64,1024]{2,1,0:T(8,128)(2,1)} %get-tuple-element.63.proj_ref), custom_call_target="tpu_custom_call" | custom-call | tf_op jit(solution)/shard_map/heads_forward/pallas_call | solution.py:868
  197.0 1.2 constant_dynamic-slice_fusion.3.label_ref
  202.1 7.0 %heads_middle.1 = (bf16[4,768,128]{2,1,0:T(8,128)(2,1)}, f32[3,1024,256]{2,1,0:T(8,128)}, f32[3,32,256]{2,1,0:T(8,128)}, f32[5,8,768]{2,1,0:T(8,128)}, f32[3,8,32]{2,1,0:T(8,128)}) custom-call(bf16[4,768,128]{2,1,0:T(8,128)(2,1)} %get-tuple-element.64.q_ref, f32[768,4]{1,0:T(8,128)} %bitcast.159, f32[256,3]{1,0:T(8,128)} %bitcast.168, ...), custom_call_target="tpu_custom_call" | custom-call | tf_op jit(solution)/shard_map/heads_middle/pallas_call | solution.py:952
  209.1 130.9 %heads_backward.1 = (f32[3,704,512]{2,1,0:T(8,128)}, f32[512,512]{1,0:T(8,128)}, f32[8,128]{1,0:T(8,128)}) custom-call(bf16[4,768,128]{2,1,0:T(8,128)(2,1)} %get-tuple-element.67.dq_ref, bf16[8,512,512]{2,1,0:T(8,128)(2,1)} %get-tuple-element.68.xall_ref, bf16[3,704,512]{2,1,0:T(8,128)(2,1)} %bitcast.145), custom_call_target="tpu_custom_call" | custom-call | tf_op jit(solution)/shard_map/heads_backward/pallas_call | solution.py:1429
  345.2 1.2 slice.177
  348.5 116.6 %block_backward.1 = (f32[512,512]{1,0:T(8,128)}, f32[64,2176]{1,0:T(8,128)}, f32[3,128,256]{2,1,0:T(8,128)}, f32[80,128]{1,0:T(8,128)}, f32[4,8,128]{2,1,0:T(8,1...) custom-call(f32[512,512]{1,0:T(8,128)} %get-tuple-element.69.gz_ref, bf16[512,512]{1,0:T(8,128)(2,1)} %bitcast.157, ...), custom_call_target="tpu_custom_call" | custom-call | tf_op jit(solution)/shard_map/block_backward/pallas_call | solution.py:2072
  465.2 1.3 fusion.37
  466.4 2.4 fusion.29
  468.8 2.7 fusion.26
  471.6 2.4 fusion.24
  474.0 2.7 copy.210
  479.6 1.8 broadcast_multiply_fusion
  481.4 1.0 slice-done
  482.7 10.3 %fusion.18 = (bf16[3,9,96,512]{3,2,1,0:T(8,128)(2,1)}, f32[3,9,96,512]{3,2,1,0:T(8,128)}, f32[3,9,96,512]{3,2,1,0:T(8,128)}, f32[3,9,96,512]{3,2,1,0:T(8,128)}) fusion(f32[3,9,96,512]{3,2,1,0:T(8,128)S(1)} %bitcast.140, f32[3,9,96,512]{3,2,1,0:T(8,128)S(1)} %bitcast.147, f32[3,9,96,512]{3,2,1,0:T(8,128)} %param.50, f32[3,9,96,512]{3,2,1,0:T(8,128)S(1)} %bitcast.141), kind=kLoop, calls=%fused_computation.103 | loop fusion | flops 21233664 | bytes 39813120 | tf_op jit(solution)/shard_map/convert_element_type | solution.py:2294
  493.0 3.4 fusion.16
  497.4 1.4 multiply_subtract_fusion.7
  498.8 1.3 multiply_subtract_fusion.6
  500.7 1.9 copy.229
  502.5 1.0 copy.230
  (148 shorter events, 29.0 us)
Async XLA Ops:
  0.7 197.5 %copy-start = (f32[3,4,128]{2,1,0:T(4,128)S(1)}, f32[3,4,128]{2,1,0:T(4,128)}, u32[]{:S(2)}) copy-start(f32[3,4,128]{2,1,0:T(4,128)} %param.34) | copy-start | bytes 18436
  91.6 100.2 %slice-start.4 = ((f32[9751]{0:T(1024)}), f32[3072]{0:T(1024)S(1)}, s32[]{:S(2)}) async-start(f32[9751]{0:T(1024)} %param.57), calls=%async_computation.4 | async-start | bytes 24576 | tf_op jit(solution)/shard_map/slice | solution.py:95
  91.6 101.1 %slice-start.5 = ((f32[9751]{0:T(1024)}), f32[768]{0:T(1024)S(1)}, s32[]{:S(2)}) async-start(f32[9751]{0:T(1024)} %param.57), calls=%async_computation.5 | async-start | bytes 8192 | tf_op jit(solution)/shard_map/slice | solution.py:95
  91.6 101.9 %copy-start.10 = (f32[9751]{0:T(1024)S(1)}, f32[9751]{0:T(1024)}, u32[]{:S(2)}) copy-start(f32[9751]{0:T(1024)} %param.57) | copy-start | bytes 117016
  342.6 123.9 %copy-start.6 = (f32[512,64]{0,1:T(8,128)S(1)}, f32[512,64]{0,1:T(8,128)}, u32[]{:S(2)}) copy-start(f32[512,64]{0,1:T(8,128)} %param.36) | copy-start | bytes 393220
  342.6 123.9 %copy-start.13 = (f32[512,64]{0,1:T(8,128)S(1)}, f32[512,64]{0,1:T(8,128)}, u32[]{:S(2)}) copy-start(f32[512,64]{0,1:T(8,128)} %param.37) | copy-start | bytes 393220
  342.6 123.9 %copy-start.14 = (f32[512,64]{0,1:T(8,128)S(1)}, f32[512,64]{0,1:T(8,128)}, u32[]{:S(2)}) copy-start(f32[512,64]{0,1:T(8,128)} %param.38) | copy-start | bytes 393220
  348.5 120.4 %copy-start.3 = (f32[9,64,128]{2,1,0:T(8,128)S(1)}, f32[9,64,128]{2,1,0:T(8,128)}, u32[]{:S(2)}) copy-start(f32[9,64,128]{2,1,0:T(8,128)} %param.39) | copy-start | bytes 884740
  348.5 120.4 %copy-start.8 = (f32[9,64,128]{2,1,0:T(8,128)S(1)}, f32[9,64,128]{2,1,0:T(8,128)}, u32[]{:S(2)}) copy-start(f32[9,64,128]{2,1,0:T(8,128)} %param.40) | copy-start | bytes 884740
  348.5 120.4 %copy-start.9 = (f32[9,64,128]{2,1,0:T(8,128)S(1)}, f32[9,64,128]{2,1,0:T(8,128)}, u32[]{:S(2)}) copy-start(f32[9,64,128]{2,1,0:T(8,128)} %param.41) | copy-start | bytes 884740
  348.5 123.1 %copy-start.7 = (f32[64,512]{1,0:T(8,128)S(1)}, f32[64,512]{1,0:T(8,128)}, u32[]{:S(2)}) copy-start(f32[64,512]{1,0:T(8,128)} %param.42) | copy-start | bytes 393220
  348.5 123.1 %copy-start.15 = (f32[64,512]{1,0:T(8,128)S(1)}, f32[64,512]{1,0:T(8,128)}, u32[]{:S(2)}) copy-start(f32[64,512]{1,0:T(8,128)} %param.43) | copy-start | bytes 393220
  348.5 123.1 %copy-start.16 = (f32[64,512]{1,0:T(8,128)S(1)}, f32[64,512]{1,0:T(8,128)}, u32[]{:S(2)}) copy-start(f32[64,512]{1,0:T(8,128)} %param.44) | copy-start | bytes 393220
  471.6 5.9 %copy-start.11 = (f32[512,96]{0,1:T(8,128)S(1)}, f32[512,96]{0,1:T(8,128)}, u32[]{:S(2)}) copy-start(f32[512,96]{0,1:T(8,128)} %param.46) | copy-start | bytes 589828
  471.6 5.9 %copy-start.12 = (f32[512,96]{0,1:T(8,128)S(1)}, f32[512,96]{0,1:T(8,128)}, u32[]{:S(2)}) copy-start(f32[512,96]{0,1:T(8,128)} %param.47) | copy-start | bytes 589828
  482.7 14.6 %copy-start.23 = (f32[4,8,128]{2,1,0:T(8,128)S(1)}, f32[4,8,128]{2,1,0:T(8,128)}, u32[]{:S(2)}) copy-start(f32[4,8,128]{2,1,0:T(8,128)} %get-tuple-element.87) | copy-start | bytes 49156
  482.7 14.7 %copy-start.17 = (f32[2,3072]{1,0:T(2,128)S(1)}, f32[2,3072]{1,0:T(2,128)}, u32[]{:S(2)}) copy-start(f32[2,3072]{1,0:T(2,128)} %param.54) | copy-start | bytes 73732
  482.7 14.7 %copy-start.21 = (f32[2,3072]{1,0:T(2,128)S(1)}, f32[2,3072]{1,0:T(2,128)}, u32[]{:S(2)}) copy-start(f32[2,3072]{1,0:T(2,128)} %param.55) | copy-start | bytes 73732
  482.7 14.7 %copy-start.22 = (f32[2,3072]{1,0:T(2,128)S(1)}, f32[2,3072]{1,0:T(2,128)}, u32[]{:S(2)}) copy-start(f32[2,3072]{1,0:T(2,128)} %param.56) | copy-start | bytes 73732
  482.7 16.1 %copy-start.18 = (f32[9751]{0:T(1024)S(1)}, f32[9751]{0:T(1024)}, u32[]{:S(2)}) copy-start(f32[9751]{0:T(1024)} %param.58) | copy-start | bytes 117016
  482.7 16.1 %copy-start.19 = (f32[9751]{0:T(1024)S(1)}, f32[9751]{0:T(1024)}, u32[]{:S(2)}) copy-start(f32[9751]{0:T(1024)} %param.59) | copy-start | bytes 117016
  482.7 16.1 %copy-start.20 = (f32[80,128]{1,0:T(8,128)S(1)}, f32[80,128]{1,0:T(8,128)}, u32[]{:S(2)}) copy-start(f32[80,128]{1,0:T(8,128)} %get-tuple-element.89) | copy-start | bytes 122884
  482.7 20.8 %copy-start.1 = (f32[3,4,128]{2,1,0:T(4,128)S(1)}, f32[3,4,128]{2,1,0:T(4,128)}, u32[]{:S(2)}) copy-start(f32[3,4,128]{2,1,0:T(4,128)} %param.34) | copy-start | bytes 18436
  493.0 9.5 %copy-start.4 = (f32[512,512]{1,0:T(8,128)S(1)}, f32[512,512]{1,0:T(8,128)}, u32[]{:S(2)}) copy-start(f32[512,512]{1,0:T(8,128)} %get-tuple-element.82) | copy-start | bytes 3145732
  (6 other events, 15.8 us)

commit v4 on v3

--- a/solution.py
+++ b/solution.py
@@ -588,6 +588,12 @@
 COLS = 3 * HID // NPIX
 SEGS = COLS // 32
 VMEM_LIMIT = 60 * 2**20
+SLOT = (0, 2, 3, 1)
+ROWS_AHEAD = 3
+BLOCK_VMEM = 60 * 2**20
+SMALL_ROWS = 64
+SMALL_PART = SMALL_ROWS // NCH
+ROOT_TAP = 6
 
 
 REACH = tuple(rate // ROWS for rate in aspp_rates)
@@ -661,7 +667,15 @@
     barrier = pltpu.get_barrier_semaphore()
     for target in targets:
         pl.semaphore_signal(barrier, inc=1, device_id=target, device_id_type=MESH)
-    pl.semaphore_wait(barrier, len(targets))
+    return len(targets)
+
+
+def await_greetings(count):
+    pl.semaphore_wait(pltpu.get_barrier_semaphore(), count)
+
+
+def from_hbm():
+    return pl.BlockSpec(memory_space=pl.ANY)
 
 
 def remote(src, dst, send_sem, recv_sem, target):
@@ -674,306 +688,6 @@
     p = lax.axis_index("pix")
     c = lax.axis_index("ch")
     return p, c, p // 2, lax.rem(p, 2), c // 2, lax.rem(c, 2)
-
-
-def heads_forward_kernel(
-    x_ref, w_ref, proj_ref, q_ref, xall_ref, wpt_ref,
-    acc, y_tmp, core_buf, core_in, x_buf, x_in, row_buf, local_sem,
-    zr_send, zl_send, z_recv, y_send, y_recv, core_send, core_recv, x_send, x_recv, row_send, row_recv,
-    pj_send, pj_recv,
-):
-    p, c, z, y, x, core = place()
-    zcount = NPIX // 2
-    up = (2 * lax.rem(z + 1, zcount) + y, c)
-    down = (2 * lax.rem(z + zcount - 1, zcount) + y, c)
-    other_y = (2 * z + 1 - y, c)
-    other_core = (p, 2 * x + 1 - core)
-    other_x = (p, 2 * (1 - x) + core)
-    row_targets = [(lax.rem(p + d, NPIX), c) for d in range(1, NPIX)]
-    ch_targets = [(p, lax.rem(c + d, NCH)) for d in range(1, NCH)]
-    greet(row_targets + ch_targets)
-
-    own = pltpu.make_async_copy(x_ref, xall_ref.at[p], local_sem.at[0])
-    own.start()
-    wpt_ref[c] = proj_ref[...]
-    proj_copies = [
-        remote(proj_ref, wpt_ref.at[c], pj_send.at[d - 1], pj_recv.at[d - 1], ch_targets[d - 1])
-        for d in range(1, NCH)
-    ]
-    for copy in proj_copies:
-        copy.start()
-
-    def to_up(source):
-        return remote(xall_ref.at[source], xall_ref.at[source], zr_send.at[source // 2], z_recv.at[source // 2], up)
-
-    def to_down(source):
-        return remote(xall_ref.at[source], xall_ref.at[source], zl_send.at[source // 2], z_recv.at[source // 2], down)
-
-    def to_y(source):
-        return remote(xall_ref.at[source], xall_ref.at[source], y_send.at[source // 2], y_recv.at[source // 2], other_y)
-
-    def step_of(i):
-        near = jnp.where(z == 0, i, jnp.where(z == 3, 3 - i, 0))
-        one = jnp.where(i == 0, 1, jnp.where(i == 1, 0, i))
-        two = jnp.where(i == 0, 2, jnp.where(i == 1, 3, 3 - i))
-        two = jnp.where(i == 2, 1, jnp.where(i == 3, 0, two))
-        return jnp.where(z == 1, one, jnp.where(z == 2, two, near))
-
-    acc[...] = jnp.zeros_like(acc)
-    own.wait()
-
-    def process(src):
-        xb = xall_ref[src]
-
-        first_row = pl.multiple_of(window_of(src) * 96, 32)
-
-        def one_seg(s, carry):
-            y_tmp[pl.ds(first_row, WINDOW), :] = nt_dot(w_ref[s, pl.ds(first_row, WINDOW), :], xb)
-
-            def add_group(dest, branch, first_tap, shifts):
-                rows = pl.ds(pl.multiple_of(branch * COLS + s * 32, 32), 32)
-                for r in range(ROWS):
-                    lanes = pl.ds(r * WIDTH, WIDTH)
-                    total = acc[dest, rows, lanes]
-                    for i, shift in enumerate(shifts):
-                        tile = y_tmp[pl.ds((first_tap + i) * 32, 32), lanes]
-                        total = total + slide(tile, shift)
-                    acc[dest, rows, lanes] = total
-
-            for branch, first_tap, step, reach, shifts in TAP_GROUPS:
-                dest = src - step * reach
-                if step == 0:
-                    add_group(dest, branch, first_tap, shifts)
-                else:
-
-                    @pl.when((dest >= 0) & (dest < NPIX))
-                    def _():
-                        add_group(dest, branch, first_tap, shifts)
-
-            return carry
-
-        lax.fori_loop(0, SEGS, one_seg, 0)
-
-    def gather_step(i, carry):
-        zs = step_of(i)
-        mine = 2 * zs + y
-        theirs = 2 * zs + 1 - y
-
-        @pl.when(i > 0)
-        def _():
-            to_up(mine).wait_recv()
-
-        @pl.when((zs <= z) & (z < zcount - 1))
-        def _():
-            to_up(mine).start()
-
-        @pl.when((zs >= z) & (z > 0))
-        def _():
-            to_down(mine).start()
-
-        to_y(mine).start()
-        process(mine)
-        to_y(theirs).wait_recv()
-        process(theirs)
-        return carry
-
-    lax.fori_loop(0, zcount, gather_step, 0)
-
-    def drain(zs, carry):
-        mine = 2 * zs + y
-
-        @pl.when((zs <= z) & (z < zcount - 1))
-        def _():
-            to_up(mine).wait_send()
-
-        @pl.when((zs >= z) & (z > 0))
-        def _():
-            to_down(mine).wait_send()
-
-        to_y(mine).wait_send()
-        return carry
-
-    lax.fori_loop(0, zcount, drain, 0)
-
-    def lanes_of(ch):
-        return pl.ds(pl.multiple_of(ch * WIDTH, WIDTH), WIDTH)
-
-    def core_copy(b):
-        return remote(core_buf.at[b], core_in.at[b], core_send.at[b], core_recv.at[b], other_core)
-
-    def x_copy(b):
-        return remote(x_buf.at[b], x_in.at[b], x_send.at[b], x_recv.at[b], other_x)
-
-    def row_copy(b, slot):
-        return remote(
-            row_buf.at[b],
-            q_ref.at[:, pl.ds(pl.multiple_of(COLS * p, 32), COLS), :],
-            row_send.at[slot],
-            row_recv.at[slot],
-            (b, c),
-        )
-
-    def core_step(d, carry):
-        b = lax.rem(p + d, NPIX)
-        for xx in range(2):
-            core_buf[b, xx] = acc[b, :, lanes_of(2 * xx + 1 - core)].astype(BF)
-        core_copy(b).start()
-        return carry
-
-    lax.fori_loop(0, NPIX, core_step, 0)
-
-    def x_step(d, carry):
-        b = lax.rem(p + d, NPIX)
-        core_copy(b).wait_recv()
-        x_buf[b] = (acc[b, :, lanes_of(2 * (1 - x) + core)] + core_in[b, 1 - x].astype(F32)).astype(BF)
-        x_copy(b).start()
-        return carry
-
-    lax.fori_loop(0, NPIX, x_step, 0)
-
-    def finish(b):
-        x_copy(b).wait_recv()
-        total = acc[b, :, lanes_of(c)] + core_in[b, x].astype(F32) + x_in[b].astype(F32)
-        return total.astype(BF).reshape(4, COLS, WIDTH)
-
-    def row_step(d, carry):
-        b = lax.rem(p + d, NPIX)
-        row_buf[b] = finish(b)
-        row_copy(b, d - 1).start()
-        return carry
-
-    lax.fori_loop(1, NPIX, row_step, 0)
-    q_ref[:, pl.ds(pl.multiple_of(COLS * p, 32), COLS), :] = finish(p)
-
-    def settle(d, carry):
-        b = lax.rem(p + d, NPIX)
-        row_copy(b, d - 1).wait()
-        return carry
-
-    lax.fori_loop(1, NPIX, settle, 0)
-
-    def settle_more(b, carry):
-        core_copy(b).wait_send()
-        x_copy(b).wait_send()
-        return carry
-
-    lax.fori_loop(0, NPIX, settle_more, 0)
-    for copy in proj_copies:
-        copy.wait()
-
-
-def heads_forward(block_out, w_seg, proj_own):
-    dma = pltpu.SemaphoreType.DMA
-    zc = NPIX // 2
-    return pl.pallas_call(
-        heads_forward_kernel,
-        out_shape=(
-            jax.ShapeDtypeStruct((4, 3 * HID, WIDTH), BF),
-            jax.ShapeDtypeStruct((NPIX, PX, CIN), BF),
-            jax.ShapeDtypeStruct((NCH, 3, HID // NCH, 4 * HID), BF),
-        ),
-        in_specs=[whole_vmem()] * 3,
-        out_specs=[whole_vmem()] * 3,
-        scratch_shapes=[
-            pltpu.VMEM((NPIX, 4 * COLS, PX), F32),
-            pltpu.VMEM((SEG_ROWS, PX), F32),
-            pltpu.VMEM((NPIX, 2, 4 * COLS, WIDTH), BF),
-            pltpu.VMEM((NPIX, 2, 4 * COLS, WIDTH), BF),
-            pltpu.VMEM((NPIX, 4 * COLS, WIDTH), BF),
-            pltpu.VMEM((NPIX, 4 * COLS, WIDTH), BF),
-            pltpu.VMEM((NPIX, 4, COLS, WIDTH), BF),
-            dma((1,)),
-            dma((zc,)), dma((zc,)), dma((zc,)), dma((zc,)), dma((zc,)),
-            dma((NPIX,)), dma((NPIX,)), dma((NPIX,)), dma((NPIX,)),
-            dma((NPIX - 1,)), dma((NPIX - 1,)),
-            dma((NCH - 1,)), dma((NCH - 1,)),
-        ],
-        compiler_params=pltpu.CompilerParams(
-            collective_id=1, has_side_effects=True, vmem_limit_bytes=VMEM_LIMIT
-        ),
-        name="heads_forward",
-    )(block_out, w_seg, proj_own)
-
-
-def heads_middle_kernel(
-    q_ref, bias_ref, pbias_ref, wpt_ref, wot_ref, obias_ref, label_ref, target_ref, mask_ref, count_ref,
-    dq_ref, dwp_ref, dwo_ref, rows_ref, obg_ref,
-    hid,
-):
-    ones = jnp.ones((8, WIDTH), BF)
-    for k in range(4):
-        hid[k] = gelu_of(q_ref[k].astype(F32) + bias_ref[:, k : k + 1]).astype(BF)
-    row = lax.broadcasted_iota(jnp.int32, (32, WIDTH), 0)
-    for t in range(3):
-        cols = slice(t * HID, (t + 1) * HID)
-        wpt = wpt_ref[:, t].reshape(HID, 4 * HID)
-        zt = pbias_ref[:, t : t + 1] + jnp.zeros((HID, WIDTH), F32)
-        for k in range(4):
-            zt = zt + nn_dot(wpt[:, k * HID : (k + 1) * HID], hid[k, cols, :])
-        ut = gelu_of(zt).astype(BF)
-        out = lax.dot_general(
-            wot_ref[t], ut, (((0,), (0,)), ((), ())), preferred_element_type=F32
-        ) + obias_ref[:, t : t + 1]
-        scale = mask_ref[t : t + 1, :] / count_ref[t : t + 1, :]
-        if t == 0:
-            live = row < NCLS
-            highest = jnp.max(jnp.where(live, out, -1e30), axis=0, keepdims=True)
-            raised = jnp.where(live, jnp.exp(jnp.minimum(out - highest, 0.0)), 0.0)
-            probs = raised / jnp.sum(raised, axis=0, keepdims=True)
-            onehot = (row == label_ref[0:1, :]).astype(F32)
-            slope = scale * (probs - onehot)
-        elif t == 1:
-            gap = out - target_ref[0:1, :]
-            slope = jnp.where(row < 1, scale * gap / jnp.sqrt(gap * gap + 1.0), 0.0)
-        else:
-            target = jnp.zeros((32, WIDTH), F32)
-            for i in range(3):
-                target = jnp.where(row == i, target_ref[1 + i : 2 + i, :], target)
-            slope = jnp.where(row < 3, scale * (out - target), 0.0)
-        ot = slope.astype(BF)
-        dwo_ref[t] = nt_dot(ot, ut)
-        obg_ref[t] = nt_dot(ones, ot)
-        dz = (nn_dot(wot_ref[t], ot) * gelu_slope(zt)).astype(BF)
-        rows_ref[4, :, cols] = nt_dot(ones, dz)
-        for k in range(4):
-            part = hid[k, cols, :]
-            dwp_ref[t, k * HID : (k + 1) * HID, :] = nt_dot(part, dz)
-            dcat = lax.dot_general(
-                wpt[:, k * HID : (k + 1) * HID], dz, (((0,), (0,)), ((), ())),
-                preferred_element_type=F32,
-            )
-            before = q_ref[k, cols, :].astype(F32) + bias_ref[cols, k : k + 1]
-            dq_ref[k, cols, :] = (dcat * gelu_slope(before)).astype(BF)
-    for k in range(4):
-        rows_ref[k] = nt_dot(ones, dq_ref[k])
-
-
-def heads_middle(q, bias, pbias, wpt, wot, obias, label, target, mask, count):
-    return pl.pallas_call(
-        heads_middle_kernel,
-        out_shape=(
-            jax.ShapeDtypeStruct((4, 3 * HID, WIDTH), BF),
-            jax.ShapeDtypeStruct((3, 4 * HID, HID), F32),
-            jax.ShapeDtypeStruct((3, 32, HID), F32),
-            jax.ShapeDtypeStruct((5, 8, 3 * HID), F32),
-            jax.ShapeDtypeStruct((3, 8, 32), F32),
-        ),
-        in_specs=[whole_vmem()] * 10,
-        out_specs=[whole_vmem()] * 5,
-        scratch_shapes=[pltpu.VMEM((4, 3 * HID, WIDTH), BF)],
-        compiler_params=pltpu.CompilerParams(vmem_limit_bytes=VMEM_LIMIT),
-        name="heads_middle",
-    )(q, bias, pbias, wpt, wot, obias, label, target, mask, count)
-
-
-def fold(values):
-    rows, lanes = values.shape
-    total = values[0:8, 0:128]
-    for r in range(rows // 8):
-        for l in range(lanes // 128):
-            if r or l:
-                total = total + values[8 * r : 8 * r + 8, 128 * l : 128 * l + 128]
-    return total
 
 
 def moved_segments():
@@ -993,13 +707,474 @@
 MOVES = moved_segments()
 
 
+NALL = NPIX * NCH
+
+
+def all_targets():
+    me = lax.axis_index("pix") * NCH + lax.axis_index("ch")
+    targets = []
+    for d in range(1, NALL):
+        other = lax.rem(me + d, NALL)
+        targets.append((other // NCH, lax.rem(other, NCH)))
+    return targets
+
+
+def sum_everywhere(row, inbox, send_sem, recv_sem):
+    me = lax.axis_index("pix") * NCH + lax.axis_index("ch")
+    inbox[me, 0:1, :] = row
+    view = inbox.at[me, 0:1]
+    copies = [
+        remote(view, view, send_sem.at[i], recv_sem.at[i], target) for i, target in enumerate(all_targets())
+    ]
+    for copy in copies:
+        copy.start()
+    for copy in copies:
+        copy.wait()
+    total = inbox[0, 0:1, :]
+    for i in range(1, NALL):
+        total = total + inbox[i, 0:1, :]
+    return total
+
+
+def heads_forward_kernel(
+    x_ref, rates_hbm, root_ref, proj_ref, q_ref, xall_out, wpt_ref, w_out, w_more_ref,
+    rates_ref, xall_ref, w_ref, acc, y_tmp, core_buf, core_in, x_buf, x_in, row_buf, local_sem,
+    zr_send, zl_send, z_recv, y_send, y_recv, core_send, core_recv, x_send, x_recv, row_send, row_recv,
+    pj_send, pj_recv, wm_send, wm_recv, eh_send, eh_recv,
+):
+    p, c, z, y, x, core = place()
+    zcount = NPIX // 2
+    up = (2 * lax.rem(z + 1, zcount) + y, c)
+    down = (2 * lax.rem(z + zcount - 1, zcount) + y, c)
+    other_y = (2 * z + 1 - y, c)
+    other_core = (p, 2 * x + 1 - core)
+    other_x = (p, 2 * (1 - x) + core)
+    row_targets = [(lax.rem(p + d, NPIX), c) for d in range(1, NPIX)]
+    ch_targets = [(p, lax.rem(c + d, NCH)) for d in range(1, NCH)]
+    greeted = greet(row_targets + ch_targets)
+    rates_in = pltpu.make_async_copy(rates_hbm, rates_ref, local_sem.at[3])
+    rates_in.start()
+
+    own = pltpu.make_async_copy(x_ref, xall_ref.at[p], local_sem.at[0])
+    own.start()
+    wpt_ref[c] = proj_ref[...]
+    await_greetings(greeted)
+    proj_copies = [
+        remote(proj_ref, wpt_ref.at[c], pj_send.at[d - 1], pj_recv.at[d - 1], ch_targets[d - 1])
+        for d in range(1, NCH)
+    ]
+    for copy in proj_copies:
+        copy.start()
+
+    def to_up(source):
+        return remote(xall_ref.at[source], xall_ref.at[source], zr_send.at[source // 2], z_recv.at[source // 2], up)
+
+    def to_down(source):
+        return remote(xall_ref.at[source], xall_ref.at[source], zl_send.at[source // 2], z_recv.at[source // 2], down)
+
+    def to_y(source):
+        return remote(xall_ref.at[source], xall_ref.at[source], y_send.at[source // 2], y_recv.at[source // 2], other_y)
+
+    def half_to(source, i, target):
+        view = xall_ref.at[source, PX // 2 : PX]
+        return remote(view, view, eh_send.at[i], eh_recv.at[i], target)
+
+    def to_y_part(source):
+        view = xall_ref.at[source, 0 : PX // 2]
+        return remote(view, view, y_send.at[source // 2], y_recv.at[source // 2], other_y)
+
+    def is_far_end(zs):
+        return ((zs == 0) | (zs == zcount - 1)) & (zs != z)
+
+    def step_of(i):
+        near = jnp.where(z == 0, i, jnp.where(z == 3, 3 - i, 0))
+        one = jnp.where(i == 0, 1, jnp.where(i == 1, 0, i))
+        two = jnp.where(i == 0, 2, jnp.where(i == 1, 3, 3 - i))
+        two = jnp.where(i == 2, 1, jnp.where(i == 3, 0, two))
+        return jnp.where(z == 1, one, jnp.where(z == 2, two, near))
+
+    own.wait()
+    to_y(p).start()
+
+    @pl.when(z < zcount - 1)
+    def _():
+        to_up(p).start()
+
+    @pl.when(z > 0)
+    def _():
+        to_down(p).start()
+
+    acc[...] = jnp.zeros_like(acc)
+    root = root_ref[...]
+    rates_in.wait()
+    for s in range(SEGS):
+        w_ref[s, ROOT_TAP * 32 : (ROOT_TAP + 1) * 32, :] = root[s * 32 : (s + 1) * 32].astype(BF)
+        for branch, first, step, reach, shifts in TAP_GROUPS:
+            if branch > 0:
+                value = rates_ref[branch - 1, 3 * (step + 1) : 3 * (step + 2), s * 32 : (s + 1) * 32, :]
+                w_ref[s, first * 32 : (first + 3) * 32, :] = value.astype(BF).reshape(96, CIN)
+
+    def process(src):
+        xb = xall_ref[src]
+
+        first_row = pl.multiple_of(window_of(src) * 96, 32)
+
+        def one_seg(s, carry):
+            y_tmp[pl.ds(first_row, WINDOW), :] = nt_dot(w_ref[s, pl.ds(first_row, WINDOW), :], xb)
+
+            def add_group(dest, branch, first_tap, shifts):
+                rows = pl.ds(pl.multiple_of(SLOT[branch] * COLS + s * 32, 32), 32)
+                for r in range(ROWS):
+                    lanes = pl.ds(r * WIDTH, WIDTH)
+                    total = acc[dest, rows, lanes]
+                    for i, shift in enumerate(shifts):
+                        tile = y_tmp[pl.ds((first_tap + i) * 32, 32), lanes]
+                        total = total + slide(tile, shift)
+                    acc[dest, rows, lanes] = total
+
+            for branch, first_tap, step, reach, shifts in TAP_GROUPS:
+                dest = src - step * reach
+                if step == 0:
+                    add_group(dest, branch, first_tap, shifts)
+                else:
+
+                    @pl.when((dest >= 0) & (dest < NPIX))
+                    def _():
+                        add_group(dest, branch, first_tap, shifts)
+
+            return carry
+
+        lax.fori_loop(0, SEGS, one_seg, 0)
+
+    def lanes_of(ch):
+        return pl.ds(pl.multiple_of(ch * WIDTH, WIDTH), WIDTH)
+
+    half_rows = (slice(0, 2 * COLS), slice(2 * COLS, 4 * COLS))
+
+    def core_copy(b, half):
+        return remote(core_buf.at[half, b], core_in.at[half, b], core_send.at[half, b], core_recv.at[half, b], other_core)
+
+    def x_copy(b, half):
+        return remote(x_buf.at[half, b], x_in.at[half, b], x_send.at[half, b], x_recv.at[half, b], other_x)
+
+    def row_copy(b, half, slot):
+        return remote(
+            row_buf.at[half, b],
+            q_ref.at[2 * half : 2 * half + 2, pl.ds(pl.multiple_of(COLS * p, 32), COLS), :],
+            row_send.at[half, slot],
+            row_recv.at[half, slot],
+            (b, c),
+        )
+
+    def core_start(b, half):
+        for xx in range(2):
+            core_buf[half, b, xx] = acc[b, half_rows[half], lanes_of(2 * xx + 1 - core)].astype(BF)
+        core_copy(b, half).start()
+
+    def x_start(b, half):
+        core_copy(b, half).wait_recv()
+        x_buf[half, b] = (
+            acc[b, half_rows[half], lanes_of(2 * (1 - x) + core)] + core_in[half, b, 1 - x].astype(F32)
+        ).astype(BF)
+        x_copy(b, half).start()
+
+    def finish(b, half):
+        x_copy(b, half).wait_recv()
+        total = (
+            acc[b, half_rows[half], lanes_of(c)] + core_in[half, b, x].astype(F32) + x_in[half, b].astype(F32)
+        )
+        return total.astype(BF).reshape(2, COLS, WIDTH)
+
+    def gather_step(i, carry):
+        zs = step_of(i)
+        mine = 2 * zs + y
+        theirs = 2 * zs + 1 - y
+
+        @pl.when(i > 0)
+        def _():
+            to_up(mine).wait_recv()
+
+        @pl.when((zs < z) & (z < zcount - 1))
+        def _():
+            to_up(mine).start()
+
+        @pl.when((zs > z) & (z > 0))
+        def _():
+            to_down(mine).start()
+
+        far = is_far_end(zs)
+
+        @pl.when((i > 0) & jnp.logical_not(far))
+        def _():
+            to_y(mine).start()
+
+        @pl.when(far)
+        def _():
+            to_y_part(mine).start()
+
+        process(mine)
+        core_start(mine, 0)
+
+        @pl.when(i > 0)
+        def _():
+            x_start(2 * step_of(i - 1) + 1 - y, 0)
+
+        @pl.when(jnp.logical_not(far))
+        def _():
+            to_y(theirs).wait_recv()
+
+        for end, i_end in ((0, 0), (zcount - 1, 1)):
+            onward = up if end == 0 else down
+
+            @pl.when((zs == end) & (z == end))
+            def _():
+                half_to(theirs, i_end, onward).start()
+
+            @pl.when((zs == end) & (z != end))
+            def _():
+                to_y_part(theirs).wait_recv()
+                half_to(theirs, i_end, onward).wait_recv()
+
+            @pl.when((zs == end) & (z != end) & (z != zcount - 1 - end))
+            def _():
+                half_to(theirs, i_end, onward).start()
+
+        process(theirs)
+        core_start(theirs, 0)
+        x_start(mine, 0)
+        return carry
+
+    lax.fori_loop(0, zcount, gather_step, 0)
+    leaving = [
+        pltpu.make_async_copy(xall_ref, xall_out, local_sem.at[1]),
+        pltpu.make_async_copy(w_ref, w_out, local_sem.at[2]),
+    ]
+    for copy in leaving:
+        copy.start()
+
+    def weight_copy(i):
+        return remote(w_ref.at[MOVES[i][1]], w_more_ref, wm_send.at[0], wm_recv.at[0], other_y)
+
+    for i, (giver, s, receiver) in enumerate(MOVES):
+
+        @pl.when(p == giver)
+        def _():
+            weight_copy(i).start()
+
+    def block_after(d):
+        return lax.rem(p + 1 + d, NPIX)
+
+    def late_core(d, carry):
+        core_start(block_after(d), 1)
+        return carry
+
+    lax.fori_loop(0, NPIX, late_core, 0)
+    x_start(2 * step_of(zcount - 1) + 1 - y, 0)
+
+    def late_x(d, carry):
+        x_start(block_after(d), 1)
+        return carry
+
+    lax.fori_loop(0, NPIX, late_x, 0)
+    own_rows = pl.ds(pl.multiple_of(COLS * p, 32), COLS)
+    for half in range(2):
+
+        def row_step(d, carry):
+            b = block_after(d)
+            row_buf[half, b] = finish(b, half)
+            row_copy(b, half, d).start()
+            return carry
+
+        lax.fori_loop(0, NPIX - 1, row_step, 0)
+        q_ref[2 * half : 2 * half + 2, own_rows, :] = finish(p, half)
+
+    def drain(zs, carry):
+        mine = 2 * zs + y
+
+        @pl.when((zs <= z) & (z < zcount - 1))
+        def _():
+            to_up(mine).wait_send()
+
+        @pl.when((zs >= z) & (z > 0))
+        def _():
+            to_down(mine).wait_send()
+
+        far = is_far_end(zs)
+
+        @pl.when(jnp.logical_not(far))
+        def _():
+            to_y(mine).wait_send()
+
+        @pl.when(far)
+        def _():
+            to_y_part(mine).wait_send()
+
+        return carry
+
+    lax.fori_loop(0, zcount, drain, 0)
+    for end, i_end in ((0, 0), (zcount - 1, 1)):
+
+        @pl.when(z != zcount - 1 - end)
+        def _():
+            half_to(2 * end + 1 - y, i_end, up).wait_send()
+
+    for half in range(2):
+
+        def settle(d, carry):
+            row_copy(block_after(d), half, d).wait()
+            return carry
+
+        lax.fori_loop(0, NPIX - 1, settle, 0)
+
+        def settle_more(b, carry):
+            core_copy(b, half).wait_send()
+            x_copy(b, half).wait_send()
+            return carry
+
+        lax.fori_loop(0, NPIX, settle_more, 0)
+    for copy in proj_copies + leaving:
+        copy.wait()
+    for i, (giver, s, receiver) in enumerate(MOVES):
+
+        @pl.when(p == giver)
+        def _():
+            weight_copy(i).wait_send()
+
+        @pl.when(p == receiver)
+        def _():
+            weight_copy(i).wait_recv()
+
+
+def heads_forward(block_out, rates, root, proj_own):
+    dma = pltpu.SemaphoreType.DMA
+    zc = NPIX // 2
+    return pl.pallas_call(
+        heads_forward_kernel,
+        out_shape=(
+            jax.ShapeDtypeStruct((4, 3 * HID, WIDTH), BF),
+            jax.ShapeDtypeStruct((NPIX, PX, CIN), BF),
+            jax.ShapeDtypeStruct((NCH, 3, HID // NCH, 4 * HID), BF),
+            jax.ShapeDtypeStruct((SEGS, SEG_ROWS, CIN), BF),
+            jax.ShapeDtypeStruct((SEG_ROWS, CIN), BF),
+        ),
+        in_specs=[whole_vmem(), from_hbm(), whole_vmem(), whole_vmem()],
+        out_specs=[whole_vmem(), from_hbm(), whole_vmem(), from_hbm(), whole_vmem()],
+        scratch_shapes=[
+            pltpu.VMEM((3, 9, COLS, CIN), F32),
+            pltpu.VMEM((NPIX, PX, CIN), BF),
+            pltpu.VMEM((SEGS, SEG_ROWS, CIN), BF),
+            pltpu.VMEM((NPIX, 4 * COLS, PX), F32),
+            pltpu.VMEM((SEG_ROWS, PX), F32),
+            pltpu.VMEM((2, NPIX, 2, 2 * COLS, WIDTH), BF),
+            pltpu.VMEM((2, NPIX, 2, 2 * COLS, WIDTH), BF),
+            pltpu.VMEM((2, NPIX, 2 * COLS, WIDTH), BF),
+            pltpu.VMEM((2, NPIX, 2 * COLS, WIDTH), BF),
+            pltpu.VMEM((2, NPIX, 2, COLS, WIDTH), BF),
+            dma((4,)),
+            dma((zc,)), dma((zc,)), dma((zc,)), dma((zc,)), dma((zc,)),
+            dma((2, NPIX)), dma((2, NPIX)), dma((2, NPIX)), dma((2, NPIX)),
+            dma((2, NPIX - 1)), dma((2, NPIX - 1)),
+            dma((NCH - 1,)), dma((NCH - 1,)), dma((1,)), dma((1,)), dma((2,)), dma((2,)),
+        ],
+        compiler_params=pltpu.CompilerParams(
+            collective_id=1, has_side_effects=True, vmem_limit_bytes=VMEM_LIMIT
+        ),
+        name="heads_forward",
+    )(block_out, rates, root, proj_own)
+
+
+def heads_middle_part(
+    q_ref, wpt_ref, small_ref, cols_ref, stats_ref, label_ref, depth_ref, normal_ref, mask_ref,
+    dq_ref, dwp_ref, sums_ref, hid,
+):
+    c = lax.axis_index("ch")
+    ones = jnp.ones((8, WIDTH), BF)
+    columns = jnp.transpose(small_ref[...])
+    out_w = jnp.transpose(cols_ref[...]).astype(BF)
+    out_bias = columns[0:32, 15:16]
+    sums_ref[...] = jnp.zeros_like(sums_ref)
+
+    def spread(rows_8):
+        return rows_8[0:1, :]
+
+    for k in range(4):
+        for t in range(3):
+            cols = slice(t * HID, (t + 1) * HID)
+            i = 3 * k + t
+            hid[k, cols, :] = gelu_of(q_ref[SLOT[k], cols, :].astype(F32) + columns[:, i : i + 1]).astype(BF)
+    row = lax.broadcasted_iota(jnp.int32, (32, WIDTH), 0)
+    own_row = pl.ds(c, 1)
+    out_sum = jnp.zeros((32, HID), F32)
+    bias_sum = jnp.zeros((8, 32), F32)
+    for t in range(3):
+        cols = slice(t * HID, (t + 1) * HID)
+        wpt = wpt_ref[:, t].reshape(HID, 4 * HID)
+        zt = columns[:, 12 + t : 13 + t] + jnp.zeros((HID, WIDTH), F32)
+        for k in range(4):
+            zt = zt + nn_dot(wpt[:, k * HID : (k + 1) * HID], hid[k, cols, :])
+        ut = gelu_of(zt).astype(BF)
+        out = nn_dot(out_w, ut) + out_bias
+        count = jnp.maximum(jnp.sum(stats_ref[2 + t : 3 + t, :], axis=1, keepdims=True), 1.0)
+        scale = mask_ref[t, own_row, :].astype(F32) / count
+        if t == 0:
+            live = row < NCLS
+            highest = jnp.max(jnp.where(live, out, -1e30), axis=0, keepdims=True)
+            raised = jnp.where(live, jnp.exp(jnp.minimum(out - highest, 0.0)), 0.0)
+            probs = raised / jnp.sum(raised, axis=0, keepdims=True)
+            onehot = (row == label_ref[own_row, :]).astype(F32)
+            slope = scale * (probs - onehot)
+        elif t == 1:
+            gap = out - depth_ref[own_row, :]
+            slope = jnp.where(row == NCLS, scale * gap / jnp.sqrt(gap * gap + 1.0), 0.0)
+        else:
+            target = jnp.zeros((32, WIDTH), F32)
+            for i in range(3):
+                target = jnp.where(row == NCLS + 1 + i, normal_ref[i, own_row, :], target)
+            slope = jnp.where((row > NCLS) & (row < NCLS + 4), scale * (out - target), 0.0)
+        ot = slope.astype(BF)
+        out_sum = out_sum + nt_dot(ot, ut)
+        bias_sum = bias_sum + nt_dot(ones, ot)
+        back = lax.dot_general(out_w, ot, (((0,), (0,)), ((), ())), preferred_element_type=F32)
+        dz = (back * gelu_slope(zt)).astype(BF)
+        sums_ref[12 + t : 13 + t, :] = spread(nt_dot(ones, dz))
+        for k in range(4):
+            part = hid[k, cols, :]
+            product = nt_dot(part, dz).astype(BF)
+            for half in range(2):
+                for quarter in range(NCH):
+                    start = half * 128 + quarter * 32
+                    dwp_ref[quarter, t, 2 * k + half] = product[start : start + 32]
+            dcat = lax.dot_general(
+                wpt[:, k * HID : (k + 1) * HID], dz, (((0,), (0,)), ((), ())),
+                preferred_element_type=F32,
+            )
+            i = 3 * k + t
+            before = q_ref[SLOT[k], cols, :].astype(F32) + columns[:, i : i + 1]
+            dq = (dcat * gelu_slope(before)).astype(BF)
+            dq_ref[k, cols, :] = dq
+            sums_ref[i : i + 1, :] = spread(nt_dot(ones, dq))
+    sums_ref[15:16, 0:32] = spread(bias_sum)
+    sums_ref[16:48, :] = out_sum
+
+
+def fold(values):
+    rows, lanes = values.shape
+    total = values[0:8, 0:128]
+    for r in range(rows // 8):
+        for l in range(lanes // 128):
+            if r or l:
+                total = total + values[8 * r : 8 * r + 8, 128 * l : 128 * l + 128]
+    return total
+
+
 def heads_backward_kernel(
-    dq_ref, xall_ref, w_ref, dw_ref, gz_ref, square_ref,
-    dq_all, dq_more, w_more, wt, dcol, dcol_more, work, buf, z_out, oi_in, ac_in, grads,
-    gram_own, gram_ch, gram_px, gsum,
-    local_sem, row_send, row_recv, x_send, x_recv, ca_send, ca_recv, cb_send, cb_recv,
-    more_send, more_recv, fan_send, fan_recv, wm_send, wm_recv,
-    y_send, y_recv, oi_send, oi_recv, ac_send, ac_recv, gc_send, gc_recv, gp_send, gp_recv,
+    q_ref, wpt_ref, small_ref, cols_ref, stats_ref, label_ref, depth_ref, normal_ref, mask_ref, xall_hbm, w_ref, w_more,
+    rates_ref, gz_ref, square_ref, proj_out_ref, sums_out_ref, root_out_ref,
+    dq_ref, dwp_ref, sums_ref, hid, dq_all, dq_more, wt, dcol, dcol_more, work, buf, z_out, oi_in, ac_in,
+    gram_own, gram_all, proj_in, sums_in, dw_ref, blank, xall_ref,
+    local_sem, out_sem, row_send, row_recv, x_send, x_recv, ca_send, ca_recv, cb_send, cb_recv,
+    more_send, more_recv, fan_send, fan_recv,
+    y_send, y_recv, oi_send, oi_recv, ac_send, ac_recv, gram_send, gram_recv, sp_send, sp_recv,
 ):
     p, c, z, y, x, core = place()
     zcount = NPIX // 2
@@ -1008,7 +1183,14 @@
     other_x = (p, 2 * (1 - x) + core)
     pix_targets = [(lax.rem(p + d, NPIX), c) for d in range(1, NPIX)]
     ch_targets = [(p, lax.rem(c + d, NCH)) for d in range(1, NCH)]
-    greet(pix_targets + ch_targets)
+    greeted = greet(all_targets())
+    coming = pltpu.make_async_copy(xall_hbm, xall_ref, local_sem.at[1])
+    coming.start()
+    heads_middle_part(
+        q_ref, wpt_ref, small_ref, cols_ref, stats_ref, label_ref, depth_ref, normal_ref, mask_ref,
+        dq_ref, dwp_ref, sums_ref, hid,
+    )
+    await_greetings(greeted)
     far = 2 * (1 - x) + core
 
     def cols_of(b):
@@ -1026,9 +1208,6 @@
             more_send.at[i], more_recv.at[source], (receiver, c),
         )
 
-    def weight_copy(i):
-        return remote(w_ref.at[MOVES[i][1]], w_more, wm_send.at[0], wm_recv.at[0], other_y)
-
     def fan_copy(i, ch, target):
         return remote(dq_more.at[:, ch], dq_more.at[:, ch], fan_send.at[i], fan_recv.at[i], target)
 
@@ -1040,7 +1219,7 @@
 
     receives = any_of([p == move[2] for move in MOVES])
 
-    for d in range(1, NPIX):
+    for d in range(1, 1 + ROWS_AHEAD):
         row_copy(d).start()
     own = pltpu.make_async_copy(dq_ref.at[:, cols_of(p), :], dq_all.at[p, c], local_sem.at[0])
     own.start()
@@ -1054,10 +1233,6 @@
         @pl.when(p != receiver)
         def _():
             more_copy(i, p).start()
-
-        @pl.when(p == giver)
-        def _():
-            weight_copy(i).start()
 
     own.wait()
 
@@ -1084,7 +1259,9 @@
     for d in range(NPIX):
         b = lax.rem(p + NPIX - d, NPIX)
         if d > 0:
-            row_copy(d).wait_recv()
+            row_copy(d).wait()
+            if d + ROWS_AHEAD < NPIX:
+                row_copy(d + ROWS_AHEAD).start()
         x_copy(d, b, c).start()
         ca_copy(d, b, c).start()
         if d > 0:
@@ -1108,10 +1285,10 @@
         x_copy(d, b, far).wait_recv()
         cb_copy(d, b, far).start()
     dw_ref[...] = jnp.zeros_like(dw_ref)
+    blank[...] = jnp.zeros_like(blank)
 
     @pl.when(receives)
     def _():
-        weight_copy(0).wait_recv()
         for win in range(3):
             wt[win, :, SEGS * WINDOW :] = jnp.transpose(
                 w_more[win * 96 : win * 96 + WINDOW, :].astype(F32)
@@ -1128,6 +1305,15 @@
     def _():
         fan_copy(1, 2 * x + 1 - core, other_core).wait_recv()
         fan_copy(2, 2 * (1 - x) + 1 - core, other_core).wait_recv()
+
+    ride = []
+    for d in range(1, NCH):
+        other = lax.rem(c + d, NCH)
+        part = pl.ds(pl.multiple_of(other * SMALL_PART, SMALL_PART), SMALL_PART)
+        ride.append(remote(dwp_ref.at[other], proj_in.at[c], sp_send.at[0, d - 1], sp_recv.at[0, d - 1], (p, other)))
+        ride.append(remote(sums_ref.at[part], sums_in.at[c], sp_send.at[1, d - 1], sp_recv.at[1, d - 1], (p, other)))
+    for copy in ride:
+        copy.start()
 
     def one_block(b):
         win = window_of(b)
@@ -1275,15 +1461,17 @@
     lax.fori_loop(0, zcount, block_pair, 0)
 
     def weight_block(b, carry):
-        first_row = pl.multiple_of(window_of(b) * 96, 32)
+        first_tap = window_of(b) * 3
 
         def one_seg(s, inner_carry):
             rows = pl.ds(pl.multiple_of(s * WINDOW, WINDOW), WINDOW)
-            dw_ref[s, pl.ds(first_row, WINDOW), :] += nn_dot(dcol[b, rows, :], xall_ref[b])
+            taps = pl.ds(first_tap, WINDOW // 32)
+            dw_ref[s, taps] += nn_dot(dcol[b, rows, :], xall_ref[b]).reshape(WINDOW // 32, 32, CIN)
             return inner_carry
 
         return lax.fori_loop(0, SEGS, one_seg, carry)
 
+    coming.wait()
     lax.fori_loop(0, NPIX // 2, weight_block, 0)
 
     @pl.when(inner)
@@ -1295,74 +1483,94 @@
         oi_copy(2, ac_in.at[2]).start()
 
     lax.fori_loop(NPIX // 2, NPIX, weight_block, 0)
+    out_copies = []
+    at = {(group[0] - 1, group[2]): group[1] for group in TAP_GROUPS if group[0] > 0}
+    for rate_index in range(3):
+        for step in (-1, 0, 1):
+            first = at.get((rate_index, step))
+            for s in range(SEGS):
+                source = blank if first is None else dw_ref.at[s, first : first + 3]
+                out_copies.append(
+                    pltpu.make_async_copy(
+                        source,
+                        rates_ref.at[rate_index, 3 * (step + 1) : 3 * (step + 2), s * 32 : (s + 1) * 32, :],
+                        out_sem.at[len(out_copies)],
+                    )
+                )
+    for copy in out_copies:
+        copy.start()
     square_ref[...] = jnp.zeros_like(square_ref)
 
     def square_rows(m, carry):
         s = m // TAPS
-        part = dw_ref[s, pl.ds(pl.multiple_of(lax.rem(m, TAPS) * 32, 32), 32), :]
+        part = dw_ref[s, lax.rem(m, TAPS)]
         square_ref[...] += fold(part * part)
         return carry
 
     lax.fori_loop(0, SEGS * TAPS, square_rows, 0)
 
+    for copy in ride:
+        copy.wait()
+    for t in range(3):
+        total = dwp_ref[c, t].astype(F32)
+        for d in range(1, NCH):
+            total = total + proj_in[lax.rem(c + d, NCH), t].astype(F32)
+        total = total.astype(BF)
+        for b in range(NPIX):
+            proj_out_ref[b, t] = total[b]
+    total = sums_ref[pl.ds(pl.multiple_of(c * SMALL_PART, SMALL_PART), SMALL_PART), :]
+    for d in range(1, NCH):
+        total = total + sums_in[lax.rem(c + d, NCH)]
+    sums_out_ref[...] = total
+    for s in range(SEGS):
+        root_out_ref[s * 32 : (s + 1) * 32, :] = dw_ref[s, ROOT_TAP]
+
+    for copy in out_copies:
+        copy.wait()
     near_task = jnp.where(mirrored, 2, 0)
     far_task = jnp.where(mirrored, 0, 2)
     y_copy(true_z(order(zcount - 1))).wait_recv()
+
+    def keep(task, value):
+        dw_ref[task, 0:16] = value.reshape(16, 32, PX)
 
     @pl.when(outer)
     def _():
         for i in range(3):
             oi_copy(i, z_out.at[0]).wait_recv()
-        grads[near_task] = (
-            buf[block_at(0)].astype(F32) + buf[arrived_at(0)].astype(F32) + oi_in[0].astype(F32)
-        )
-        grads[1] = oi_in[1].astype(F32)
-        grads[far_task] = oi_in[2].astype(F32)
+        keep(near_task, buf[block_at(0)].astype(F32) + buf[arrived_at(0)].astype(F32) + oi_in[0].astype(F32))
+        keep(1, oi_in[1].astype(F32))
+        keep(far_task, oi_in[2].astype(F32))
 
     @pl.when(inner)
     def _():
         oi_copy(2, z_out.at[0]).wait_recv()
         ac_copy(1, z_out.at[0]).wait_recv()
         ac_copy(3, z_out.at[0]).wait_recv()
-        grads[near_task] = oi_in[2].astype(F32) + buf[near_at(1)].astype(F32)
-        grads[1] = buf[mid_at(1)].astype(F32) + ac_in[1].astype(F32)
-        grads[far_task] = ac_in[3].astype(F32)
+        keep(near_task, oi_in[2].astype(F32) + buf[near_at(1)].astype(F32))
+        keep(1, buf[mid_at(1)].astype(F32) + ac_in[1].astype(F32))
+        keep(far_task, ac_in[3].astype(F32))
 
     pairs = ((0, 0), (0, 1), (0, 2), (1, 1), (1, 2), (2, 2))
     gram_own[...] = jnp.zeros_like(gram_own)
 
     def gram_rows(m, carry):
-        rows = pl.ds(pl.multiple_of(m * 32, 32), 32)
-        tasks = [grads[t, rows, :] for t in range(3)]
+        tasks = [dw_ref[t, m] for t in range(3)]
         for i, (a, b) in enumerate(pairs):
             gram_own[i] += fold(tasks[a] * tasks[b])
         return carry
 
     lax.fori_loop(0, CIN // 32, gram_rows, 0)
 
-    def gc_copy(d):
-        return remote(gram_own, gram_ch.at[d - 1], gc_send.at[d - 1], gc_recv.at[d - 1], ch_targets[d - 1])
-
-    for d in range(1, NCH):
-        gc_copy(d).start()
-    for d in range(1, NCH):
-        gc_copy(d).wait()
-    gsum[...] = gram_own[...] + gram_ch[0] + gram_ch[1] + gram_ch[2]
-
-    def gp_copy(d):
-        return remote(gsum, gram_px.at[d - 1], gp_send.at[d - 1], gp_recv.at[d - 1], pix_targets[d - 1])
-
-    for d in range(1, NPIX):
-        gp_copy(d).start()
-    for d in range(1, NPIX):
-        gp_copy(d).wait()
+    lane = lax.broadcasted_iota(jnp.int32, (1, 128), 1)
+    row = jnp.zeros((1, 128), F32)
+    for i in range(6):
+        value = jnp.sum(column_sums(gram_own[i]), axis=1, keepdims=True)
+        row = row + jnp.where(lane == i, value, 0.0)
+    row = sum_everywhere(row, gram_all, gram_send, gram_recv)
     entry = {}
     for i, (a, b) in enumerate(pairs):
-        total = gsum[i]
-        for d in range(NPIX - 1):
-            total = total + gram_px[d, i]
-        value = jnp.sum(total, axis=0, keepdims=True)
-        value = jnp.sum(value, axis=1, keepdims=True)
+        value = jnp.sum(jnp.where(lane == i, row, 0.0), axis=1, keepdims=True)
         entry[(a, b)] = value
         entry[(b, a)] = value
     lengths = [jnp.sqrt(entry[(t, t)] + 1e-12) for t in range(3)]
@@ -1385,12 +1593,10 @@
     alpha_zero = 1.0 - alpha_one - alpha_two
 
     for m in range(CIN // 128):
-        rows = pl.ds(m * 128, 128)
-        mixed = alpha_zero * grads[0, rows, :] + alpha_one * grads[1, rows, :] + alpha_two * grads[2, rows, :]
+        tasks = [dw_ref[t, 4 * m : 4 * m + 4].reshape(128, PX) for t in range(3)]
+        mixed = alpha_zero * tasks[0] + alpha_one * tasks[1] + alpha_two * tasks[2]
         gz_ref[:, m * 128 : (m + 1) * 128] = jnp.transpose(mixed)
 
-    for d in range(1, NPIX):
-        row_copy(d).wait_send()
     for d in range(NPIX):
         b = lax.rem(p + NPIX - d, NPIX)
         x_copy(d, b, c).wait_send()
@@ -1402,10 +1608,6 @@
         def _():
             more_copy(i, p).wait_send()
 
-        @pl.when(p == giver)
-        def _():
-            weight_copy(i).wait_send()
-
     @pl.when(receives)
     def _():
         fan_copy(0, c, other_x).wait_send()
@@ -1423,22 +1625,28 @@
             ac_copy(i, z_out.at[0]).wait_send()
 
 
-def heads_backward(dq, xall, w_seg):
+def heads_backward(*operands):
     dma = pltpu.SemaphoreType.DMA
     zc = NPIX // 2
     return pl.pallas_call(
         heads_backward_kernel,
         out_shape=(
-            jax.ShapeDtypeStruct((SEGS, SEG_ROWS, CIN), F32),
+            jax.ShapeDtypeStruct((3, 9, COLS, CIN), F32),
             jax.ShapeDtypeStruct((PX, CIN), F32),
             jax.ShapeDtypeStruct((8, 128), F32),
+            jax.ShapeDtypeStruct((NPIX, 3, 32, HID), BF),
+            jax.ShapeDtypeStruct((SMALL_PART, HID), F32),
+            jax.ShapeDtypeStruct((COLS, CIN), F32),
         ),
-        in_specs=[whole_vmem()] * 3,
-        out_specs=[whole_vmem()] * 3,
+        in_specs=[whole_vmem()] * 9 + [from_hbm()] + [whole_vmem()] * 2,
+        out_specs=[pl.BlockSpec(memory_space=pl.ANY)] + [whole_vmem()] * 5,
         scratch_shapes=[
+            pltpu.VMEM((4, 3 * HID, WIDTH), BF),
+            pltpu.VMEM((NCH, 3, NPIX, 32, HID), BF),
+            pltpu.VMEM((SMALL_ROWS, HID), F32),
+            pltpu.VMEM((4, 3 * HID, WIDTH), BF),
             pltpu.VMEM((NPIX, NCH, 4, COLS, WIDTH), BF),
             pltpu.VMEM((NPIX, NCH, 4, 32, WIDTH), BF),
-            pltpu.VMEM((SEG_ROWS, CIN), BF),
             pltpu.VMEM((3, CIN, (SEGS + 1) * WINDOW), BF),
             pltpu.VMEM((NPIX, SEGS * WINDOW, PX), BF),
             pltpu.VMEM((WINDOW, PX), BF),
@@ -1447,49 +1655,26 @@
             pltpu.VMEM((3, CIN, PX), BF),
             pltpu.VMEM((3, CIN, PX), BF),
             pltpu.VMEM((4, CIN, PX), BF),
-            pltpu.VMEM((3, CIN, PX), F32),
             pltpu.VMEM((6, 8, 128), F32),
-            pltpu.VMEM((NCH - 1, 6, 8, 128), F32),
-            pltpu.VMEM((NPIX - 1, 6, 8, 128), F32),
-            pltpu.VMEM((6, 8, 128), F32),
-            dma((1,)),
+            pltpu.VMEM((NALL, 8, 128), F32),
+            pltpu.VMEM((NCH, 3, NPIX, 32, HID), BF),
+            pltpu.VMEM((NCH, SMALL_PART, HID), F32),
+            pltpu.VMEM((SEGS, TAPS, 32, CIN), F32),
+            pltpu.VMEM((3, 32, CIN), F32),
+            pltpu.VMEM((NPIX, PX, CIN), BF),
+            dma((2,)), dma((9 * SEGS,)),
             dma((NPIX - 1,)), dma((NPIX - 1,)),
             dma((NPIX,)), dma((NPIX,)), dma((NPIX,)), dma((NPIX,)), dma((NPIX,)), dma((NPIX,)),
-            dma((len(MOVES),)), dma((NPIX,)), dma((3,)), dma((3,)), dma((1,)), dma((1,)),
+            dma((len(MOVES),)), dma((NPIX,)), dma((3,)), dma((3,)),
             dma((zc,)), dma((zc,)), dma((3,)), dma((3,)), dma((4,)), dma((4,)),
-            dma((NCH - 1,)), dma((NCH - 1,)),
-            dma((NPIX - 1,)), dma((NPIX - 1,)),
+            dma((NALL - 1,)), dma((NALL - 1,)),
+            dma((2, NCH - 1)), dma((2, NCH - 1)),
         ],
         compiler_params=pltpu.CompilerParams(
             collective_id=2, has_side_effects=True, vmem_limit_bytes=VMEM_LIMIT
         ),
         name="heads_backward",
-    )(dq, xall, w_seg)
-
-
-def tap_weights(head_weight, head_rates):
-    rates = head_rates.astype(BF)
-    pieces = []
-    for branch, first, step, reach, shifts in TAP_GROUPS:
-        if branch == 0:
-            pieces.append(jnp.transpose(head_weight.astype(BF))[None])
-        else:
-            pieces.append(rates[branch - 1, 3 * (step + 1) : 3 * (step + 2)])
-    taps = jnp.concatenate(pieces, axis=0)
-    taps = taps.reshape(TAPS, SEGS, 32, CIN).transpose(1, 0, 2, 3)
-    return taps.reshape(SEGS, SEG_ROWS, CIN)
-
-
-def tap_grads(dw):
-    taps = dw.reshape(SEGS, TAPS, 32, CIN).transpose(1, 0, 2, 3).reshape(TAPS, COLS, CIN)
-    at = {(group[0], group[2]): group[1] for group in TAP_GROUPS}
-    head = jnp.transpose(taps[at[(0, 0)]])
-    rates = []
-    for rate_index in range(3):
-        for step in (-1, 0, 1):
-            first = at.get((rate_index + 1, step))
-            rates.append(jnp.zeros((3, COLS, CIN), F32) if first is None else taps[first : first + 3])
-    return head, jnp.stack(rates).reshape(3, 9, COLS, CIN)
+    )(*operands)
 
 
 MID = M // NCH
@@ -1499,7 +1684,6 @@
 W_DILATED = slice(CIN, CIN + TAP_LANES)
 W_EXPAND = slice(CIN + TAP_LANES, 2 * CIN + TAP_LANES)
 W_LANES = 2 * CIN + TAP_LANES
-SMALL_ROWS = 80
 
 
 def slide_rows(tile, steps):
@@ -1518,10 +1702,11 @@
     return jnp.sum(values, axis=0, keepdims=True)
 
 
-def pix_copies(inbox, send_sem, recv_sem):
+def pix_copies(inbox, send_sem, recv_sem, rows=8):
     p, c = lax.axis_index("pix"), lax.axis_index("ch")
+    view = inbox.at[p] if rows == 8 else inbox.at[p, 0:rows]
     return [
-        remote(inbox.at[p], inbox.at[p], send_sem.at[d - 1], recv_sem.at[d - 1], (lax.rem(p + d, NPIX), c))
+        remote(view, view, send_sem.at[d - 1], recv_sem.at[d - 1], (lax.rem(p + d, NPIX), c))
         for d in range(1, NPIX)
     ]
 
@@ -1553,9 +1738,10 @@
 
 
 def block_forward_kernel(
-    x_ref, mask_ref, w_ref, proj_ref, narrow_ref, wide_ref,
-    out_ref, hat_one_ref, hat_two_ref, hat_three_ref, wall_ref, first_ref, second_ref, stats_ref, stats_wide_ref, wpt_ref,
-    work, ch_buf, ch_in, halo_buf, halo_in, stat_one, stat_two, stat_three,
+    x_ref, mask_ref, label_ref, reduce_ref, dilated_ref, expand_ref, head_proj_ref, norm_ref,
+    out_ref, hat_one_out, hat_two_out, hat_three_ref, wall_out, first_out, second_out, stats_ref, stats_wide_ref, wpt_ref,
+    hat_one_ref, hat_two_ref, wall_ref, first_ref, second_ref, out_sem,
+    w_ref, proj_ref, turned, mask_t, work, ch_buf, ch_in, halo_buf, halo_in, stat_one, stat_two, stat_three,
     local_sem, wz_send, wz_recv, wy_send, wy_recv, c_send, c_recv, s_send, s_recv, h_send, h_recv,
 ):
     p, c, z, y, x, core = place()
@@ -1563,7 +1749,22 @@
     other_y = (2 * z + 1 - y, c)
     pix_targets = [(lax.rem(p + d, NPIX), c) for d in range(1, NPIX)]
     ch_targets = [(p, lax.rem(c + d, NCH)) for d in range(1, NCH)]
-    greet(pix_targets + ch_targets)
+    greeted = greet(pix_targets + ch_targets)
+    w_ref[:, W_REDUCE] = reduce_ref[...].astype(BF)
+    for tap in range(9):
+        w_ref[:, CIN + tap * MID : CIN + (tap + 1) * MID] = dilated_ref[tap].astype(BF)
+    w_ref[:, W_EXPAND] = expand_ref[...].astype(BF)
+    for t in range(3):
+        turned[...] = jnp.transpose(head_proj_ref[t])
+        quarter = pl.ds(pl.multiple_of(c * (HID // NCH), HID // NCH), HID // NCH)
+        proj_ref[t] = turned[quarter, :].astype(BF)
+    mask_t[...] = jnp.zeros_like(mask_t)
+    mask_t[0:ROWS, :] = mask_ref[...].astype(F32)
+
+    def param(row, offset, width):
+        return norm_ref[row : row + 1, pl.ds(pl.multiple_of(offset + c * width, 128), width)]
+
+    await_greetings(greeted)
     parts = (pl.ds(0, CIN), pl.ds(CIN, TAP_LANES), pl.ds(CIN + TAP_LANES, CIN))
 
     def shard(part):
@@ -1588,10 +1789,12 @@
             src, spot(part, source), wy_send.at[part, d], wy_recv.at[part, d], other_y
         )
 
-    for part in range(4):
-        wy_copy(part, 0).start()
+    def send_z(part):
         for d in range(1, zcount):
             wz_copy(part, d).start()
+
+    wy_copy(0, 0).start()
+    send_z(0)
     own = pltpu.make_async_copy(w_ref, wall_ref.at[p], local_sem.at[0])
     own.start()
     own_proj = pltpu.make_async_copy(proj_ref, spot(3, p), local_sem.at[1])
@@ -1612,14 +1815,13 @@
         return wall_ref[:, :, lanes].reshape(M, lanes.stop - lanes.start)
 
     def stat_round(index, inbox, values):
-        if index > 0:
-            inbox[p] = jnp.zeros_like(inbox[p])
         inbox[p, 0:1, :] = column_sums(values)
         inbox[p, 1:2, :] = column_sums(values * values)
-        copies = pix_copies(inbox, s_send.at[index], s_recv.at[index])
+        rows = 8 if index == 0 else 2
+        copies = pix_copies(inbox, s_send.at[index], s_recv.at[index], rows)
         start_all(copies)
         wait_all(copies)
-        return add_up(inbox)
+        return add_up(inbox[:, 0:rows])
 
     count_all = float(NPIX * PX)
 
@@ -1630,7 +1832,9 @@
         return hat, hat * gain + shift, scale
 
     forward_part(0)
+    send_z(1)
     receive_part(0)
+    wy_copy(1, 0).start()
     for m in range(NCH):
         wanted = wall_ref[2 * m : 2 * m + 2, :, W_REDUCE].reshape(MID, CIN)
         value = nt_dot(x_ref[...], wanted)
@@ -1643,17 +1847,19 @@
     reduce_copies = ch_copies(lambda other: ch_buf.at[0, other], ch_in, c_send.at[0], c_recv.at[0])
     start_all(reduce_copies)
     wait_all(reduce_copies)
+    forward_part(1)
     reduced = work[...]
     for d in range(1, NCH):
         reduced = reduced + ch_in[lax.rem(c + d, NCH)].astype(F32)
     stat_one[p] = jnp.zeros((8, MID), F32)
-    stat_one[p, 2:3, :] = narrow_ref[4:5, :]
+    for t in range(3):
+        stat_one[p, 2 + t : 3 + t, :] = column_sums(label_ref[t].astype(F32))
     sums = stat_round(0, stat_one, reduced)
-    hat, normed, scale = norm_of(reduced, sums, narrow_ref[0:1, :], narrow_ref[1:2, :])
+    hat, normed, scale = norm_of(reduced, sums, param(0, 0, MID), param(1, 0, MID))
     hat_one_ref[...] = hat
     stats_ref[...] = jnp.zeros_like(stats_ref)
     stats_ref[0:1, :] = scale
-    stats_ref[2:3, :] = jnp.maximum(sums[2:3], 1.0)
+    stats_ref[2:5, :] = sums[2:5]
 
     def own_lanes():
         return pl.ds(pl.multiple_of(c * MID, MID), MID)
@@ -1669,12 +1875,17 @@
             )
         return copies
 
-    first_ref[:, own_lanes()] = (gelu_of(normed) * mask_ref[...]).astype(BF)
+    mask = jnp.transpose(mask_t[...])
+    mask = jnp.concatenate(
+        [jnp.broadcast_to(mask[:, r : r + 1], (WIDTH, MID)) for r in range(ROWS)], axis=0
+    )
+    first_ref[:, own_lanes()] = (gelu_of(normed) * mask).astype(BF)
     copies = gather_copies(first_ref, 1)
     start_all(copies)
-    forward_part(1)
+    send_z(2)
     wait_all(copies)
     receive_part(1)
+    wy_copy(2, 0).start()
 
     def row_part(step):
         total = jnp.zeros((PX, MID), F32)
@@ -1713,9 +1924,11 @@
         work[...] += halo_in[1].astype(F32)
 
     forward_part(2)
+    send_z(3)
+    wy_copy(3, 0).start()
     middle = work[...]
     sums = stat_round(1, stat_two, middle)
-    hat, normed, scale = norm_of(middle, sums, narrow_ref[2:3, :], narrow_ref[3:4, :])
+    hat, normed, scale = norm_of(middle, sums, param(0, M, MID), param(1, M, MID))
     hat_two_ref[...] = hat
     stats_ref[1:2, :] = scale
     second_ref[:, own_lanes()] = gelu_of(normed).astype(BF)
@@ -1726,13 +1939,24 @@
     receive_part(2)
     hat_three_ref[...] = nn_dot(second_ref[...], weights(W_EXPAND))
     expanded = hat_three_ref[...]
+    leaving = [
+        pltpu.make_async_copy(ref, out, out_sem.at[i])
+        for i, (ref, out) in enumerate(
+            (
+                (hat_one_ref, hat_one_out), (hat_two_ref, hat_two_out), (wall_ref, wall_out),
+                (first_ref, first_out), (second_ref, second_out),
+            )
+        )
+    ]
+    start_all(leaving)
     forward_part(3)
     sums = stat_round(2, stat_three, expanded)
-    hat, normed, scale = norm_of(expanded, sums, wide_ref[0:1, :], wide_ref[1:2, :])
+    hat, normed, scale = norm_of(expanded, sums, param(0, 2 * M, CIN), param(1, 2 * M, CIN))
     hat_three_ref[...] = hat
     stats_wide_ref[...] = jnp.broadcast_to(scale, stats_wide_ref.shape)
     out_ref[...] = gelu_of(normed + x_ref[...].astype(F32)).astype(BF)
     receive_part(3)
+    wait_all(leaving)
 
     for part in range(4):
         for d in range(zcount):
@@ -1749,7 +1973,7 @@
         halo_copy(1).wait_send()
 
 
-def block_forward(flat_in, mask, w_shard, proj_shard, narrow, wide):
+def block_forward(*operands):
     dma = pltpu.SemaphoreType.DMA
     zc = NPIX // 2
     shape = jax.ShapeDtypeStruct
@@ -1767,9 +1991,19 @@
             shape((8, CIN), F32),
             shape((3, HID // NCH, 4 * HID), BF),
         ),
-        in_specs=[whole_vmem()] * 6,
-        out_specs=[whole_vmem()] * 10,
+        in_specs=[whole_vmem()] * 8,
+        out_specs=[whole_vmem()] + [from_hbm()] * 2 + [whole_vmem()] + [from_hbm()] * 3 + [whole_vmem()] * 3,
         scratch_shapes=[
+            pltpu.VMEM((PX, MID), F32),
+            pltpu.VMEM((PX, MID), F32),
+            pltpu.VMEM((NPIX, WPART, W_LANES), BF),
+            pltpu.VMEM((PX, M), BF),
+            pltpu.VMEM((PX, M), BF),
+            dma((5,)),
+            pltpu.VMEM((WPART, W_LANES), BF),
+            pltpu.VMEM((3, HID // NCH, 128), BF),
+            pltpu.VMEM((HID, 128), F32),
+            pltpu.VMEM((8, WIDTH), F32),
             pltpu.VMEM((PX, MID), F32),
             pltpu.VMEM((1, NCH, PX, MID), BF),
             pltpu.VMEM((NCH, PX, MID), BF),
@@ -1785,89 +2019,129 @@
             dma((2,)), dma((2,)),
         ],
         compiler_params=pltpu.CompilerParams(
-            collective_id=0, has_side_effects=True, vmem_limit_bytes=VMEM_LIMIT
+            collective_id=0, has_side_effects=True, vmem_limit_bytes=BLOCK_VMEM
         ),
         name="block_forward",
-    )(flat_in, mask, w_shard, proj_shard, narrow, wide)
+    )(*operands)
 
 
 def block_backward_kernel(
-    gz_ref, x_ref, mask_ref, wall_ref, hat_one_ref, hat_two_ref, hat_three_ref, first_ref, second_ref,
-    narrow_ref, wide_ref, stats_ref, stats_wide_ref, dwp_ref, small_ref, square_ref,
-    ingrad_ref, wgrad_ref, pgrad_ref, sgrad_ref, ngrad_ref, ngrad_wide_ref, total_ref,
-    ds, ds_low, turned, ch_buf, ch_in, halo_in, taps, back_t, stat_three, stat_two, stat_one,
-    we_buf, we_in, wd_buf, wd_in, wr_buf, wr_in, pc_buf, pc_in, pr_buf, pr_in, pg_in,
-    small_ch, small_px, sq_ch, sq_px, norm_in, norm_wide_in,
-    c_send, c_recv, s_send, s_recv, h_send, h_recv, g_send, g_recv,
-    pc_send, pc_recv, pg_send, pg_recv, t_send, t_recv, u_send, u_recv, n_send, n_recv,
+    gz_hbm, x_hbm, mask_ref, wall_hbm, hat_one_hbm, hat_two_hbm, hat_three_hbm, first_hbm, second_hbm,
+    norm_ref, stats_ref, stats_wide_ref, proj_hbm, small_ref, square_ref,
+    ingrad_ref, wgrad_ref, pgrad_ref, sgrad_ref, ngrad_ref, total_ref,
+    gz_ref, x_ref, hat_three_ref, second_ref, first_ref, wall_ref, proj_ref, hat_two_ref, hat_one_ref, in_sem,
+    ds, ds_low, turned, ch_buf, ch_in, halo_in, taps, back_t, mask_t, stat_three, stat_two, stat_one,
+    we_buf, we_y, we_z, we_in, wd_buf, wd_y, wd_z, wd_in, wr_buf, wr_y, wr_z, wr_in, pr_in, pg_in,
+    small_px, sq_all, norm_in, norm_wide_in,
+    c_send, c_recv, s_send, s_recv, h_send, h_recv, gy_send, gy_recv, gz_send, gz_recv,
+    pr_send, pr_recv, pg_send, pg_recv, t_send, t_recv, u_send, u_recv, n_send, n_recv,
 ):
     p, c, z, y, x, core = place()
+    zcount = NPIX // 2
+    other_y = (2 * z + 1 - y, c)
     pix_targets = [(lax.rem(p + d, NPIX), c) for d in range(1, NPIX)]
     ch_targets = [(p, lax.rem(c + d, NCH)) for d in range(1, NCH)]
-    greet(pix_targets + ch_targets)
+    greeted = greet(all_targets())
+    coming = [
+        pltpu.make_async_copy(source, ref, in_sem.at[i])
+        for i, (source, ref) in enumerate(
+            (
+                (gz_hbm, gz_ref), (x_hbm, x_ref), (hat_three_hbm, hat_three_ref), (second_hbm, second_ref),
+                (first_hbm, first_ref), (wall_hbm, wall_ref), (proj_hbm, proj_ref), (hat_two_hbm, hat_two_ref),
+                (hat_one_hbm, hat_one_ref),
+            )
+        )
+    ]
+    start_all(coming)
     count_all = float(NPIX * PX)
+
+    def param(row, offset, width):
+        return norm_ref[row : row + 1, pl.ds(pl.multiple_of(offset + c * width, 128), width)]
+
+    gain_one, shift_one = param(0, 0, MID), param(1, 0, MID)
+    gain_two, shift_two = param(0, M, MID), param(1, M, MID)
+    gain_three, shift_three = param(0, 2 * M, CIN), param(1, 2 * M, CIN)
 
     def weights(lanes):
         return wall_ref[:, :, lanes].reshape(M, lanes.stop - lanes.start)
 
-    def own_lanes():
-        return pl.ds(pl.multiple_of(c * MID, MID), MID)
-
     def stat_round(index, inbox, upstream, hat):
-        inbox[p] = jnp.zeros_like(inbox[p])
         inbox[p, 0:1, :] = column_sums(upstream)
         inbox[p, 1:2, :] = column_sums(upstream * hat)
-        copies = pix_copies(inbox, s_send.at[index], s_recv.at[index])
+        copies = pix_copies(inbox, s_send.at[index], s_recv.at[index], 2)
         start_all(copies)
         return copies
 
     def stat_end(copies, inbox):
         wait_all(copies)
-        return add_up(inbox)
+        return add_up(inbox[:, 0:2])
 
     def norm_back(upstream, hat, sums, gain, scale):
         return gain * scale * (upstream - sums[0:1] / count_all - hat * (sums[1:2] / count_all))
 
     def own_ch_copies(ref, inbox_index):
+        return [
+            remote(
+                ref.at[c], ref.at[c], n_send.at[inbox_index, d - 1], n_recv.at[inbox_index, d - 1],
+                ch_targets[d - 1],
+            )
+            for d in range(1, NCH)
+        ]
+
+    def sum_y(index, buf, y_in):
+        return remote(buf.at[:, 1 - y], y_in, gy_send.at[index], gy_recv.at[index], other_y)
+
+    def sum_z(index, z_buf, z_in):
         copies = []
-        for d in range(1, NCH):
+        for d in range(1, zcount):
+            zz = lax.rem(z + d, zcount)
             copies.append(
-                remote(ref.at[c], ref.at[c], n_send.at[inbox_index, d - 1], n_recv.at[inbox_index, d - 1], ch_targets[d - 1])
+                remote(
+                    z_buf.at[zz], z_in.at[d - 1], gz_send.at[index, d - 1], gz_recv.at[index, d - 1],
+                    (2 * zz + y, c),
+                )
             )
         return copies
 
-    small_ch[c] = small_ref[...]
-    small_copies = own_ch_copies(small_ch, 0)
-    start_all(small_copies)
-
-    for other in range(NCH):
-        for t in range(3):
-            for b in range(NPIX):
-                start = b * 128 + other * 32
-                pc_buf[other, t, b] = dwp_ref[t, start : start + 32, :].astype(BF)
-    proj_copies = ch_copies(lambda other: pc_buf.at[other], pc_in, pc_send, pc_recv)
+    def sum_middle(index, buf, y_in, z_buf, z_in):
+        sum_y(index, buf, y_in).wait()
+        for zz in range(zcount):
+            z_buf[zz] = (buf[zz, y].astype(F32) + y_in[zz].astype(F32)).astype(BF)
+        start_all(sum_z(index, z_buf, z_in))
+
+    def sum_end(index, z_buf, z_in, lanes):
+        wait_all(sum_z(index, z_buf, z_in))
+        total = z_buf[z].astype(F32)
+        for d in range(zcount - 1):
+            total = total + z_in[d].astype(F32)
+        wgrad_ref[:, lanes] = total
+        return fold(total * total)
 
     wide_rows = 64
 
     def expand_rows(m, carry):
         rows = pl.ds(pl.multiple_of(m * wide_rows, wide_rows), wide_rows)
-        summed = hat_three_ref[rows, :] * wide_ref[0:1, :] + wide_ref[1:2, :] + x_ref[rows, :].astype(F32)
+        summed = hat_three_ref[rows, :] * gain_three + shift_three + x_ref[rows, :].astype(F32)
         ds[rows, :] = gz_ref[rows, :] * gelu_slope(summed)
         return carry
 
+    wait_all(coming[:3])
     lax.fori_loop(0, PX // wide_rows, expand_rows, 0)
+    await_greetings(greeted)
     copies = stat_round(0, stat_three, ds[...], hat_three_ref[...])
-    start_all(proj_copies)
+    wait_all(coming[3:])
     turned[0] = jnp.transpose(second_ref[...].astype(F32)).astype(BF)
     turned[1] = jnp.transpose(first_ref[...].astype(F32)).astype(BF)
+    mask_t[...] = jnp.zeros_like(mask_t)
+    mask_t[0:ROWS, :] = mask_ref[...].astype(F32)
     sums = stat_end(copies, stat_three)
-    norm_wide_in[c] = sums
-    ds_low[...] = norm_back(ds[...], hat_three_ref[...], sums, wide_ref[0:1, :], stats_wide_ref[0:1, :]).astype(BF)
+    norm_wide_in[c] = jnp.zeros((8, CIN), F32)
+    norm_wide_in[c, 0:2, :] = sums
+    ds_low[...] = norm_back(ds[...], hat_three_ref[...], sums, gain_three, stats_wide_ref[0:1, :]).astype(BF)
 
     def scatter_ch(index, product):
         for m in range(NCH):
-            value = product(m)
-            ch_buf[index, m] = value.astype(BF)
+            ch_buf[index, m] = product(m).astype(BF)
         copies = ch_copies(lambda other: ch_buf.at[index, other], ch_in.at[index], c_send.at[index], c_recv.at[index])
         start_all(copies)
         return copies
@@ -1879,44 +2153,34 @@
             total = total + ch_in[index, lax.rem(c + d, NCH)].astype(F32)
         return total
 
-    def grad_copies(index, buf, inbox):
-        copies = []
-        for d in range(1, NPIX):
-            b = lax.rem(p + d, NPIX)
-            copies.append(
-                remote(buf.at[b], inbox.at[d - 1], g_send.at[index, d - 1], g_recv.at[index, d - 1], (b, c))
-            )
-        return copies
-
     def expand_back(m):
         wanted = wall_ref[2 * m : 2 * m + 2, :, W_EXPAND].reshape(MID, CIN)
         return nt_dot(ds_low[...], wanted)
 
     copies = scatter_ch(0, expand_back)
-    we_buf[...] = nn_dot(turned[0], ds_low[...]).astype(BF).reshape(NPIX, WPART, CIN)
-    we_copies = grad_copies(0, we_buf, we_in)
-    start_all(we_copies)
+    proj_copies = []
+    for d in range(1, NPIX):
+        b = lax.rem(p + d, NPIX)
+        proj_copies.append(remote(proj_ref.at[b], pr_in.at[d - 1], pr_send.at[d - 1], pr_recv.at[d - 1], (b, c)))
+    start_all(proj_copies)
+    small_px[p] = small_ref[...]
+    small_copies = pix_copies(small_px, t_send, t_recv)
+    start_all(small_copies)
+    we_buf[...] = nn_dot(turned[0], ds_low[...]).astype(BF).reshape(zcount, 2, WPART, CIN)
+    sum_y(0, we_buf, we_y).start()
     hat = hat_two_ref[...]
-    slope = gelu_slope(hat * narrow_ref[2:3, :] + narrow_ref[3:4, :])
+    slope = gelu_slope(hat * gain_two + shift_two)
     upstream = scatter_end(0, copies) * slope
     copies = stat_round(1, stat_two, upstream, hat)
-    wait_all(proj_copies)
-    for t in range(3):
-        total = pc_buf[c, t].astype(F32)
-        for d in range(1, NCH):
-            total = total + pc_in[lax.rem(c + d, NCH), t].astype(F32)
-        pr_buf[:, t] = total.astype(BF)
-    wait_all(small_copies)
-    small_px[p] = add_up(small_ch)
     sums = stat_end(copies, stat_two)
     norm_in[c, 2:4, :] = sums[0:2]
 
     def halo_copy(side):
         target = (p - 1, c) if side == 0 else (p + 1, c)
-        return remote(back_t.at[0], halo_in.at[side], h_send.at[side], h_recv.at[side], target)
-
-    gradient = norm_back(upstream, hat, sums, narrow_ref[2:3, :], stats_ref[1:2, :])
-    back_t[0] = gradient.astype(BF)
+        return remote(back_t, halo_in.at[side], h_send.at[side], h_recv.at[side], target)
+
+    gradient = norm_back(upstream, hat, sums, gain_two, stats_ref[1:2, :])
+    back_t[...] = gradient.astype(BF)
 
     @pl.when(p > 0)
     def _():
@@ -1932,7 +2196,7 @@
             moved = slide_rows(source.astype(F32), DILATION_RATE * (col - 1))
             taps[:, tap * MID : (tap + 1) * MID] = moved.astype(BF)
 
-    fill_taps(0, back_t[0])
+    fill_taps(0, back_t[...])
 
     @pl.when(p < NPIX - 1)
     def _():
@@ -1959,25 +2223,22 @@
         return nt_dot(taps[...], wanted)
 
     copies = scatter_ch(1, dilated_back)
-    proj_rows = grad_copies(3, pr_buf, pr_in)
-    start_all(proj_rows)
+    sum_middle(0, we_buf, we_y, we_z, we_in)
     for m in range(NPIX):
-        wd_buf[m] = nn_dot(turned[1, m * WPART : (m + 1) * WPART, :], taps[...]).astype(BF)
-    wd_copies = grad_copies(1, wd_buf, wd_in)
-    start_all(wd_copies)
+        wd_buf[m // 2, m % 2] = nn_dot(turned[1, m * WPART : (m + 1) * WPART, :], taps[...]).astype(BF)
+    sum_y(1, wd_buf, wd_y).start()
     hat = hat_one_ref[...]
-    slope = gelu_slope(hat * narrow_ref[0:1, :] + narrow_ref[1:2, :]) * mask_ref[...]
+    mask = jnp.transpose(mask_t[...])
+    mask = jnp.concatenate(
+        [jnp.broadcast_to(mask[:, r : r + 1], (WIDTH, MID)) for r in range(ROWS)], axis=0
+    )
+    slope = gelu_slope(hat * gain_one + shift_one) * mask
     upstream = scatter_end(1, copies) * slope
     copies = stat_round(2, stat_one, upstream, hat)
-    small_rows = [
-        remote(small_px.at[p], small_px.at[p], t_send.at[d - 1], t_recv.at[d - 1], pix_targets[d - 1])
-        for d in range(1, NPIX)
-    ]
-    start_all(small_rows)
     sums = stat_end(copies, stat_one)
     norm_in[c, 0:2, :] = sums[0:2]
     norm_in[c, 4:8, :] = jnp.zeros((4, MID), F32)
-    gradient = norm_back(upstream, hat, sums, narrow_ref[0:1, :], stats_ref[0:1, :])
+    gradient = norm_back(upstream, hat, sums, gain_one, stats_ref[0:1, :])
 
     own_rows = pl.ds(pl.multiple_of(c * MID, MID), MID)
     turned[2, own_rows, :] = jnp.transpose(gradient).astype(BF)
@@ -1989,68 +2250,57 @@
         for d in range(1, NCH)
     ]
     start_all(copies)
-    norm_copies = own_ch_copies(norm_in, 1) + own_ch_copies(norm_wide_in, 2)
+    norm_copies = own_ch_copies(norm_in, 0) + own_ch_copies(norm_wide_in, 1)
     start_all(norm_copies)
+    sum_middle(1, wd_buf, wd_y, wd_z, wd_in)
     wait_all(copies)
-    wr_buf[...] = nn_dot(turned[2], x_ref[...]).astype(BF).reshape(NPIX, WPART, CIN)
-    wr_copies = grad_copies(2, wr_buf, wr_in)
-    start_all(wr_copies)
-    full = jnp.transpose(turned[2].astype(F32)).astype(BF)
-    ingrad_ref[...] = nn_dot(full, weights(W_REDUCE)) + ds[...]
-    wait_all(proj_rows)
+    wr_buf[...] = nn_dot(turned[2], x_ref[...]).astype(BF).reshape(zcount, 2, WPART, CIN)
+    sum_y(2, wr_buf, wr_y).start()
+    wait_all(proj_copies)
     for t in range(3):
-        total = pr_buf[p, t].astype(F32)
+        total = proj_ref[p, t].astype(F32)
         for d in range(NPIX - 1):
             total = total + pr_in[d, t].astype(F32)
         pg_in[c, t] = total
-    pg_copies = [
-        remote(pg_in.at[c], pg_in.at[c], pg_send.at[d - 1], pg_recv.at[d - 1], ch_targets[d - 1])
+    wait_all(small_copies)
+    sgrad_ref[c] = add_up(small_px)
+    ch_final = [
+        remote(pg_in.at[c], pg_in.at[c], pg_send.at[0, d - 1], pg_recv.at[0, d - 1], ch_targets[d - 1])
+        for d in range(1, NCH)
+    ] + [
+        remote(sgrad_ref.at[c], sgrad_ref.at[c], pg_send.at[1, d - 1], pg_recv.at[1, d - 1], ch_targets[d - 1])
         for d in range(1, NCH)
     ]
-    start_all(pg_copies)
-
-    def grad_end(copies, buf, inbox, lanes):
-        wait_all(copies)
-        total = buf[p].astype(F32)
-        for d in range(NPIX - 1):
-            total = total + inbox[d].astype(F32)
-        wgrad_ref[:, lanes] = total
-        return fold(total * total)
-
-    squares = square_ref[...] + grad_end(we_copies, we_buf, we_in, W_EXPAND)
-    squares = squares + grad_end(wd_copies, wd_buf, wd_in, W_DILATED)
-    wait_all(pg_copies)
+    start_all(ch_final)
+    sum_middle(2, wr_buf, wr_y, wr_z, wr_in)
+    full = jnp.transpose(turned[2].astype(F32)).astype(BF)
+    ingrad_ref[...] = nn_dot(full, weights(W_REDUCE)) + ds[...]
+    squares = square_ref[...] + sum_end(0, we_z, we_in, W_EXPAND)
+    squares = squares + sum_end(1, wd_z, wd_in, W_DILATED)
+    wait_all(ch_final)
     for t in range(3):
         for other in range(NCH):
             pgrad_ref[t, other * 32 : (other + 1) * 32, :] = pg_in[other, t]
         squares = squares + fold(pg_in[c, t] * pg_in[c, t])
-    wait_all(small_rows)
-    sgrad_ref[...] = add_up(small_px)
     wait_all(norm_copies)
-    ngrad_ref[...] = norm_in[...]
-    ngrad_wide_ref[...] = norm_wide_in[...]
-    shared = fold(sgrad_ref[...] * sgrad_ref[...])
     for other in range(NCH):
+        for row in range(2):
+            for offset, width, value in (
+                (0, MID, norm_in[other, 1 - row : 2 - row, :]),
+                (M, MID, norm_in[other, 3 - row : 4 - row, :]),
+                (2 * M, CIN, norm_wide_in[other, 1 - row : 2 - row, :]),
+            ):
+                start = offset + other * width
+                ngrad_ref[row : row + 1, start : start + width] = value
+    shared = jnp.zeros((8, 128), F32)
+    for other in range(NCH):
+        shared = shared + fold(sgrad_ref[other] * sgrad_ref[other])
         shared = shared + fold(norm_in[other] * norm_in[other])
-        piece = norm_wide_in[other]
-        shared = shared + fold(piece * piece)
-    squares = squares + grad_end(wr_copies, wr_buf, wr_in, W_REDUCE)
-    sq_ch[c] = squares
-    copies = [
-        remote(sq_ch.at[c], sq_ch.at[c], u_send.at[0, d - 1], u_recv.at[0, d - 1], ch_targets[d - 1])
-        for d in range(1, NCH)
-    ]
-    start_all(copies)
-    wait_all(copies)
-    sq_px[p] = add_up(sq_ch)
-    copies = [
-        remote(sq_px.at[p], sq_px.at[p], u_send.at[1, d - 1], u_recv.at[1, d - 1], pix_targets[d - 1])
-        for d in range(1, NPIX)
-    ]
-    start_all(copies)
-    wait_all(copies)
-    everything = add_up(sq_px) + shared
-    total = jnp.sum(jnp.sum(everything, axis=0, keepdims=True), axis=1, keepdims=True)
+        shared = shared + fold(norm_wide_in[other] * norm_wide_in[other])
+    squares = squares + sum_end(2, wr_z, wr_in, W_REDUCE)
+    summed = sum_everywhere(column_sums(squares), sq_all, u_send, u_recv)
+    everything = summed + column_sums(shared)
+    total = jnp.sum(everything, axis=1, keepdims=True)
     norm = jnp.sqrt(total)
     factor = jnp.minimum(1.0, CLIP_NORM / (norm + 1e-06))
     line = lax.broadcasted_iota(jnp.int32, (8, 128), 0)
@@ -2069,20 +2319,39 @@
     dma = pltpu.SemaphoreType.DMA
     shape = jax.ShapeDtypeStruct
     vmem = pltpu.VMEM
+    zc = NPIX // 2
+
+    def sum_buffers(lanes):
+        return [
+            vmem((zc, 2, WPART, lanes), BF),
+            vmem((zc, WPART, lanes), BF),
+            vmem((zc, WPART, lanes), BF),
+            vmem((zc - 1, WPART, lanes), BF),
+        ]
+
     return pl.pallas_call(
         block_backward_kernel,
         out_shape=(
             shape((PX, CIN), F32),
             shape((WPART, W_LANES), F32),
             shape((3, 128, HID), F32),
-            shape((SMALL_ROWS, 128), F32),
-            shape((NCH, 8, MID), F32),
-            shape((NCH, 8, CIN), F32),
+            shape((NCH, SMALL_PART, HID), F32),
+            shape((2, 2 * M + C), F32),
             shape((8, 128), F32),
         ),
-        in_specs=[whole_vmem()] * 16,
-        out_specs=[whole_vmem()] * 7,
+        in_specs=[from_hbm()] * 2 + [whole_vmem()] + [from_hbm()] * 6 + [whole_vmem()] * 3 + [from_hbm()] + [whole_vmem()] * 2,
+        out_specs=[whole_vmem()] * 6,
         scratch_shapes=[
+            vmem((PX, CIN), F32),
+            vmem((PX, CIN), BF),
+            vmem((PX, CIN), F32),
+            vmem((PX, M), BF),
+            vmem((PX, M), BF),
+            vmem((NPIX, WPART, W_LANES), BF),
+            vmem((NPIX, 3, 32, HID), BF),
+            vmem((PX, MID), F32),
+            vmem((PX, MID), F32),
+            dma((9,)),
             vmem((PX, CIN), F32),
             vmem((PX, CIN), BF),
             vmem((3, M, PX), BF),
@@ -2090,42 +2359,91 @@
             vmem((2, NCH, PX, MID), BF),
             vmem((2, PX, MID), BF),
             vmem((PX, TAP_LANES), BF),
-            vmem((1, PX, MID), BF),
+            vmem((PX, MID), BF),
+            vmem((8, WIDTH), F32),
             vmem((NPIX, 8, CIN), F32),
             vmem((NPIX, 8, MID), F32),
             vmem((NPIX, 8, MID), F32),
-            vmem((NPIX, WPART, CIN), BF),
-            vmem((NPIX - 1, WPART, CIN), BF),
-            vmem((NPIX, WPART, TAP_LANES), BF),
-            vmem((NPIX - 1, WPART, TAP_LANES), BF),
-            vmem((NPIX, WPART, CIN), BF),
-            vmem((NPIX - 1, WPART, CIN), BF),
-            vmem((NCH, 3, NPIX, 32, HID), BF),
-            vmem((NCH, 3, NPIX, 32, HID), BF),
-            vmem((NPIX, 3, 32, HID), BF),
+        ]
+        + sum_buffers(CIN)
+        + sum_buffers(TAP_LANES)
+        + sum_buffers(CIN)
+        + [
             vmem((NPIX - 1, 3, 32, HID), BF),
             vmem((NCH, 3, 32, HID), F32),
-            vmem((NCH, SMALL_ROWS, 128), F32),
-            vmem((NPIX, SMALL_ROWS, 128), F32),
-            vmem((NCH, 8, 128), F32),
-            vmem((NPIX, 8, 128), F32),
+            vmem((NPIX, SMALL_PART, HID), F32),
+            vmem((NALL, 8, 128), F32),
             vmem((NCH, 8, MID), F32),
             vmem((NCH, 8, CIN), F32),
             dma((3, NCH - 1)), dma((3, NCH - 1)),
             dma((3, NPIX - 1)), dma((3, NPIX - 1)),
             dma((2,)), dma((2,)),
-            dma((4, NPIX - 1)), dma((4, NPIX - 1)),
-            dma((NCH - 1,)), dma((NCH - 1,)),
-            dma((NCH - 1,)), dma((NCH - 1,)),
+            dma((3,)), dma((3,)), dma((3, zc - 1)), dma((3, zc - 1)),
             dma((NPIX - 1,)), dma((NPIX - 1,)),
-            dma((2, NPIX - 1)), dma((2, NPIX - 1)),
-            dma((3, NCH - 1)), dma((3, NCH - 1)),
+            dma((2, NCH - 1)), dma((2, NCH - 1)),
+            dma((NPIX - 1,)), dma((NPIX - 1,)),
+            dma((NALL - 1,)), dma((NALL - 1,)),
+            dma((2, NCH - 1)), dma((2, NCH - 1)),
         ],
         compiler_params=pltpu.CompilerParams(
-            collective_id=3, has_side_effects=True, vmem_limit_bytes=VMEM_LIMIT
+            collective_id=3, has_side_effects=True, vmem_limit_bytes=BLOCK_VMEM
         ),
         name="block_backward",
     )(*operands)
+
+
+def adam_parts(weight, first, second, grad, rate=RATE_MATRIX, decay=DECAY):
+    first_new = BETA_ONE * first + (1.0 - BETA_ONE) * grad
+    second_new = BETA_TWO * second + (1.0 - BETA_TWO) * grad * grad
+    first_hat = first_new * (1.0 / (1.0 - BETA_ONE**STEP))
+    second_hat = second_new * (1.0 / (1.0 - BETA_TWO**STEP))
+    weight_new = weight - rate * (first_hat / (jnp.sqrt(second_hat) + ADAM_EPS) + decay * weight)
+    return weight_new, first_new, second_new
+
+
+def adam_store(olds, news, at, grad):
+    weight, first, second = adam_parts(olds[0][at], olds[1][at], olds[2][at], grad)
+    news[0][at] = weight
+    news[1][at] = first
+    news[2][at] = second
+    news[3][at] = weight.astype(BF)
+
+
+def adam_matrices_kernel(*refs):
+    total_ref, w_ref, tap_ref, p_ref, n_ref = refs[:5]
+    olds = [refs[5 + 3 * i : 8 + 3 * i] for i in range(6)]
+    news = [refs[23 + 4 * i : 27 + 4 * i] for i in range(6)]
+    factor = total_ref[1:2, 0:1]
+    every = (slice(None), slice(None))
+    adam_store(olds[0], news[0], every, w_ref[:, W_REDUCE] * factor)
+    for tap in range(9):
+        lanes = slice(CIN + tap * MID, CIN + (tap + 1) * MID)
+        adam_store(olds[1], news[1], (tap, slice(None), slice(None)), w_ref[:, lanes] * factor)
+    adam_store(olds[2], news[2], every, w_ref[:, W_EXPAND] * factor)
+    adam_store(olds[3], news[3], every, tap_ref[...] * factor)
+    for t in range(3):
+        adam_store(olds[4], news[4], (t, slice(None), slice(None)), p_ref[t] * factor)
+    values = adam_parts(
+        olds[5][0][...], olds[5][1][...], olds[5][2][...], n_ref[...] * factor, RATE_SMALL, 0.0
+    )
+    for ref, value in zip(news[5], values):
+        ref[...] = value
+
+
+def adam_matrices(totals, w_grad, tap_grad, proj_grad, norm_grad, states):
+    flat = [array for state in states for array in state]
+    outs = []
+    for state in states[:5]:
+        outs += [jax.ShapeDtypeStruct(state[0].shape, F32)] * 3 + [jax.ShapeDtypeStruct(state[0].shape, BF)]
+    outs += [jax.ShapeDtypeStruct(states[5][0].shape, F32)] * 3
+    return pl.pallas_call(
+        adam_matrices_kernel,
+        out_shape=tuple(outs),
+        in_specs=[whole_vmem()] * (5 + len(flat)),
+        out_specs=[whole_vmem()] * len(outs),
+        compiler_params=pltpu.CompilerParams(vmem_limit_bytes=VMEM_LIMIT),
+        name="adam_matrices",
+    )(totals, w_grad, tap_grad, proj_grad, norm_grad, *flat)
 
 
 def per_device_rows(
@@ -2161,141 +2479,97 @@
     small_v,
 ):
 
-    block_id = lax.axis_index("ch")
     flat_in = features.reshape(PX, CIN)
-    mask_column = valid_mask.reshape(PX, 1).astype(F32)
-    gains = norm_params[0]
-    shifts = norm_params[1]
-
-    def owned(vector, offset, width):
-        return lax.dynamic_slice_in_dim(vector, offset + block_id * width, width)
-
-    def own_row(array, axis):
-        return lax.dynamic_slice_in_dim(array, block_id, 1, axis=axis)
-
-    w_shard = jnp.concatenate(
-        [w_reduce.T, w_dilated.transpose(1, 0, 2).reshape(WPART, TAP_LANES), w_expand], axis=1
-    ).astype(BF)
-    w_seg = tap_weights(head_weight, head_rates)
-    local_counts = jnp.sum(label_mask.astype(F32), axis=(1, 2))
-    narrow = jnp.stack(
+    shared, hat_one, hat_two, hat_three, w_all, first, second, stats, stats_wide, proj_own = block_forward(
+        flat_in, valid_mask, label_mask, w_reduce.T, w_dilated, w_expand, head_proj, norm_params
+    )
+    q_rows, shared_all, proj_t, w_seg, w_more = heads_forward(shared, head_rates, head_weight.T, proj_own)
+    at_out = 15 * HID
+    rest = at_out + HID * NCLS
+    small_cols = jnp.concatenate(
         [
-            owned(gains, 0, MID),
-            owned(shifts, 0, MID),
-            owned(gains, M, MID),
-            owned(shifts, M, MID),
-            jnp.pad(local_counts, (0, MID - 3)),
-        ]
-        + [jnp.zeros((MID,), F32)] * 3
-    )
-    wide = jnp.stack([owned(gains, 2 * M, CIN), owned(shifts, 2 * M, CIN)] + [jnp.zeros((CIN,), F32)] * 6)
-    proj_shard_t = jnp.transpose(
-        lax.dynamic_slice_in_dim(head_proj, block_id * (HID // NCH), HID // NCH, axis=2), (0, 2, 1)
-    ).astype(BF)
-    shared, hat_one, hat_two, hat_three, w_all, first, second, stats, stats_wide, proj_own = block_forward(
-        flat_in, mask_column, w_shard, proj_shard_t, narrow, wide
-    )
-    branch_bias, proj_bias, sem_w, depth_w, normal_w, sem_b, depth_b, normal_b = unpack_small(
-        head_small
-    )
-    out_stack = jnp.stack(
-        [jnp.pad(weight.astype(BF), ((0, 0), (0, 32 - weight.shape[1]))) for weight in (sem_w, depth_w, normal_w)]
-    )
-    out_bias = jnp.stack(
-        [jnp.pad(bias, (0, 32 - bias.shape[0])) for bias in (sem_b, depth_b, normal_b)], axis=1
-    )
-    q_rows, shared_all, proj_t = heads_forward(shared, w_seg, proj_own)
-    targets = jnp.concatenate([own_row(depth_target, 0), own_row(normal_target, 1)[:, 0]], axis=0)
-    pre_grad, proj_part, out_grad, bias_rows, out_bias_rows = heads_middle(
-        q_rows,
-        branch_bias.T,
-        proj_bias.T,
-        proj_t,
-        out_stack,
-        out_bias,
-        own_row(sem_label, 0),
-        targets,
-        own_row(label_mask, 1)[:, 0].astype(F32),
-        jnp.broadcast_to(stats[2, :3][:, None], (3, WIDTH)),
-    )
-    small_term = pack_small(
-        [bias_rows[:4, 0], bias_rows[4, 0]]
-        + [out_grad[0, :NCLS].T, out_grad[1, :1].T, out_grad[2, :3].T]
-        + [out_bias_rows[0, 0, :NCLS], out_bias_rows[1, 0, :1], out_bias_rows[2, 0, :3]]
-    )
-    small_count = small_term.shape[0]
-    small_term = jnp.pad(small_term, (0, SMALL_ROWS * 128 - small_count)).reshape(SMALL_ROWS, 128)
-    tap_sums, combined, squares = heads_backward(pre_grad, shared_all, w_seg)
-    head_shard, rates_shard = tap_grads(tap_sums)
-    input_grad, w_grad, proj_shard, small_sum, norm_narrow, norm_wide, totals = block_backward(
-        combined, flat_in, mask_column, w_all, hat_one, hat_two, hat_three, first, second,
-        narrow, wide, stats, stats_wide, proj_part, small_term, squares,
-    )
-    reduce_shard = w_grad[:, W_REDUCE].T
-    dilated_shard = w_grad[:, W_DILATED].reshape(WPART, 9, MID).transpose(1, 0, 2)
-    expand_shard = w_grad[:, W_EXPAND]
-    small_grad = small_sum.reshape(-1)[:small_count]
-    norm_grad = jnp.stack(
+            head_small[at_out:rest].reshape(HID, NCLS),
+            head_small[rest : rest + HID].reshape(HID, 1),
+            head_small[rest + HID : rest + 4 * HID].reshape(HID, 3),
+            jnp.zeros((HID, 32 - NCLS - 4), F32),
+        ],
+        axis=1,
+    )
+    out_bias = jnp.pad(head_small[rest + 4 * HID :], (0, HID - NCLS - 4))
+    small_rows = jnp.concatenate([head_small[:at_out], out_bias]).reshape(16, HID)
+    rates_shard, combined, squares, proj_sums, small_sums, root_sums = heads_backward(
+        q_rows, proj_t, small_rows, small_cols, stats, sem_label, depth_target, normal_target, label_mask,
+        shared_all, w_seg, w_more,
+    )
+    input_grad, w_grad, proj_shard, small_total, norm_grad, totals = block_backward(
+        combined, flat_in, valid_mask, w_all, hat_one, hat_two, hat_three, first, second,
+        norm_params, stats, stats_wide, proj_sums, small_sums, squares,
+    )
+    (
+        reduce_new, reduce_first, reduce_second, reduce_copy,
+        dilated_new, dilated_first, dilated_second, dilated_copy,
+        expand_new, expand_first, expand_second, expand_copy,
+        head_new, head_first, head_second, head_copy,
+        proj_new, proj_first, proj_second, proj_copy,
+        norm_new, norm_first, norm_second,
+    ) = adam_matrices(
+        totals, w_grad, root_sums, proj_shard, norm_grad,
+        (
+            (w_reduce.T, m_reduce.T, v_reduce.T),
+            (w_dilated, m_dilated, v_dilated),
+            (w_expand, m_expand, v_expand),
+            (head_weight.T, m_head.T, v_head.T),
+            (head_proj, m_proj, v_proj),
+            (norm_params, norm_m, norm_v),
+        ),
+    )
+    small_total = small_total.reshape(SMALL_ROWS, HID)
+    small_grad = jnp.concatenate(
         [
-            jnp.concatenate([norm_narrow[:, 1].reshape(-1), norm_narrow[:, 3].reshape(-1), norm_wide[:, 1].reshape(-1)]),
-            jnp.concatenate([norm_narrow[:, 0].reshape(-1), norm_narrow[:, 2].reshape(-1), norm_wide[:, 0].reshape(-1)]),
+            small_total[:15].reshape(-1),
+            small_total[16 : 16 + NCLS].T.reshape(-1),
+            small_total[16 + NCLS],
+            small_total[17 + NCLS : 20 + NCLS].T.reshape(-1),
+            small_total[15, : NCLS + 4],
         ]
     )
     grad_norm = totals[0, 0]
     factor = totals[1, 0]
-    reduce_new, reduce_first, reduce_second = adam_step(
-        w_reduce, m_reduce, v_reduce, reduce_shard * factor, RATE_MATRIX, DECAY
-    )
-    dilated_new, dilated_first, dilated_second = adam_step(
-        w_dilated, m_dilated, v_dilated, dilated_shard * factor, RATE_MATRIX, DECAY
-    )
-    expand_new, expand_first, expand_second = adam_step(
-        w_expand, m_expand, v_expand, expand_shard * factor, RATE_MATRIX, DECAY
-    )
-    head_new, head_first, head_second = adam_step(
-        head_weight, m_head, v_head, head_shard * factor, RATE_MATRIX, DECAY
-    )
     rates_new, rates_first, rates_second = adam_step(
         head_rates, m_rates, v_rates, rates_shard * factor, RATE_MATRIX, DECAY
     )
-    proj_new, proj_first, proj_second = adam_step(
-        head_proj, m_proj, v_proj, proj_shard * factor, RATE_MATRIX, DECAY
-    )
-    norm_new, norm_first, norm_second = adam_step(
-        norm_params, norm_m, norm_v, norm_grad * factor, RATE_SMALL, 0.0
-    )
     small_new, small_first, small_second = adam_step(
         head_small, small_m, small_v, small_grad * factor, RATE_SMALL, 0.0
     )
-    depth_bias_grad = small_grad[small_count - 4]
+    depth_bias_grad = small_total[15, NCLS]
     return (
         shared.reshape(ROWS, WIDTH, CIN),
         input_grad.reshape(ROWS, WIDTH, CIN),
         grad_norm,
-        reduce_new,
-        reduce_first,
-        reduce_second,
-        reduce_new.astype(jnp.bfloat16),
+        reduce_new.T,
+        reduce_first.T,
+        reduce_second.T,
+        reduce_copy.T,
         dilated_new,
         dilated_first,
         dilated_second,
-        dilated_new.astype(jnp.bfloat16),
+        dilated_copy,
         expand_new,
         expand_first,
         expand_second,
-        expand_new.astype(jnp.bfloat16),
-        head_new,
-        head_first,
-        head_second,
-        head_new.astype(jnp.bfloat16),
+        expand_copy,
+        head_new.T,
+        head_first.T,
+        head_second.T,
+        head_copy.T,
         rates_new,
         rates_first,
         rates_second,
-        rates_new.astype(jnp.bfloat16),
+        rates_new.astype(BF),
         proj_new,
         proj_first,
         proj_second,
-        proj_new.astype(jnp.bfloat16),
+        proj_copy,
         norm_new,
         norm_first,
         norm_second,

time: 505 us -> 394 us (0.78)
  Pallas kernels: 431 us -> 367 us
  local copies, waits for them, and re-layouts: 33.4 us -> 9.79 us
  other arithmetic: 37.9 us -> 15.7 us
    pallas_call x1, Pallas kernels: 117 us -> 77.4 us  [block_backward(): pl.pallas_call(block_backward_kernel, out_shape=(shape((PX, CIN), F32), s...]
    convert_element_type x10 -> x1, other arithmetic: 26.3 us -> 13.6 us  [per_device_rows(): rates_new.astype(BF)]
    pallas_call x1, Pallas kernels: 98.4 us -> 87.5 us  [heads_forward(): pl.pallas_call(heads_forward_kernel, out_shape=(jax.ShapeDtypeStruct((4,...]
    pallas_call x2, Pallas kernels: 138 us -> 129 us  [the longest x1 124 us: heads_backward(): pl.pallas_call(heads_backward_kernel, out_shape=(jax.ShapeDtypeStruct((3,...]
where the time goes in v4:
time: 394 us
  Pallas kernels  367 us (93%)
  other arithmetic  15.7 us (4%)
  local copies, waits for them, and re-layouts  9.79 us (2%)
    pallas_call x1, Pallas kernels, heads_backward(): pl.pallas_call(heads_backward_kernel, out_shape=(jax.ShapeDtypeStruct((3,...  124 us
    pallas_call x1, Pallas kernels, heads_forward(): pl.pallas_call(heads_forward_kernel, out_shape=(jax.ShapeDtypeStruct((4,...  87.5 us
    pallas_call x1, Pallas kernels, block_backward(): pl.pallas_call(block_backward_kernel, out_shape=(shape((PX, CIN), F32), s...  77.4 us
    pallas_call x1, Pallas kernels, block_forward(): pl.pallas_call(block_forward_kernel, out_shape=(shape((PX, CIN), BF), sha...  73.4 us
    convert_element_type x1, other arithmetic, per_device_rows(): rates_new.astype(BF)  13.6 us

profile of v4, /device:TPU:0, one launch (start us, length us, event | category | flops | bytes accessed | tf_op | source)
XLA Modules:
  0.0 393.5 jit_solution(4441512101720772829)
XLA Ops:
  0.7 73.4 %block_forward.1 = (bf16[512,512]{1,0:T(8,128)(2,1)}, f32[512,128]{1,0:T(8,128)}, f32[512,128]{1,0:T(8,128)}, f32[512,512]{1,0:T(8,128)}, bf16[8,64,2176]{2,1,0:...) custom-call(bf16[512,512]{1,0:T(8,128)(2,1)} %bitcast.31, ...), custom_call_target="tpu_custom_call" | custom-call | tf_op jit(solution)/shard_map/block_forward/pallas_call | solution.py:1980
  74.1 87.5 %heads_forward.1 = (bf16[4,768,128]{2,1,0:T(8,128)(2,1)}, bf16[8,512,512]{2,1,0:T(8,128)(2,1)}, bf16[4,3,64,1024]{3,2,1,0:T(8,128)(2,1)}, bf16[3,704,512]{2,1,0:T(8,128)(2,1)}, bf16[704,512]{1,0:T(8,128)(2,1)}) custom-call(bf16[512,512]{1,0:T(8,128)(2,1)} %get-tuple-element.84.x_ref, f32[3,9,96,512]{3,2,1,0:T(8,128)} %rates_hbm.1, f32[96,512]{1,0:T(8,128)} %bitcast.35, ...), custom_call_target="tpu_custom_call" | custom-call | tf_op jit(solution)/shard_map/heads_forward/pallas_call | solution.py:1051
  161.7 0.2 reshape.104
  161.9 0.2 reshape.106
  162.1 0.1 copy.72
  162.3 0.8 maximum_maximum_fusion.cols_ref
  163.1 0.6 reshape.103.small_ref
  163.7 124.1 %heads_backward.1 = (f32[3,9,96,512]{3,2,1,0:T(8,128)}, f32[512,512]{1,0:T(8,128)}, f32[8,128]{1,0:T(8,128)}, bf16[8,3,32,256]{3,2,1,0:T(8,128)(2,1)}, f32[16,256]{1,0:T(8,128)}, /*index=5*/f32[96,512]{1,0:T(8,128)}) custom-call(bf16[4,768,128]{2,1,0:T(8,128)(2,1)} %get-tuple-element.86.q_ref, bf16[4,3,64,1024]{3,2,1,0:T(8,128)(2,1)} %get-tuple-element.87.wpt_ref, ...), custom_call_target="tpu_custom_call" | custom-call | tf_op jit(solution)/shard_map/heads_backward/pallas_call | solution.py:1631
  287.9 77.4 %block_backward.1 = (f32[512,512]{1,0:T(8,128)}, f32[64,2176]{1,0:T(8,128)}, f32[3,128,256]{2,1,0:T(8,128)}, f32[4,16,256]{2,1,0:T(8,128)}, f32[2,3072]{1,0:T(2,128)}, /*index=5*/f32[8,128]{1,0:T(8,128)}) custom-call(f32[512,512]{1,0:T(8,128)} %get-tuple-element.92.gz_hbm, bf16[512,512]{1,0:T(8,128)(2,1)} %bitcast.32, s32[4,128]{1,0:T(4,128)} %mask_ref.5, ...), custom_call_target="tpu_custom_call" | custom-call | tf_op jit(solution)/shard_map/block_backward/pallas_call | solution.py:2332
  365.3 0.7 slice_bitcast_fusion
  366.1 0.2 reshape.110
  366.3 0.7 slice.52
  367.1 0.7 slice.54
  367.8 0.7 slice_bitcast_fusion.1
  368.5 0.1 copy.74
  368.6 0.2 reshape.111
  368.9 0.7 constant_dynamic-update-slice_fusion
  369.6 1.3 fusion.5
  370.8 1.3 multiply_subtract_fusion.1
  372.1 13.6 %fusion.3 = (bf16[3,9,96,512]{3,2,1,0:T(8,128)(2,1)}, f32[3,9,96,512]{3,2,1,0:T(8,128)}, f32[3,9,96,512]{3,2,1,0:T(8,128)}, f32[3,9,96,512]{3,2,1,0:T(8,128)}) fusion(f32[3,9,96,512]{3,2,1,0:T(8,128)} %rates_hbm.1, f32[3,9,96,512]{3,2,1,0:T(8,128)} %get-tuple-element.125, f32[]{:T(128)} %bitcast.19, f32[3,9,96,512]{3,2,1,0:T(8,128)} %param.49, ...), kind=kLoop, calls=%fused_computation.19 | loop fusion | flops 22560768 | bytes 39813124 | tf_op jit(solution)/shard_map/convert_element_type | solution.py:2568
  385.8 4.7 %adam_matrices.1 = (f32[64,512]{1,0:T(8,128)}, f32[64,512]{1,0:T(8,128)}, f32[64,512]{1,0:T(8,128)}, bf16[64,512]{1,0:T(8,128)(2,1)}, f32[9,64,128]{2,1,0:T(8,12...) custom-call(f32[8,128]{1,0:T(8,128)} %get-tuple-element.104.refs_0_,, ...), custom_call_target="tpu_custom_call" | custom-call | tf_op jit(solution)/shard_map/adam_matrices/pallas_call | solution.py:2439
  390.5 1.3 slice.57
  391.8 0.8 copy.82
  392.6 1.0 copy.83
  (26 shorter events, 0.3 us)
Async XLA Ops:
  0.7 161.0 %copy-start.2 = (f32[9751]{0:T(1024)S(1)}, f32[9751]{0:T(1024)}, u32[]{:S(2)}) copy-start(f32[9751]{0:T(1024)} %param.57) | copy-start | bytes 117016
  0.7 162.4 %slice-start = ((f32[9751]{0:T(1024)}), f32[3840]{0:T(1024)S(1)}, s32[]{:S(2)}) async-start(f32[9751]{0:T(1024)} %param.57), calls=%async_computation | async-start | bytes 32768 | tf_op jit(solution)/shard_map/slice | solution.py:2499
  287.9 82.9 %copy-start.3 = (f32[9751]{0:T(1024)S(1)}, f32[9751]{0:T(1024)}, u32[]{:S(2)}) copy-start(f32[9751]{0:T(1024)} %param.58) | copy-start | bytes 117016
  287.9 82.9 %copy-start.4 = (f32[9751]{0:T(1024)S(1)}, f32[9751]{0:T(1024)}, u32[]{:S(2)}) copy-start(f32[9751]{0:T(1024)} %param.59) | copy-start | bytes 117016
  372.1 19.6 %copy-start = (bf16[512,512]{1,0:T(8,128)(2,1)S(1)}, bf16[512,512]{1,0:T(8,128)(2,1)}, u32[]{:S(2)}) copy-start(bf16[512,512]{1,0:T(8,128)(2,1)} %get-tuple-element.84.x_ref) | copy-start | bytes 1572868
  385.8 6.8 %copy-start.1 = (f32[512,512]{1,0:T(8,128)S(1)}, f32[512,512]{1,0:T(8,128)}, u32[]{:S(2)}) copy-start(f32[512,512]{1,0:T(8,128)} %get-tuple-element.103) | copy-start | bytes 3145732

commit v5 on v4

--- a/solution.py
+++ b/solution.py
@@ -2412,7 +2412,9 @@
 def adam_matrices_kernel(*refs):
     total_ref, w_ref, tap_ref, p_ref, n_ref = refs[:5]
     olds = [refs[5 + 3 * i : 8 + 3 * i] for i in range(6)]
-    news = [refs[23 + 4 * i : 27 + 4 * i] for i in range(6)]
+    news = [refs[25 + 4 * i : 29 + 4 * i] for i in range(5)] + [refs[45:48]]
+    for i in range(2):
+        refs[48 + i][...] = refs[23 + i][...]
     factor = total_ref[1:2, 0:1]
     every = (slice(None), slice(None))
     adam_store(olds[0], news[0], every, w_ref[:, W_REDUCE] * factor)
@@ -2430,20 +2432,21 @@
         ref[...] = value
 
 
-def adam_matrices(totals, w_grad, tap_grad, proj_grad, norm_grad, states):
+def adam_matrices(totals, w_grad, tap_grad, proj_grad, norm_grad, states, results):
     flat = [array for state in states for array in state]
     outs = []
     for state in states[:5]:
         outs += [jax.ShapeDtypeStruct(state[0].shape, F32)] * 3 + [jax.ShapeDtypeStruct(state[0].shape, BF)]
     outs += [jax.ShapeDtypeStruct(states[5][0].shape, F32)] * 3
+    outs += [jax.ShapeDtypeStruct(result.shape, result.dtype) for result in results]
     return pl.pallas_call(
         adam_matrices_kernel,
         out_shape=tuple(outs),
-        in_specs=[whole_vmem()] * (5 + len(flat)),
+        in_specs=[whole_vmem()] * (7 + len(flat)),
         out_specs=[whole_vmem()] * len(outs),
         compiler_params=pltpu.CompilerParams(vmem_limit_bytes=VMEM_LIMIT),
         name="adam_matrices",
-    )(totals, w_grad, tap_grad, proj_grad, norm_grad, *flat)
+    )(totals, w_grad, tap_grad, proj_grad, norm_grad, *flat, *results)
 
 
 def per_device_rows(
@@ -2511,7 +2514,7 @@
         expand_new, expand_first, expand_second, expand_copy,
         head_new, head_first, head_second, head_copy,
         proj_new, proj_first, proj_second, proj_copy,
-        norm_new, norm_first, norm_second,
+        norm_new, norm_first, norm_second, shared, input_grad,
     ) = adam_matrices(
         totals, w_grad, root_sums, proj_shard, norm_grad,
         (
@@ -2522,6 +2525,7 @@
             (head_proj, m_proj, v_proj),
             (norm_params, norm_m, norm_v),
         ),
+        (shared, input_grad),
     )
     small_total = small_total.reshape(SMALL_ROWS, HID)
     small_grad = jnp.concatenate(

time: 394 us -> 393 us (level)
  no operation moved by 1% of the time
where the time goes in v5:
time: 393 us
  Pallas kernels  368 us (94%)
  other arithmetic  15.7 us (4%)
  local copies, waits for them, and re-layouts  8.04 us (2%)
    pallas_call x1, Pallas kernels, heads_backward(): pl.pallas_call(heads_backward_kernel, out_shape=(jax.ShapeDtypeStruct((3,...  124 us
    pallas_call x1, Pallas kernels, heads_forward(): pl.pallas_call(heads_forward_kernel, out_shape=(jax.ShapeDtypeStruct((4,...  87.5 us
    pallas_call x1, Pallas kernels, block_backward(): pl.pallas_call(block_backward_kernel, out_shape=(shape((PX, CIN), F32), s...  77.4 us
    pallas_call x1, Pallas kernels, block_forward(): pl.pallas_call(block_forward_kernel, out_shape=(shape((PX, CIN), BF), sha...  73.4 us
    convert_element_type x1, other arithmetic, per_device_rows(): rates_new.astype(BF)  13.6 us

profile of v5, /device:TPU:0, one launch (start us, length us, event | category | flops | bytes accessed | tf_op | source)
XLA Modules:
  0.0 392.6 jit_solution(15429713522714304872)
XLA Ops:
  0.7 73.4 %block_forward.1 = (bf16[512,512]{1,0:T(8,128)(2,1)}, f32[512,128]{1,0:T(8,128)}, f32[512,128]{1,0:T(8,128)}, f32[512,512]{1,0:T(8,128)}, bf16[8,64,2176]{2,1,0:...) custom-call(bf16[512,512]{1,0:T(8,128)(2,1)} %bitcast.31, ...), custom_call_target="tpu_custom_call" | custom-call | tf_op jit(solution)/shard_map/block_forward/pallas_call | solution.py:1980
  74.1 87.5 %heads_forward.1 = (bf16[4,768,128]{2,1,0:T(8,128)(2,1)}, bf16[8,512,512]{2,1,0:T(8,128)(2,1)}, bf16[4,3,64,1024]{3,2,1,0:T(8,128)(2,1)}, bf16[3,704,512]{2,1,0:T(8,128)(2,1)}, bf16[704,512]{1,0:T(8,128)(2,1)}) custom-call(bf16[512,512]{1,0:T(8,128)(2,1)} %get-tuple-element.86.x_ref.refs_23_, f32[3,9,96,512]{3,2,1,0:T(8,128)} %rates_hbm.1, ...), custom_call_target="tpu_custom_call" | custom-call | tf_op jit(solution)/shard_map/heads_forward/pallas_call | solution.py:1051
  161.7 0.2 reshape.103
  161.9 0.2 reshape.105
  162.1 0.1 copy.72
  162.2 0.1 pad.8.clone
  162.3 0.8 maximum_maximum_fusion.cols_ref
  163.1 0.6 reshape.102.small_ref
  163.7 124.2 %heads_backward.1 = (f32[3,9,96,512]{3,2,1,0:T(8,128)}, f32[512,512]{1,0:T(8,128)}, f32[8,128]{1,0:T(8,128)}, bf16[8,3,32,256]{3,2,1,0:T(8,128)(2,1)}, f32[16,256]{1,0:T(8,128)}, /*index=5*/f32[96,512]{1,0:T(8,128)}) custom-call(bf16[4,768,128]{2,1,0:T(8,128)(2,1)} %get-tuple-element.88.q_ref, bf16[4,3,64,1024]{3,2,1,0:T(8,128)(2,1)} %get-tuple-element.89.wpt_ref, ...), custom_call_target="tpu_custom_call" | custom-call | tf_op jit(solution)/shard_map/heads_backward/pallas_call | solution.py:1631
  287.9 77.4 %block_backward.1 = (f32[512,512]{1,0:T(8,128)}, f32[64,2176]{1,0:T(8,128)}, f32[3,128,256]{2,1,0:T(8,128)}, f32[4,16,256]{2,1,0:T(8,128)}, f32[2,3072]{1,0:T(2,128)}, /*index=5*/f32[8,128]{1,0:T(8,128)}) custom-call(f32[512,512]{1,0:T(8,128)} %get-tuple-element.94.gz_hbm, bf16[512,512]{1,0:T(8,128)(2,1)} %bitcast.32, s32[4,128]{1,0:T(4,128)} %mask_ref.5, ...), custom_call_target="tpu_custom_call" | custom-call | tf_op jit(solution)/shard_map/block_backward/pallas_call | solution.py:2332
  365.4 0.7 slice_bitcast_fusion
  366.1 0.1 copy.73
  366.2 0.2 reshape.110
  366.4 0.7 slice.52
  367.2 0.7 slice.54
  367.9 0.7 slice_bitcast_fusion.1
  368.6 0.1 copy.74
  368.7 0.2 reshape.111
  368.9 0.7 constant_dynamic-update-slice_fusion
  369.6 1.3 fusion.5
  370.9 1.3 multiply_subtract_fusion.1
  372.2 13.6 %fusion.3 = (bf16[3,9,96,512]{3,2,1,0:T(8,128)(2,1)}, f32[3,9,96,512]{3,2,1,0:T(8,128)}, f32[3,9,96,512]{3,2,1,0:T(8,128)}, f32[3,9,96,512]{3,2,1,0:T(8,128)}) fusion(f32[3,9,96,512]{3,2,1,0:T(8,128)} %rates_hbm.1, f32[3,9,96,512]{3,2,1,0:T(8,128)} %get-tuple-element.129, f32[]{:T(128)} %bitcast.19, f32[3,9,96,512]{3,2,1,0:T(8,128)} %param.49, ...), kind=kLoop, calls=%fused_computation.19 | loop fusion | flops 22560768 | bytes 39813124 | tf_op jit(solution)/shard_map/convert_element_type | solution.py:2572
  385.8 5.5 %adam_matrices.1 = (f32[64,512]{1,0:T(8,128)}, f32[64,512]{1,0:T(8,128)}, f32[64,512]{1,0:T(8,128)}, bf16[64,512]{1,0:T(8,128)(2,1)}, f32[9,64,128]{2,1,0:T(8,12...) custom-call(f32[8,128]{1,0:T(8,128)} %get-tuple-element.105.refs_0_,, ...), custom_call_target="tpu_custom_call" | custom-call | tf_op jit(solution)/shard_map/adam_matrices/pallas_call | solution.py:2442
  391.3 1.3 slice.57
  (20 shorter events, 0.1 us)
Async XLA Ops:
  0.7 161.0 %copy-start = (f32[9751]{0:T(1024)S(1)}, f32[9751]{0:T(1024)}, u32[]{:S(2)}) copy-start(f32[9751]{0:T(1024)} %param.57) | copy-start | bytes 117016
  0.7 162.4 %slice-start = ((f32[9751]{0:T(1024)}), f32[3840]{0:T(1024)S(1)}, s32[]{:S(2)}) async-start(f32[9751]{0:T(1024)} %param.57), calls=%async_computation | async-start | bytes 32768 | tf_op jit(solution)/shard_map/slice | solution.py:2502
  287.9 83.0 %copy-start.1 = (f32[9751]{0:T(1024)S(1)}, f32[9751]{0:T(1024)}, u32[]{:S(2)}) copy-start(f32[9751]{0:T(1024)} %param.58) | copy-start | bytes 117016
  287.9 83.0 %copy-start.2 = (f32[9751]{0:T(1024)S(1)}, f32[9751]{0:T(1024)}, u32[]{:S(2)}) copy-start(f32[9751]{0:T(1024)} %param.59) | copy-start | bytes 117016
